TPU v7x, 32 devices: a whole 2x2x4 slice. The times are simulated.
32 devices in a mesh: region: 32 (over z, y, x, core).
Axes of the slice: x: 2, y: 2, z: 4, core: 2. Of those that a mesh axis runs over, the one named last changes fastest.
Arguments:
- sample_points: float32 [8192, 3, 128], P('region'), may hold values from -6 to 6
- sample_spacing: float32 [8192, 128], P('region'), may hold values from 0.004 to 0.04
- crossed: int32 [8192, 4], P('region'), may hold values from 0 to 31, all different within a row; in each aligned block of 256 rows (0 to 255, 256 to 511, ...) at most 80 rows name the same one
- colour_grad: float32 [3, 8192], P(None, 'region'), may hold values from -24 to 24
- freq: bfloat16 [32, 3, 64], P('region'), may hold values from -18 to 18
- w_hidden: bfloat16 [32, 128, 256], P('region'), may hold values from -0.5 to 0.5
- w_head: bfloat16 [32, 4, 256], P('region'), may hold values from -0.375 to 0.375
Outputs:
- rendered: float32 [3, 8192], P(None, 'region')
- head_grad: float32 [32, 4, 256], P('region')
Inputs may be any that keep to these rules, and one draw needn't show every extreme that they name: `crossed`: row r lists 4 distinct regions, in the order ray r meets them. In each aligned block of 256 rays (the rays of one device) no region is listed by more than 80 rays; in some block some region is listed by exactly 80 rays. Every region is listed by some ray.
All inputs are finite; a program needn't handle non-finite values.
Results may differ from a plain program's by a relative error of at most 0.0019.
Values may be sent and summed in bfloat16 or wider, within the bound.
No kernel may reach another device: no remote copies, remote signals or barrier semaphores. Data moves between devices by JAX's collectives and lax.ppermute only.
A program may use at most 192 MiB of HBM per device.

v0:
```python
import jax
import jax.numpy as jnp
from jax import lax
from jax.sharding import PartitionSpec as P


def hidden_layer(points, freq, w_hidden):
    coords = points.reshape(points.shape[0], 3, -1)
    freq32 = freq.astype(jnp.float32)
    phases = coords[:, 0, :, None] * freq32[0][None, None, :]
    phases = phases + coords[:, 1, :, None] * freq32[1][None, None, :]
    phases = phases + coords[:, 2, :, None] * freq32[2][None, None, :]
    feature = jnp.concatenate([jnp.sin(phases), jnp.cos(phases)], axis=-1).astype(jnp.bfloat16)
    hidden = jnp.einsum("bsf,fh->bsh", feature, w_hidden, preferred_element_type=jnp.float32)
    return jnp.maximum(hidden, 0.0).astype(jnp.bfloat16)


def region_forward(points, freq, w_hidden, w_head):
    hidden = hidden_layer(points, freq, w_hidden)
    raw_out = jnp.einsum("bsh,oh->bos", hidden, w_head, preferred_element_type=jnp.float32)
    return (raw_out, hidden)


def render(raw_out, spacing):
    samples = spacing.shape[-1]
    upper = (jnp.arange(samples)[:, None] <= jnp.arange(samples)[None, :]).astype(jnp.float32)
    density = jax.nn.softplus(raw_out[0])
    colour = jax.nn.sigmoid(raw_out[1:])
    optical = density * spacing
    running = jnp.dot(optical, upper, precision=lax.Precision.HIGHEST)
    transmit = jnp.exp(optical - running)
    weight = transmit * (1.0 - jnp.exp(-optical))
    seg_colour = jnp.sum(weight[None] * colour, axis=-1)
    seg_trans = jnp.exp(-running[:, -1])
    return jnp.concatenate([seg_colour, seg_trans[None]], axis=0).T


def grouped(func, items, item_count, per_item):
    group_size = 1
    for candidate in range(1, item_count + 1):
        if item_count % candidate == 0 and candidate * per_item <= 16384:
            group_size = candidate
    shaped = jax.tree.map(
        lambda value: value.reshape((item_count // group_size, group_size) + value.shape[1:]), items
    )
    result = lax.map(lambda group_data: jax.vmap(func)(*group_data), shaped)
    return jax.tree.map(lambda value: value.reshape((item_count,) + value.shape[2:]), result)


def slot_numbers(flat_region, regions, capacity):
    seg_total = flat_region.shape[0]
    row_block = min(128, seg_total)
    onehot = (flat_region[:, None] == jnp.arange(regions, dtype=jnp.int32)[None, :]).astype(
        jnp.float32
    )
    onehot = onehot.reshape(seg_total // row_block, row_block, regions)
    strict_lower = (jnp.arange(row_block)[:, None] > jnp.arange(row_block)[None, :]).astype(
        jnp.float32
    )
    within = jnp.einsum("ij,bjn->bin", strict_lower, onehot)
    block_sums = jnp.sum(onehot, axis=1)
    offsets = jnp.cumsum(block_sums, axis=0) - block_sums
    slot_rank = jnp.sum(onehot * (within + offsets[:, None, :]), axis=-1).reshape(seg_total)
    return flat_region * capacity + slot_rank.astype(jnp.int32)


def composite(partials, colour_grad):
    upstream = colour_grad.T
    crossings = partials.shape[1]
    before = jnp.ones(partials.shape[:1], partials.dtype)
    befores = []
    rendered = jnp.zeros_like(upstream)
    for k in range(crossings):
        befores.append(before)
        rendered = rendered + before[:, None] * partials[:, k, :3]
        before = before * partials[:, k, 3]
    behind = jnp.zeros_like(upstream)
    seg_grads = [None] * crossings
    for k in range(crossings - 1, -1, -1):
        grad_colour = befores[k][:, None] * upstream
        grad_trans = befores[k] * jnp.sum(upstream * behind, axis=-1)
        seg_grads[k] = jnp.concatenate([grad_colour, grad_trans[:, None]], axis=-1)
        behind = partials[:, k, :3] + partials[:, k, 3][:, None] * behind
    return (rendered.T, jnp.stack(seg_grads, axis=1))


def on_device(sample_points, sample_spacing, crossed, colour_grad, freq, w_hidden, w_head):
    regions = lax.axis_size("region")
    ray_count, crossings = crossed.shape
    capacity = max(2, 5 * ray_count * crossings // (2 * regions))
    samples = sample_spacing.shape[1] // crossings
    per_item = capacity * samples
    flat_region = crossed.reshape(-1)
    slots = slot_numbers(flat_region, regions, capacity)
    points_seg = sample_points.reshape(ray_count, 3, crossings, samples).transpose(0, 2, 1, 3)
    points_seg = points_seg.reshape(ray_count * crossings, 3 * samples)
    spacing_seg = sample_spacing.reshape(ray_count * crossings, samples)
    point_buf = jnp.zeros((regions * capacity, 3 * samples), jnp.float32)
    point_buf = point_buf.at[slots].set(points_seg).reshape(regions, capacity, 3 * samples)
    own_freq = freq[0]
    own_hidden = w_hidden[0]
    own_head = w_head[0]
    got_points = lax.all_to_all(point_buf, "region", split_axis=0, concat_axis=0, tiled=True)
    raw_local, hidden_kept = grouped(
        lambda rows_in: region_forward(rows_in, own_freq, own_hidden, own_head),
        (got_points,),
        regions,
        per_item,
    )
    returned = lax.all_to_all(raw_local, "region", split_axis=0, concat_axis=0, tiled=True)
    raw_seg = returned.reshape(regions * capacity, 4, samples)[slots].transpose(1, 0, 2)
    seg_parts, pullback = jax.vjp(lambda value: render(value, spacing_seg), raw_seg)
    partials = seg_parts.reshape(ray_count, crossings, 4)
    rendered, seg_grads = composite(partials, colour_grad)
    raw_grad = pullback(seg_grads.reshape(-1, 4))[0].astype(jnp.bfloat16)
    grad_buf = jnp.zeros((regions * capacity, 4, samples), jnp.bfloat16)
    grad_buf = (
        grad_buf.at[slots].set(raw_grad.transpose(1, 0, 2)).reshape(regions, capacity, 4, samples)
    )
    got_grads = lax.all_to_all(grad_buf, "region", split_axis=0, concat_axis=0, tiled=True)
    head_grad = jnp.einsum(
        "nbos,nbsh->oh", got_grads, hidden_kept, preferred_element_type=jnp.float32
    )[None]
    return (rendered, head_grad)


def solution(mesh):
    return jax.shard_map(
        on_device,
        mesh=mesh,
        in_specs=(
            P("region", None, None),
            P("region", None),
            P("region", None),
            P(None, "region"),
            P("region", None, None),
            P("region", None, None),
            P("region", None, None),
        ),
        out_specs=(P(None, "region"), P("region", None, None)),
        check_vma=False,
    )
```

profile of v0, /device:TPU:0, one launch (start us, length us, event | category | flops | bytes accessed | tf_op | source)
XLA Modules:
  0.0 512.5 jit_solution(16107398574177552432)
XLA Ops:
  0.6 0.8 copy.100
  2.9 1.2 copy.101
  4.1 1.3 copy.102
  5.4 0.8 reshape.239
  6.2 4.2 scatter_custom_fusion
  10.4 7.3 %all-to-all-start = ((f32[32,80,96]{2,1,0:T(8,128)}), f32[32,80,96]{2,1,0:T(8,128)S(1)}, u32[]{:S(2)}, u32[]{:S(2)}) async-start(f32[32,80,96]{2,1,0:T(8,128)} %bitcast.20), calls=%async_computation | async-start | bytes 2621440 | tf_op jit(solution)/shard_map/all_to_all | solution.py:103
  17.7 32.1 %all-to-all-done = f32[32,80,96]{2,1,0:T(8,128)S(1)} async-done(((f32[32,80,96]{2,1,0:T(8,128)}), f32[32,80,96]{2,1,0:T(8,128)S(1)}, u32[]{:S(2)}, u32[]{:S(2)}) %all-to-all-start) | async-done | bytes 983072 | tf_op jit(solution)/shard_map/all_to_all | solution.py:103
  49.8 232.2 %while.12 = (s32[]{:T(128)}, f32[8,4,80,4,32]{2,4,3,1,0:T(8,128)}, bf16[8,4,80,32,256]{4,3,2,1,0:T(8,128)(2,1)}, f32[8,4,80,96]{3,2,1,0:T(8,128)S(1)}, bf16[3,64...) while((s32[]{:T(128)}, f32[8,4,80,4,32]{2,4,3,1,0:T(8,128)}, ...), condition=%wide.region_5.6_spmd, body=%wide.region_4.5_spmd.sunk | while | flops 707133632 | bytes 23067096 | solution.py:46
  50.4 20.1 %sine_convert_fusion.2 = (bf16[4,80,32,64]{3,2,1,0:T(8,128)(2,1)S(1)}, bf16[4,80,32,64]{3,2,1,0:T(8,128)(2,1)S(1)}) fusion(f32[64]{0:T(128)S(1)} %get-tuple-element.183, f32[4,80,32]{2,1,0:T(8,128)S(1)} %copy.144, f32[64]{0:T(128)S(1)} %get-tuple-element.185, f32[4,80,32]{2,1,0:T(8,128)S(1)} %copy.145, f32[64]{0:T(128)S(1)} %get-tuple-element.187, ...), kind=kLoop, calls=%fused_computation.6.clone.1 | loop fusion | flops 4587520 | bytes 2745088 | tf_op jit(solution)/shard_map/convert
  70.5 3.9 bitcast_dynamic-update-slice_fusion.2
  74.4 3.5 convolution_bitcast_fusion.2
  78.1 0.7 constant_dynamic-update-slice_fusion.2
  79.4 20.1 %sine_convert_fusion.2 = (bf16[4,80,32,64]{3,2,1,0:T(8,128)(2,1)S(1)}, bf16[4,80,32,64]{3,2,1,0:T(8,128)(2,1)S(1)}) fusion(f32[64]{0:T(128)S(1)} %get-tuple-element.183, f32[4,80,32]{2,1,0:T(8,128)S(1)} %copy.144, f32[64]{0:T(128)S(1)} %get-tuple-element.185, f32[4,80,32]{2,1,0:T(8,128)S(1)} %copy.145, f32[64]{0:T(128)S(1)} %get-tuple-element.187, ...), kind=kLoop, calls=%fused_computation.6.clone.1 | loop fusion | flops 4587520 | bytes 2745088 | tf_op jit(solution)/shard_map/convert
  99.5 4.0 bitcast_dynamic-update-slice_fusion.2
  103.5 3.5 convolution_bitcast_fusion.2
  108.4 20.1 %sine_convert_fusion.2 = (bf16[4,80,32,64]{3,2,1,0:T(8,128)(2,1)S(1)}, bf16[4,80,32,64]{3,2,1,0:T(8,128)(2,1)S(1)}) fusion(f32[64]{0:T(128)S(1)} %get-tuple-element.183, f32[4,80,32]{2,1,0:T(8,128)S(1)} %copy.144, f32[64]{0:T(128)S(1)} %get-tuple-element.185, f32[4,80,32]{2,1,0:T(8,128)S(1)} %copy.145, f32[64]{0:T(128)S(1)} %get-tuple-element.187, ...), kind=kLoop, calls=%fused_computation.6.clone.1 | loop fusion | flops 4587520 | bytes 2745088 | tf_op jit(solution)/shard_map/convert
  128.6 3.9 bitcast_dynamic-update-slice_fusion.2
  132.5 3.5 convolution_bitcast_fusion.2
  136.2 0.7 constant_dynamic-update-slice_fusion.2
  137.4 20.1 %sine_convert_fusion.2 = (bf16[4,80,32,64]{3,2,1,0:T(8,128)(2,1)S(1)}, bf16[4,80,32,64]{3,2,1,0:T(8,128)(2,1)S(1)}) fusion(f32[64]{0:T(128)S(1)} %get-tuple-element.183, f32[4,80,32]{2,1,0:T(8,128)S(1)} %copy.144, f32[64]{0:T(128)S(1)} %get-tuple-element.185, f32[4,80,32]{2,1,0:T(8,128)S(1)} %copy.145, f32[64]{0:T(128)S(1)} %get-tuple-element.187, ...), kind=kLoop, calls=%fused_computation.6.clone.1 | loop fusion | flops 4587520 | bytes 2745088 | tf_op jit(solution)/shard_map/convert
  157.5 3.9 bitcast_dynamic-update-slice_fusion.2
  161.4 3.5 convolution_bitcast_fusion.2
  165.1 0.8 constant_dynamic-update-slice_fusion.2
  166.4 20.1 %sine_convert_fusion.2 = (bf16[4,80,32,64]{3,2,1,0:T(8,128)(2,1)S(1)}, bf16[4,80,32,64]{3,2,1,0:T(8,128)(2,1)S(1)}) fusion(f32[64]{0:T(128)S(1)} %get-tuple-element.183, f32[4,80,32]{2,1,0:T(8,128)S(1)} %copy.144, f32[64]{0:T(128)S(1)} %get-tuple-element.185, f32[4,80,32]{2,1,0:T(8,128)S(1)} %copy.145, f32[64]{0:T(128)S(1)} %get-tuple-element.187, ...), kind=kLoop, calls=%fused_computation.6.clone.1 | loop fusion | flops 4587520 | bytes 2745088 | tf_op jit(solution)/shard_map/convert
  186.6 3.9 bitcast_dynamic-update-slice_fusion.2
  190.5 3.5 convolution_bitcast_fusion.2
  195.4 20.1 %sine_convert_fusion.2 = (bf16[4,80,32,64]{3,2,1,0:T(8,128)(2,1)S(1)}, bf16[4,80,32,64]{3,2,1,0:T(8,128)(2,1)S(1)}) fusion(f32[64]{0:T(128)S(1)} %get-tuple-element.183, f32[4,80,32]{2,1,0:T(8,128)S(1)} %copy.144, f32[64]{0:T(128)S(1)} %get-tuple-element.185, f32[4,80,32]{2,1,0:T(8,128)S(1)} %copy.145, f32[64]{0:T(128)S(1)} %get-tuple-element.187, ...), kind=kLoop, calls=%fused_computation.6.clone.1 | loop fusion | flops 4587520 | bytes 2745088 | tf_op jit(solution)/shard_map/convert
  215.5 3.9 bitcast_dynamic-update-slice_fusion.2
  219.5 3.5 convolution_bitcast_fusion.2
  224.4 20.1 %sine_convert_fusion.2 = (bf16[4,80,32,64]{3,2,1,0:T(8,128)(2,1)S(1)}, bf16[4,80,32,64]{3,2,1,0:T(8,128)(2,1)S(1)}) fusion(f32[64]{0:T(128)S(1)} %get-tuple-element.183, f32[4,80,32]{2,1,0:T(8,128)S(1)} %copy.144, f32[64]{0:T(128)S(1)} %get-tuple-element.185, f32[4,80,32]{2,1,0:T(8,128)S(1)} %copy.145, f32[64]{0:T(128)S(1)} %get-tuple-element.187, ...), kind=kLoop, calls=%fused_computation.6.clone.1 | loop fusion | flops 4587520 | bytes 2745088 | tf_op jit(solution)/shard_map/convert
  244.5 4.0 bitcast_dynamic-update-slice_fusion.2
  248.6 3.5 convolution_bitcast_fusion.2
  252.3 0.7 constant_dynamic-update-slice_fusion.2
  253.5 20.1 %sine_convert_fusion.2 = (bf16[4,80,32,64]{3,2,1,0:T(8,128)(2,1)S(1)}, bf16[4,80,32,64]{3,2,1,0:T(8,128)(2,1)S(1)}) fusion(f32[64]{0:T(128)S(1)} %get-tuple-element.183, f32[4,80,32]{2,1,0:T(8,128)S(1)} %copy.144, f32[64]{0:T(128)S(1)} %get-tuple-element.185, f32[4,80,32]{2,1,0:T(8,128)S(1)} %copy.145, f32[64]{0:T(128)S(1)} %get-tuple-element.187, ...), kind=kLoop, calls=%fused_computation.6.clone.1 | loop fusion | flops 4587520 | bytes 2745088 | tf_op jit(solution)/shard_map/convert
  273.6 3.9 bitcast_dynamic-update-slice_fusion.2
  277.6 3.5 convolution_bitcast_fusion.2
  281.3 0.8 constant_dynamic-update-slice_fusion.2
  282.0 3.8 all-to-all-start.1
  286.2 48.4 %all-to-all-done.1 = f32[32,80,4,32]{1,3,2,0:T(8,128)S(1)} async-done(((f32[32,80,4,32]{1,3,2,0:T(8,128)}), f32[32,80,4,32]{1,3,2,0:T(8,128)S(1)}, u32[]{:S(2)}, u32[]{:S(2)}) %all-to-all-start.1) | async-done | bytes 1310752 | tf_op jit(solution)/shard_map/all_to_all | solution.py:110
  334.6 3.6 copy.105
  338.2 6.0 %gather_fusion = f32[1024,4,32]{2,1,0:T(4,128)S(1)} fusion(f32[2560,4,32]{2,1,0:T(4,128)} %bitcast.144, s32[1024]{0:T(1024)S(1)} %broadcast_clamp_fusion), kind=kCustom, calls=%fused_computation | custom fusion | bytes 1052672 | tf_op jit(solution)/shard_map/gather | solution.py:111
  344.2 0.8 copy.106
  346.4 0.8 slice_reduce_fusion.2
  349.1 1.4 copy.110
  351.3 60.5 %scatter_fusion = bf16[2560,4,32]{2,1,0:T(4,128)(2,1)S(1)} fusion(bf16[2560,4,32]{2,1,0:T(4,128)(2,1)S(1)} %broadcast_in_dim.31, s32[1024]{0:T(1024)S(1)} %bitcast.158, bf16[1024,4,32]{2,1,0:T(4,128)(2,1)} %copy.110), kind=kCustom, calls=%fused_computation.2 | custom fusion | bytes 790528 | tf_op jit(solution)/shard_map/scatter | solution.py:118
  411.7 4.3 copy.112
  416.1 30.2 %all_to_all.15 = bf16[32,80,4,32]{1,2,3,0:T(4,128)(2,1)S(1)} all-to-all(bf16[32,80,4,32]{1,2,3,0:T(4,128)(2,1)} %copy.112), channel_id=1, replica_groups=mesh['region'=32] {'region'}, dimensions={0} | all-to-all | bytes 1310720 | tf_op jit(solution)/shard_map/all_to_all | solution.py:120
  446.2 66.2 %fusion.14 = f32[1,4,256]{2,1,0:T(4,128)} fusion(bf16[32,80,4,32]{1,2,3,0:T(4,128)(2,1)S(1)} %all_to_all.15, bf16[32,80,32,256]{3,2,1,0:T(8,128)(2,1)} %bitcast.141), kind=kOutput, calls=%fused_computation.33 | convolution fusion | flops 167772160 | bytes 42602496 | tf_op jit(solution)/shard_map/nbos,nbsh->oh/dot_general | solution.py:121
  (119 shorter events, 13.3 us)
Async XLA Ops:
  2.1 47.7 %copy-start = (bf16[1,128,256]{2,1,0:T(8,128)(2,1)S(1)}, bf16[1,128,256]{2,1,0:T(8,128)(2,1)}, u32[]{:S(2)}) copy-start(bf16[1,128,256]{2,1,0:T(8,128)(2,1)} %param.14) | copy-start | bytes 196612
  2.1 47.7 %copy-start.2 = (bf16[1,4,256]{2,1,0:T(4,128)(2,1)S(1)}, bf16[1,4,256]{2,1,0:T(4,128)(2,1)}, u32[]{:S(2)}) copy-start(bf16[1,4,256]{2,1,0:T(4,128)(2,1)} %param.15) | copy-start | bytes 6148
  2.2 47.7 %copy-start.3 = (bf16[1,3,64]{2,1,0:T(4,128)(2,1)S(1)}, bf16[1,3,64]{2,1,0:T(4,128)(2,1)}, u32[]{:S(2)}) copy-start(bf16[1,3,64]{2,1,0:T(4,128)(2,1)} %param.13) | copy-start | bytes 1156
  10.4 39.4 %all-to-all-start = ((f32[32,80,96]{2,1,0:T(8,128)}), f32[32,80,96]{2,1,0:T(8,128)S(1)}, u32[]{:S(2)}, u32[]{:S(2)}) async-start(f32[32,80,96]{2,1,0:T(8,128)} %bitcast.20), calls=%async_computation | async-start | bytes 2621440 | tf_op jit(solution)/shard_map/all_to_all | solution.py:103
  49.8 236.0 %copy-start.1 = (f32[256,128]{1,0:T(8,128)S(1)}, f32[256,128]{1,0:T(8,128)}, u32[]{:S(2)}) copy-start(f32[256,128]{1,0:T(8,128)} %param.10) | copy-start | bytes 393220
  282.0 52.5 %all-to-all-start.1 = ((f32[32,80,4,32]{1,3,2,0:T(8,128)}), f32[32,80,4,32]{1,3,2,0:T(8,128)S(1)}, u32[]{:S(2)}, u32[]{:S(2)}) async-start(f32[32,80,4,32]{1,3,2,0:T(8,128)} %bitcast.150), calls=%async_computation.1 | async-start | bytes 4194304 | tf_op jit(solution)/shard_map/all_to_all | solution.py:110
  338.2 9.1 %copy-start.4 = (f32[3,256]{1,0:T(4,128)S(1)}, f32[3,256]{1,0:T(4,128)}, u32[]{:S(2)}) copy-start(f32[3,256]{1,0:T(4,128)} %param.12) | copy-start | bytes 9220
where the time goes:
time: 519 us; the launch traced here: 512 us
  other arithmetic  163 us (31%)
  matrix products  126 us (24%)
  local copies, waits for them, and re-layouts  99.5 us (19%)
  waiting for transfers between devices  80.5 us (16%)
  blocking collectives  30.2 us (6%)
  starting transfers between devices  11.1 us (2%)
    another operation x8, other arithmetic  161 us
    dot_general x1, matrix products, on_device(): jnp.einsum('nbos,nbsh->oh', got_grads, hidden_kept, preferred_element_typ...  66.2 us
    scatter x1, local copies, waits for them, and re-layouts, on_device(): grad_buf.at[slots].set(raw_grad.transpose(1, 0, 2))  60.5 us
    all_to_all x1, waiting for transfers between devices, on_device(): lax.all_to_all(raw_local, 'region', split_axis=0, concat_axis=0, tiled=True)  48.4 us
    all_to_all x1, waiting for transfers between devices, on_device(): lax.all_to_all(point_buf, 'region', split_axis=0, concat_axis=0, tiled=True)  32.1 us
    dot_general x8, matrix products, hidden_layer(): jnp.einsum('bsf,fh->bsh', feature, w_hidden, preferred_element_type=jnp.f...  31.5 us
    all_to_all x1, blocking collectives, on_device(): lax.all_to_all(grad_buf, 'region', split_axis=0, concat_axis=0, tiled=True)  30.2 us
    dot_general x8, matrix products, region_forward(): jnp.einsum('bsh,oh->bos', hidden, w_head, preferred_element_type=jnp.floa...  27.7 us
  transfers between devices with their start and end apart: 2, of which 2 were waited for; matrix products, arithmetic and copies ran while one was open for 0% of the time, Pallas kernels for 0%

commit v1 on v0

v1 whole, which is shorter than its diff:
```python
import functools
import jax
import jax.numpy as jnp
from jax import lax
from jax.experimental import pallas as pl
from jax.experimental.pallas import tpu as pltpu
from jax.sharding import PartitionSpec as P

F32 = jnp.float32
BF16 = jnp.bfloat16
GROUP = 8
UNROLL = 16
SIN_HALF = (4.44288292, -7.3082457, 3.60635441, -0.84611289, 0.10982699)
TURN = 0.15915494309189535
ROUNDER = 12582912.0


def pieces(value, count):
    parts = []
    for _ in range(count - 1):
        parts.append(value.astype(BF16).astype(F32))
        value = value - parts[-1]
    return parts + [value]


def stacked(value, axis, count):
    return jnp.concatenate(pieces(value, count), axis=axis).astype(BF16)


def folded(value, count):
    rows = value.shape[0] // count
    return functools.reduce(jnp.add, [value[i * rows : (i + 1) * rows] for i in range(count)])


def dot(a, b):
    return lax.dot_general(a, b, (((1,), (0,)), ((), ())), preferred_element_type=F32)


def dot_nt(a, b):
    return lax.dot_general(a, b, (((1,), (1,)), ((), ())), preferred_element_type=F32)


def iota(shape, axis):
    return lax.broadcasted_iota(jnp.int32, shape, axis)


def joined(ref, at):
    return jnp.concatenate([ref[half, at, :] for half in range(ref.shape[0])], axis=1)


def ones_where(condition):
    return jnp.where(condition, 1.0, 0.0).astype(BF16)


def order_kernel(
    dims,
    crossed_ref,
    points_ref,
    spacing_ref,
    freq_ref,
    hidden_w_ref,
    head_w_ref,
    slots_ref,
    meta_ref,
    rows_ref,
    turned_ref,
    small_ref,
):
    regions, rays, crossings, samples, tiles = dims
    lanes = crossings * samples
    width = meta_ref.shape[1]
    turned_ref[...] = hidden_w_ref[...].astype(F32).T.astype(BF16)
    freqs = freq_ref.shape[1]
    small_ref[...] = jnp.zeros(small_ref.shape, BF16)
    for region in range(regions):
        small_ref[region, :4, :] = head_w_ref[...]
        small_ref[region, 4:7, :freqs] = freq_ref[...]

    region_at = iota((regions, rays), 0)
    named = [jnp.where(crossed_ref[k : k + 1, :] == region_at, 1.0, 0.0) for k in range(crossings)]
    listed = functools.reduce(jnp.add, named)
    earlier = ones_where(iota((rays, rays), 0) < iota((rays, rays), 1))
    rank = dot(listed.astype(BF16), earlier)
    count = jnp.sum(listed, axis=1, keepdims=True)
    tile_count = jnp.floor((count + (GROUP - 1)) * (1.0 / GROUP))
    below = ones_where(iota((regions, regions), 1) < iota((regions, regions), 0))
    tile_count = jnp.broadcast_to(tile_count, (regions, width))
    start = dot(below, tile_count.astype(BF16))
    slot = GROUP * start[:, :1] + rank
    slot_rows = [jnp.sum(one * slot, axis=0, keepdims=True) for one in named]
    slots_ref[...] = jnp.concatenate(slot_rows, axis=0)
    ended = jnp.where(start + tile_count <= iota((regions, width), 1).astype(F32), 1.0, 0.0)
    owner = jnp.minimum(jnp.sum(ended, axis=0, keepdims=True), regions - 1.0)
    used = jnp.sum(tile_count, axis=0, keepdims=True)
    meta_ref[...] = jnp.concatenate([owner, used], axis=0).astype(jnp.int32)

    slot_row = jnp.concatenate(slot_rows, axis=1)
    parts = [points_ref[d] * TURN for d in range(3)] + [spacing_ref[...]]
    lane_group = iota((rays, lanes), 1) // samples
    by_segment = []
    for k in range(crossings):
        row = jnp.zeros((rays, lanes), F32)
        for d in range(4):
            moved = pltpu.roll(parts[d], (samples * (d - k)) % lanes, 1) if d != k else parts[d]
            row = jnp.where(lane_group == d, moved, row)
        by_segment.append(row)
    source = stacked(jnp.concatenate(by_segment, axis=0), 1, 3)
    tile_row = jnp.floor(slot_row * (1.0 / GROUP))
    place_row = slot_row - GROUP * tile_row
    in_tile = ones_where(iota((tiles, rays * crossings), 0).astype(F32) == tile_row)
    out_group = iota((tiles, lanes), 1) // samples
    per_row = lanes // samples
    halves = GROUP // per_row
    dense = [[None] * halves for _ in range(4)]
    for s in range(GROUP):
        got = dot(in_tile * ones_where(place_row == s), source)
        got = got[:, :lanes] + got[:, lanes : 2 * lanes] + got[:, 2 * lanes :]
        at, half = s % per_row, s // per_row
        for d in range(4):
            moved = pltpu.roll(got, (samples * (at - d)) % lanes, 1) if d != at else got
            if at == 0:
                dense[d][half] = moved
            else:
                dense[d][half] = jnp.where(out_group == at, moved, dense[d][half])
    rows_ref[...] = jnp.zeros(rows_ref.shape, F32)
    for d in range(4):
        for half in range(halves):
            rows_ref[half, pl.ds(4 + d, tiles, stride=8), :] = dense[d][half]


def steps_used(meta, step):
    return jnp.minimum(step, (meta[1, 0] - 1) // UNROLL)


def feature_kernel(first, meta_ref, rows_ref, small_ref, *refs):
    feature_ref = refs[-1]
    used = meta_ref[1, 0]
    step = first + pl.program_id(0)
    rows = feature_ref.shape[0] // UNROLL
    half = rows // 2

    def phases(index):
        small = small_ref[meta_ref[0, step * UNROLL + index]][:, :128].astype(F32)
        freq = jnp.concatenate([small] * 3, axis=0).T[:half].astype(BF16)
        return dot(freq, stacked(joined(rows_ref, pl.ds(index * 8, 8)), 0, 3))

    def store(index, turns):
        for at in range(0, half, 16):
            part = turns[at : at + 16]
            rest = part - ((part + ROUNDER) - ROUNDER)
            square = rest * rest
            sine = jnp.full_like(square, SIN_HALF[-1])
            for c in SIN_HALF[-2::-1]:
                sine = sine * square + c
            sine = sine * rest
            twice = sine * sine
            left = jnp.maximum(2.0 - twice, 1e-30)
            first = index * rows + at
            feature_ref[first : first + 16, :] = (sine * (left * lax.rsqrt(left))).astype(BF16)
            first = first + half
            feature_ref[first : first + 16, :] = (1.0 - twice).astype(BF16)

    @pl.when(step * UNROLL < used)
    def _():
        ahead = phases(0)
        for index in range(UNROLL):
            turns = ahead
            if index + 1 < UNROLL:
                ahead = phases(index + 1)
            store(index, turns)


def main_kernel(
    dims,
    stages,
    parts,
    meta_ref,
    me_ref,
    slots_ref,
    rows_ref,
    colour_grad_ref,
    head_ref,
    feature_ref,
    *refs,
):
    part_refs = refs[:parts]
    rendered_ref, head_grad_ref = refs[parts : parts + 2]
    hidden_ref, raw_ref, grad_ref, weight_ref, slab_ref, weight_sems, slab_sems = refs[parts + 2 :]
    regions, rays, crossings, samples, tiles = dims
    width = GROUP * samples
    halves, lanes = raw_ref.shape[0], raw_ref.shape[2]
    used = meta_ref[1, 0]
    me = me_ref[0]
    rounds = (used + (UNROLL - 1)) // UNROLL
    units = hidden_ref.shape[0] // tiles
    depth = slab_ref.shape[1] // UNROLL
    held = regions // parts

    def fetch(step, slot):
        at = pl.multiple_of(step * (UNROLL * depth), UNROLL * depth)
        return pltpu.make_async_copy(
            feature_ref.at[pl.ds(at, UNROLL * depth), :], slab_ref.at[slot], slab_sems.at[slot]
        )

    copies = [
        pltpu.make_async_copy(
            part_refs[p], weight_ref.at[p * held : (p + 1) * held], weight_sems.at[p]
        )
        for p in range(parts)
    ]
    fetch(0, 0).start()
    for copy in copies:
        copy.start()
    for copy in copies:
        copy.wait()

    def rows_of(tile, height):
        return pl.ds(pl.multiple_of(tile * height, height), height)

    def forward(step, _):
        slot = lax.rem(step, 2)

        @pl.when(step + 1 < rounds)
        def _():
            fetch(step + 1, 1 - slot).start()

        fetch(step, slot).wait()
        first = step * UNROLL
        named = [meta_ref[0, first + index] for index in range(UNROLL)]

        def layer(index):
            weights = weight_ref[place(named[index] ^ me, stages)]
            return dot(weights, slab_ref[slot, index * depth : (index + 1) * depth, :])

        ahead = layer(0)
        for index in range(UNROLL):
            result = ahead
            if index + 1 < UNROLL:
                ahead = layer(index + 1)
            head(jnp.maximum(first - UNROLL, 0) + index)
            hidden_ref[rows_of(first + index, units), :] = jnp.maximum(result.astype(BF16), 0)
        return 0

    def head(tile):
        raw = dot(head_ref[meta_ref[0, tile]], hidden_ref[rows_of(tile, units), :])
        for half in range(halves):
            raw_ref[half, rows_of(tile, 8), :] = raw[:, half * lanes : (half + 1) * lanes]

    lax.fori_loop(0, rounds, forward, 0)
    for index in range(UNROLL):
        head((rounds - 1) * UNROLL + index)

    valid = iota((tiles, width), 0) < used
    raw = [
        jnp.where(valid, joined(raw_ref, pl.ds(c, tiles, stride=8)), 0.0) for c in range(4)
    ]
    spacing = joined(rows_ref, pl.ds(7, tiles, stride=8))
    decay = jnp.exp(-jnp.abs(raw[0]))
    density = jnp.maximum(raw[0], 0.0) + jnp.log1p(decay)
    slope = jnp.where(raw[0] >= 0, 1.0, decay) / (1.0 + decay)
    colour = [1.0 / (1.0 + jnp.exp(-raw[c])) for c in (1, 2, 3)]
    optical = density * spacing
    lane_a, lane_b = iota((width, width), 0), iota((width, width), 1)
    same = (lane_a // samples) == (lane_b // samples)
    up_to = ones_where(same & (lane_a <= lane_b))
    after = ones_where(same & (lane_a > lane_b))

    def by_pieces(value, matrix):
        return functools.reduce(jnp.add, [dot(p.astype(BF16), matrix) for p in pieces(value, 2)])

    running = by_pieces(optical, up_to)
    passed = jnp.exp(-running)
    weight = jnp.exp(optical - running) * (1.0 - jnp.exp(-optical))
    weighted = [weight * one for one in colour]

    member = ones_where(iota((GROUP, width), 0) == iota((GROUP, width), 1) // samples)
    sums = []
    for value in weighted + [optical]:
        sums.append(functools.reduce(jnp.add, [dot_nt(member, p.astype(BF16)) for p in pieces(value, 2)]))
    segments = rays * crossings
    slot_row = jnp.concatenate([slots_ref[k : k + 1, :] for k in range(crossings)], axis=1)
    tile_row = jnp.floor(slot_row * (1.0 / GROUP))
    place_row = slot_row - GROUP * tile_row
    lists = ones_where(iota((tiles, segments), 0).astype(F32) == tile_row)
    mine = iota((GROUP, segments), 0).astype(F32) == place_row
    in_tile = folded(dot(stacked(jnp.concatenate(sums, axis=0), 0, 2), lists), 2)
    by_ray = [
        jnp.sum(jnp.where(mine, in_tile[c * GROUP : (c + 1) * GROUP], 0.0), axis=0, keepdims=True)
        for c in range(4)
    ]
    seg_colour = jnp.concatenate(by_ray[:3], axis=0)
    seg_trans = jnp.exp(-by_ray[3])

    upstream = colour_grad_ref[...]
    colours = [seg_colour[:, k * rays : (k + 1) * rays] for k in range(crossings)]
    transes = [seg_trans[:, k * rays : (k + 1) * rays] for k in range(crossings)]
    before = jnp.ones((1, rays), F32)
    befores = []
    rendered = jnp.zeros_like(upstream)
    for k in range(crossings):
        befores.append(before)
        rendered = rendered + before * colours[k]
        before = before * transes[k]
    rendered_ref[...] = rendered
    behind = jnp.zeros_like(upstream)
    grads = [None] * crossings
    for k in range(crossings - 1, -1, -1):
        grad_trans = befores[k] * jnp.sum(upstream * behind, axis=0, keepdims=True)
        grads[k] = jnp.concatenate([befores[k] * upstream, grad_trans * transes[k]], axis=0)
        behind = colours[k] + transes[k] * behind
    grads = jnp.concatenate(grads, axis=1)

    placed = jnp.concatenate([jnp.where(mine, grads[c : c + 1], 0.0) for c in range(4)], axis=0)
    in_slots = dot_nt(lists, stacked(placed, 0, 2)).astype(BF16)
    channel_rows = iota((8 * GROUP, width), 0) % (4 * GROUP)
    lane_place = iota((8 * GROUP, width), 1) // samples
    per_sample = [
        dot(in_slots, ones_where(channel_rows == c * GROUP + lane_place)) for c in range(4)
    ]
    inner = functools.reduce(jnp.add, [per_sample[c] * colour[c] for c in range(3)])
    later = by_pieces(weight * inner, after)
    grad_optical = passed * inner - later - per_sample[3]
    raw_grad = [grad_optical * spacing * slope]
    for c in range(3):
        raw_grad.append(per_sample[c] * weighted[c] * (1.0 - colour[c]))
    for c in range(4):
        for half in range(halves):
            at = pl.ds(c, tiles, stride=8)
            grad_ref[half, at, :] = raw_grad[c][:, half * lanes : (half + 1) * lanes]

    head_grad_ref[...] = jnp.zeros(head_grad_ref.shape, F32)

    def backward(step, _):
        first = step * UNROLL
        products = []
        for index in range(UNROLL):
            gradient = joined(grad_ref, rows_of(first + index, 8)).astype(BF16)
            products.append(dot_nt(gradient, hidden_ref[rows_of(first + index, units), :])[:4])
        for index in range(UNROLL):
            head_grad_ref[meta_ref[0, first + index]] += products[index]
        return 0

    lax.fori_loop(0, rounds, backward, 0)


def exchange_stages(count):
    stages = []
    while count > 1:
        size = 4 if count % 4 == 0 and count > 4 else min(count, 4)
        size = 2 if count == 2 else size
        count //= size
        stages.append((count, size))
    return stages


def place(offset, stages):
    at, scale = 0, 1
    for unit, size in stages:
        at = at + ((offset // unit) % size) * scale
        scale = scale * size
    return at


def share_all(value, stages, count):
    held = [value[None]]
    for unit, size in stages:
        sent = held if (unit, size) == stages[-1] else [jnp.concatenate(held, axis=0)]
        held = list(sent)
        for other in range(1, size):
            pairs = [(i, i ^ (unit * other)) for i in range(count)]
            held += [lax.ppermute(piece, "region", pairs) for piece in sent]
    return held


def on_device(sample_points, sample_spacing, crossed, colour_grad, freq, w_hidden, w_head):
    regions = lax.axis_size("region")
    rays, crossings = crossed.shape
    samples = sample_spacing.shape[1] // crossings
    segments = rays * crossings
    tiles = (segments + (GROUP - 1) * regions) // GROUP
    tiles = -(-tiles // UNROLL) * UNROLL
    width, lanes = GROUP * samples, crossings * samples
    halves = width // lanes
    features = w_hidden.shape[1]
    hidden_units = w_hidden.shape[2]
    dims = (regions, rays, crossings, samples, tiles)
    vmem, smem = pltpu.VMEM, pltpu.SMEM
    mib = 1024 * 1024
    limit = 24 * mib

    me = lax.axis_index("region").astype(jnp.int32).reshape(1)
    meta_width = -(-tiles // 128) * 128
    slots, meta, rows, turned, small = pl.pallas_call(
        functools.partial(order_kernel, dims),
        out_shape=(
            jax.ShapeDtypeStruct((crossings, rays), F32),
            jax.ShapeDtypeStruct((2, meta_width), jnp.int32),
            jax.ShapeDtypeStruct((halves, tiles * 8, lanes), F32),
            jax.ShapeDtypeStruct((hidden_units, features), BF16),
            jax.ShapeDtypeStruct((regions, 8, hidden_units), BF16),
        ),
        in_specs=[pl.BlockSpec(memory_space=vmem)] * 6,
        out_specs=[pl.BlockSpec(memory_space=vmem)] * 5,
        compiler_params=pltpu.CompilerParams(vmem_limit_bytes=limit),
        cost_estimate=pl.CostEstimate(flops=4 * 10**9, bytes_accessed=10**7, transcendentals=0),
        name="order",
    )(
        crossed.T,
        sample_points.transpose(1, 0, 2),
        sample_spacing,
        freq[0],
        w_hidden[0],
        w_head[0],
    )

    stages = exchange_stages(regions)
    all_small = lax.all_to_all(small, "region", split_axis=0, concat_axis=0, tiled=True)
    weights = share_all(turned, stages, regions)

    steps = tiles // UNROLL
    split = steps * 7 // 10
    whole = pl.BlockSpec(memory_space=vmem)
    params = pltpu.CompilerParams(vmem_limit_bytes=limit)

    def row_block(begin=0):
        return pl.BlockSpec(
            (halves, UNROLL * 8, lanes), lambda i, m: (0, steps_used(m, i + begin), 0)
        )

    def features_of(first, last, *before):
        return pl.pallas_call(
            functools.partial(feature_kernel, first),
            out_shape=jax.ShapeDtypeStruct((tiles * features, width), BF16),
            grid_spec=pltpu.PrefetchScalarGridSpec(
                num_scalar_prefetch=1,
                grid=(last - first + 1,),
                in_specs=[row_block(first), whole]
                + [pl.BlockSpec(memory_space=pl.ANY)] * len(before),
                out_specs=pl.BlockSpec(
                    (UNROLL * features, width),
                    lambda i, m: (jnp.maximum(steps_used(m, i + first), first), 0),
                ),
            ),
            input_output_aliases={3: 0} if before else {},
            compiler_params=params,
            cost_estimate=pl.CostEstimate(flops=10**10, bytes_accessed=10**7, transcendentals=0),
            name="features",
        )(meta, rows, all_small, *before)

    feature = features_of(split, steps - 1, features_of(0, split - 1))

    kept = 2 * tiles * hidden_units * width
    kept += 4 * regions * hidden_units * features + 12 * halves * tiles * 8 * lanes
    kept = min(60 * mib, kept + 4 * UNROLL * features * width + 8 * mib)
    any_space = pl.BlockSpec(memory_space=pl.ANY)
    rendered, head_grad = pl.pallas_call(
        functools.partial(main_kernel, dims, stages, len(weights)),
        out_shape=(
            jax.ShapeDtypeStruct((3, rays), F32),
            jax.ShapeDtypeStruct((regions, 4, hidden_units), F32),
        ),
        in_specs=[pl.BlockSpec(memory_space=smem)] * 2
        + [whole] * 4
        + [any_space]
        + [whole] * len(weights),
        out_specs=[whole] * 2,
        scratch_shapes=[
            pltpu.VMEM((tiles * hidden_units, width), BF16),
            pltpu.VMEM((halves, tiles * 8, lanes), F32),
            pltpu.VMEM((halves, tiles * 8, lanes), F32),
            pltpu.VMEM((regions, hidden_units, features), BF16),
            pltpu.VMEM((2, UNROLL * features, width), BF16),
            pltpu.SemaphoreType.DMA((len(weights),)),
            pltpu.SemaphoreType.DMA((2,)),
        ],
        compiler_params=pltpu.CompilerParams(vmem_limit_bytes=kept),
        cost_estimate=pl.CostEstimate(flops=2 * 10**10, bytes_accessed=3 * 10**7, transcendentals=0),
        name="render",
    )(meta, me, slots, rows, colour_grad, all_small, feature, *weights)

    partial_sums = lax.all_to_all(head_grad, "region", split_axis=0, concat_axis=0, tiled=True)
    head_grad = jnp.sum(partial_sums, axis=0, keepdims=True)
    return (rendered, head_grad)


def solution(mesh):
    return jax.shard_map(
        on_device,
        mesh=mesh,
        in_specs=(
            P("region", None, None),
            P("region", None),
            P("region", None),
            P(None, "region"),
            P("region", None, None),
            P("region", None, None),
            P("region", None, None),
        ),
        out_specs=(P(None, "region"), P("region", None, None)),
        check_vma=False,
    )
```

time: 519 us -> 81 us (0.16); the launches traced: 512 us -> 80.1 us
  other arithmetic: 163 us -> 0.67 us
  matrix products: 126 us -> 0 us
  local copies, waits for them, and re-layouts: 99.5 us -> 4.78 us
  waiting for transfers between devices: 80.5 us -> 9.52 us
  Pallas kernels: 0 us -> 36.8 us
  blocking collectives: 30.2 us -> 11.2 us
  starting transfers between devices: 11.1 us -> 16.4 us
    another operation x12 -> x0, other arithmetic: 161 us -> none
    dot_general x20 -> x0, matrix products: 126 us -> none  [the longest x1 66.2 us: on_device(): jnp.einsum('nbos,nbsh->oh', got_grads, hidden_kept, preferred_element_typ...]
    all_to_all x2 -> x1, waiting for transfers between devices: 80.5 us -> 0.01 us  [on_device(): lax.all_to_all(small, 'region', split_axis=0, concat_axis=0, tiled=True)]
    scatter x2 -> x0, local copies, waits for them, and re-layouts: 64.6 us -> none  [the longest x1 60.5 us: on_device(): grad_buf.at[slots].set(raw_grad.transpose(1, 0, 2))]
    pallas_call x0 -> x4, Pallas kernels: none -> 36.8 us  [the longest x1 23.7 us: on_device(): pl.pallas_call(functools.partial(main_kernel, dims, stages, len(weights))...]
    all_to_all x1, blocking collectives: 30.2 us -> 11.2 us  [on_device(): lax.all_to_all(head_grad, 'region', split_axis=0, concat_axis=0, tiled=True)]
    ppermute x0 -> x10, waiting for transfers between devices: none -> 9.52 us  [share_all(): held += [lax.ppermute(piece, 'region', pairs) for piece in sent]]
    ppermute x0 -> x10, starting transfers between devices: none -> 9.09 us  [share_all(): held += [lax.ppermute(piece, 'region', pairs) for piece in sent]]
  transfers between devices with their start and end apart: 2 -> 11, of which waited for: 2 -> 4; matrix products, arithmetic and copies ran while one was open for 0% -> 0% of each run, Pallas kernels for 0% -> 13%
where the time goes in v1:
time: 81 us; the launch traced here: 80.1 us
  Pallas kernels  36.8 us (45%)
  starting transfers between devices  16.4 us (20%)
  blocking collectives  11.2 us (14%)
  waiting for transfers between devices  9.52 us (12%)
  local copies, waits for them, and re-layouts  4.78 us (6%)
    pallas_call x1, Pallas kernels, on_device(): pl.pallas_call(functools.partial(main_kernel, dims, stages, len(weights))...  23.7 us
    all_to_all x1, blocking collectives, on_device(): lax.all_to_all(head_grad, 'region', split_axis=0, concat_axis=0, tiled=True)  11.2 us
    pallas_call x2, Pallas kernels, features_of(): pl.pallas_call(functools.partial(feature_kernel, first), out_shape=jax.Sh...  10.4 us
    ppermute x10, waiting for transfers between devices, share_all(): held += [lax.ppermute(piece, 'region', pairs) for piece in sent]  9.52 us
    ppermute x10, starting transfers between devices, share_all(): held += [lax.ppermute(piece, 'region', pairs) for piece in sent]  9.09 us
    all_to_all x1, starting transfers between devices, on_device(): lax.all_to_all(small, 'region', split_axis=0, concat_axis=0, tiled=True)  7.3 us
    unnamed x14, local copies, waits for them, and re-layouts  4.78 us
    pallas_call x1, Pallas kernels, on_device(): pl.pallas_call(functools.partial(order_kernel, dims), out_shape=(jax.Shap...  2.81 us
  transfers between devices with their start and end apart: 11, of which 4 were waited for; matrix products, arithmetic and copies ran while one was open for 0% of the time, Pallas kernels for 13%

profile of v1, /device:TPU:0, one launch (start us, length us, event | category | flops | bytes accessed | tf_op | source)
XLA Modules:
  0.0 80.1 jit_solution(10748915407271567870)
XLA Ops:
  0.6 0.0 copy-start
  0.6 1.0 %copy-done = f32[256,3,128]{2,0,1:T(8,128)S(1)} copy-done((f32[256,3,128]{2,0,1:T(8,128)S(1)}, f32[256,3,128]{2,0,1:T(8,128)}, u32[]{:S(2)}) %copy-start) | copy-done | bytes 393240
  1.6 0.0 copy-start.1
  1.6 0.9 %copy-done.1 = f32[256,128]{1,0:T(8,128)S(1)} copy-done((f32[256,128]{1,0:T(8,128)S(1)}, f32[256,128]{1,0:T(8,128)}, u32[]{:S(2)}) %copy-start.1) | copy-done | bytes 131096
  2.5 0.0 copy-start.2
  2.5 0.8 %copy-done.2 = bf16[1,128,256]{2,1,0:T(8,128)(2,1)S(1)} copy-done((bf16[1,128,256]{2,1,0:T(8,128)(2,1)S(1)}, bf16[1,128,256]{2,1,0:T(8,128)(2,1)}, u32[]{:S(2)}) %copy-start.2) | copy-done | bytes 65560
  3.4 0.0 copy-start.3
  3.4 0.7 copy-done.3
  4.1 0.0 copy-start.5
  4.1 0.7 copy-done.5
  4.7 0.0 copy-start.6
  4.7 0.7 copy-done.6
  5.4 2.8 %order.1 = (f32[4,256]{1,0:T(4,128)S(1)}, s32[2,256]{1,0:T(2,128)S(1)}, f32[2,1280,128]{2,1,0:T(8,128)S(1)}, bf16[256,128]{1,0:T(8,128)(2,1)S(1)}, bf16[32,8,256]{2,1,0:T(8,128)(2,1)}) custom-call(s32[4,256]{1,0:T(4,128)S(1)} %bitcast.14, f32[3,256,128]{2,1,0:T(8,128)S(1)} %bitcast.12, f32[256,128]{1,0:T(8,128)S(1)} %copy-done.1, ...), custom_call_target="tpu_custom_call" | custom-call | flops 4000000000 | bytes 10000000 | tf_op jit(solution)/shard_map/order/pallas_call | solution.py:393
  8.2 7.3 %all-to-all-start = ((bf16[32,8,256]{2,1,0:T(8,128)(2,1)}), bf16[32,8,256]{2,1,0:T(8,128)(2,1)S(1)}, u32[]{:S(2)}, u32[]{:S(2)}) async-start(bf16[32,8,256]{2,1,0:T(8,128)(2,1)} %get-tuple-element.12), calls=%async_computation | async-start | bytes 262144 | tf_op jit(solution)/shard_map/all_to_all | solution.py:417
  15.5 1.8 %collective-permute-start = (bf16[1,256,128]{2,1,0:T(8,128)(2,1)S(1)}, bf16[1,256,128]{2,1,0:T(8,128)(2,1)S(1)}, u32[]{:S(2)}, u32[]{:S(2)}) collective-permute-start(bf16[1,256,128]{2,1,0:T(8,128)(2,1)S(1)} %bitcast.8), channel_id=1, source_target_pairs={{0,8},{1,9},{2,10},{3,11},{4,12},{5,13},{6,14},{7,15},{8,0},{9,1},... | collective-permute-start | bytes 196616 | tf_op jit(solution)/shard_map/ppermute | solution.py:371
  17.4 2.4 %collective-permute-start.1 = (bf16[1,256,128]{2,1,0:T(8,128)(2,1)S(1)}, bf16[1,256,128]{2,1,0:T(8,128)(2,1)S(1)}, u32[]{:S(2)}, u32[]{:S(2)}) collective-permute-start(bf16[1,256,128]{2,1,0:T(8,128)(2,1)S(1)} %bitcast.9), channel_id=1, source_target_pairs={{0,16},{1,17},{2,18},{3,19},{4,20},{5,21},{6,22},{7,23},{8,24},{9,... | collective-permute-start | bytes 196616 | tf_op jit(solution)/shard_map/ppermute | solution.py:371
  19.8 0.2 collective-permute-start.2
  20.0 1.9 %collective-permute-done = bf16[1,256,128]{2,1,0:T(8,128)(2,1)S(1)} collective-permute-done((bf16[1,256,128]{2,1,0:T(8,128)(2,1)S(1)}, bf16[1,256,128]{2,1,0:T(8,128)(2,1)S(1)}, u32[]{:S(2)}, u32[]{:S(2)}) %collective-permute-start) | collective-permute-done | bytes 65568 | tf_op jit(solution)/shard_map/ppermute | solution.py:371
  21.9 2.4 %collective-permute-done.1 = bf16[1,256,128]{2,1,0:T(8,128)(2,1)S(1)} collective-permute-done((bf16[1,256,128]{2,1,0:T(8,128)(2,1)S(1)}, bf16[1,256,128]{2,1,0:T(8,128)(2,1)S(1)}, u32[]{:S(2)}, u32[]{:S(2)}) %collective-permute-start.1) | collective-permute-done | bytes 65568 | tf_op jit(solution)/shard_map/ppermute | solution.py:371
  24.3 2.4 %collective-permute-done.2 = bf16[1,256,128]{2,1,0:T(8,128)(2,1)S(1)} collective-permute-done((bf16[1,256,128]{2,1,0:T(8,128)(2,1)S(1)}, bf16[1,256,128]{2,1,0:T(8,128)(2,1)S(1)}, u32[]{:S(2)}, u32[]{:S(2)}) %collective-permute-start.2) | collective-permute-done | bytes 65568 | tf_op jit(solution)/shard_map/ppermute | solution.py:371
  26.7 1.5 %collective-permute-start.3 = (bf16[4,256,128]{2,1,0:T(8,128)(2,1)S(1)}, bf16[4,256,128]{2,1,0:T(8,128)(2,1)S(1)}, u32[]{:S(2)}, u32[]{:S(2)}) collective-permute-start(bf16[4,256,128]{2,1,0:T(8,128)(2,1)S(1)} %pad_maximum_fusion.refs_0_), channel_id=1, source_target_pairs={{0,2},{1,3},{2,0},{3,1},{4,6},{5,7},{6,4},{7,5},{8,10},{9,11},{10,... | collective-permute-start | bytes 786440 | tf_op jit(solution)/shard_map/ppermute | solution.py:371
  28.3 1.5 %collective-permute-start.4 = (bf16[4,256,128]{2,1,0:T(8,128)(2,1)S(1)}, bf16[4,256,128]{2,1,0:T(8,128)(2,1)S(1)}, u32[]{:S(2)}, u32[]{:S(2)}) collective-permute-start(bf16[4,256,128]{2,1,0:T(8,128)(2,1)S(1)} %pad_maximum_fusion.refs_0_), channel_id=1, source_target_pairs={{0,4},{1,5},{2,6},{3,7},{4,0},{5,1},{6,2},{7,3},{8,12},{9,13},{10,... | collective-permute-start | bytes 786440 | tf_op jit(solution)/shard_map/ppermute | solution.py:371
  29.8 0.5 collective-permute-start.5
  30.3 0.0 collective-permute-start.6
  30.3 0.0 all-to-all-done.small_ref.head_ref
  30.3 7.7 %features.2.refs_0_ = bf16[20480,256]{1,0:T(8,128)(2,1)S(1)} custom-call(s32[2,256]{1,0:T(2,128)S(1)} %get-tuple-element.9.meta_ref, f32[2,1280,128]{2,1,0:T(8,128)S(1)} %get-tuple-element.11.rows_ref, bf16[32,8,256]{2,1,0:T(8,128)(2,1)S(1)} %all-to-all-done.small_ref.head_ref), custom_call_target="tpu_custom_call" | custom-call | flops 10000000000 | bytes 10000000 | tf_op jit(solution)/shard_map/features/pallas_call | solution.py:431
  38.0 0.0 copy-start.4
  38.0 0.0 collective-permute-done.3.refs_1_
  38.0 0.6 collective-permute-start.7
  38.6 2.8 %collective-permute-done.4.refs_2_ = bf16[4,256,128]{2,1,0:T(8,128)(2,1)S(1)} collective-permute-done((bf16[4,256,128]{2,1,0:T(8,128)(2,1)S(1)}, bf16[4,256,128]{2,1,0:T(8,128)(2,1)S(1)}, u32[]{:S(2)}, u32[]{:S(2)}) %collective-permute-start.4) | collective-permute-done | bytes 262176 | tf_op jit(solution)/shard_map/ppermute | solution.py:371
  41.4 0.0 collective-permute-start.8
  41.4 0.0 collective-permute-done.5.refs_3_
  41.4 0.5 collective-permute-start.9
  41.9 2.7 %features.3.feature_ref = bf16[20480,256]{1,0:T(8,128)(2,1)S(1)} custom-call(s32[2,256]{1,0:T(2,128)S(1)} %get-tuple-element.9.meta_ref, f32[2,1280,128]{2,1,0:T(8,128)S(1)} %get-tuple-element.11.rows_ref, bf16[32,8,256]{2,1,0:T(8,128)(2,1)S(1)} %all-to-all-done.small_ref.head_ref, ...), custom_call_target="tpu_custom_call", output_to_operand_aliasing={{}: (3, {})} | custom-call | flops 10000000000 | bytes 10000000 | tf_op jit(solution)/shard_map/features/pallas_call | solution.py:431
  44.6 0.0 collective-permute-done.6.refs_4_
  44.6 0.0 collective-permute-done.7.refs_5_
  44.6 0.0 collective-permute-done.8.refs_6_
  44.6 0.0 collective-permute-done.9.refs_7_
  44.6 0.0 copy-done.4
  44.6 23.7 %render.1 = (f32[3,256]{1,0:T(4,128)}, f32[32,4,256]{2,1,0:T(4,128)S(1)}) custom-call(s32[2,256]{1,0:T(2,128)S(1)} %get-tuple-element.9.meta_ref, s32[1]{0:T(128)} %bitcast.5.me_ref, f32[4,256]{1,0:T(4,128)S(1)} %get-tuple-element.10.slots_ref, f32[2,1280,128]{2,1,0:T(8,128)S(1)} %get-tuple-element.11.rows_ref, f32[3,256]{1,0:T(4,128)S(1)} %copy-done.4, ...), custom_call_target="tpu_custom_call" | custom-call | flops 20000000000 | bytes 30000000 | tf_op jit(solution)/shard_map/render/pallas_call | solution.py:456
  68.3 11.2 %all_to_all.10 = f32[32,4,256]{2,1,0:T(4,128)S(1)} all-to-all(f32[32,4,256]{2,1,0:T(4,128)S(1)} %get-tuple-element.15), channel_id=1, replica_groups=mesh['region'=32] {'region'}, dimensions={0} | all-to-all | bytes 262144 | tf_op jit(solution)/shard_map/all_to_all | solution.py:481
  79.5 0.6 reduce_sum.9
  (1 shorter events, 0.0 us)
Async XLA Ops:
  0.6 1.0 %copy-start = (f32[256,3,128]{2,0,1:T(8,128)S(1)}, f32[256,3,128]{2,0,1:T(8,128)}, u32[]{:S(2)}) copy-start(f32[256,3,128]{2,0,1:T(8,128)} %param.7) | copy-start | bytes 1179652
  1.6 0.9 %copy-start.1 = (f32[256,128]{1,0:T(8,128)S(1)}, f32[256,128]{1,0:T(8,128)}, u32[]{:S(2)}) copy-start(f32[256,128]{1,0:T(8,128)} %spacing_ref.1) | copy-start | bytes 393220
  2.5 0.8 %copy-start.2 = (bf16[1,128,256]{2,1,0:T(8,128)(2,1)S(1)}, bf16[1,128,256]{2,1,0:T(8,128)(2,1)}, u32[]{:S(2)}) copy-start(bf16[1,128,256]{2,1,0:T(8,128)(2,1)} %param.12) | copy-start | bytes 196612
  3.4 0.7 copy-start.3
  4.1 0.7 copy-start.5
  4.7 0.7 copy-start.6
  8.2 22.0 %all-to-all-start = ((bf16[32,8,256]{2,1,0:T(8,128)(2,1)}), bf16[32,8,256]{2,1,0:T(8,128)(2,1)S(1)}, u32[]{:S(2)}, u32[]{:S(2)}) async-start(bf16[32,8,256]{2,1,0:T(8,128)(2,1)} %get-tuple-element.12), calls=%async_computation | async-start | bytes 262144 | tf_op jit(solution)/shard_map/all_to_all | solution.py:417
  15.5 6.3 %collective-permute-start = (bf16[1,256,128]{2,1,0:T(8,128)(2,1)S(1)}, bf16[1,256,128]{2,1,0:T(8,128)(2,1)S(1)}, u32[]{:S(2)}, u32[]{:S(2)}) collective-permute-start(bf16[1,256,128]{2,1,0:T(8,128)(2,1)S(1)} %bitcast.8), channel_id=1, source_target_pairs={{0,8},{1,9},{2,10},{3,11},{4,12},{5,13},{6,14},{7,15},{8,0},{9,1},... | collective-permute-start | bytes 196616 | tf_op jit(solution)/shard_map/ppermute | solution.py:371
  17.4 6.9 %collective-permute-start.1 = (bf16[1,256,128]{2,1,0:T(8,128)(2,1)S(1)}, bf16[1,256,128]{2,1,0:T(8,128)(2,1)S(1)}, u32[]{:S(2)}, u32[]{:S(2)}) collective-permute-start(bf16[1,256,128]{2,1,0:T(8,128)(2,1)S(1)} %bitcast.9), channel_id=1, source_target_pairs={{0,16},{1,17},{2,18},{3,19},{4,20},{5,21},{6,22},{7,23},{8,24},{9,... | collective-permute-start | bytes 196616 | tf_op jit(solution)/shard_map/ppermute | solution.py:371
  19.8 6.9 %collective-permute-start.2 = (bf16[1,256,128]{2,1,0:T(8,128)(2,1)S(1)}, bf16[1,256,128]{2,1,0:T(8,128)(2,1)S(1)}, u32[]{:S(2)}, u32[]{:S(2)}) collective-permute-start(bf16[1,256,128]{2,1,0:T(8,128)(2,1)S(1)} %bitcast.10), channel_id=1, source_target_pairs={{0,24},{1,25},{2,26},{3,27},{4,28},{5,29},{6,30},{7,31},{8,16},{9,... | collective-permute-start | bytes 196616 | tf_op jit(solution)/shard_map/ppermute | solution.py:371
  26.7 11.3 %collective-permute-start.3 = (bf16[4,256,128]{2,1,0:T(8,128)(2,1)S(1)}, bf16[4,256,128]{2,1,0:T(8,128)(2,1)S(1)}, u32[]{:S(2)}, u32[]{:S(2)}) collective-permute-start(bf16[4,256,128]{2,1,0:T(8,128)(2,1)S(1)} %pad_maximum_fusion.refs_0_), channel_id=1, source_target_pairs={{0,2},{1,3},{2,0},{3,1},{4,6},{5,7},{6,4},{7,5},{8,10},{9,11},{10,... | collective-permute-start | bytes 786440 | tf_op jit(solution)/shard_map/ppermute | solution.py:371
  28.3 13.1 %collective-permute-start.4 = (bf16[4,256,128]{2,1,0:T(8,128)(2,1)S(1)}, bf16[4,256,128]{2,1,0:T(8,128)(2,1)S(1)}, u32[]{:S(2)}, u32[]{:S(2)}) collective-permute-start(bf16[4,256,128]{2,1,0:T(8,128)(2,1)S(1)} %pad_maximum_fusion.refs_0_), channel_id=1, source_target_pairs={{0,4},{1,5},{2,6},{3,7},{4,0},{5,1},{6,2},{7,3},{8,12},{9,13},{10,... | collective-permute-start | bytes 786440 | tf_op jit(solution)/shard_map/ppermute | solution.py:371
  29.8 11.6 %collective-permute-start.5 = (bf16[4,256,128]{2,1,0:T(8,128)(2,1)S(1)}, bf16[4,256,128]{2,1,0:T(8,128)(2,1)S(1)}, u32[]{:S(2)}, u32[]{:S(2)}) collective-permute-start(bf16[4,256,128]{2,1,0:T(8,128)(2,1)S(1)} %pad_maximum_fusion.refs_0_), channel_id=1, source_target_pairs={{0,6},{1,7},{2,4},{3,5},{4,2},{5,3},{6,0},{7,1},{8,14},{9,15},{10,... | collective-permute-start | bytes 786440 | tf_op jit(solution)/shard_map/ppermute | solution.py:371
  30.3 14.3 %collective-permute-start.6 = (bf16[4,256,128]{2,1,0:T(8,128)(2,1)S(1)}, bf16[4,256,128]{2,1,0:T(8,128)(2,1)S(1)}, u32[]{:S(2)}, u32[]{:S(2)}) collective-permute-start(bf16[4,256,128]{2,1,0:T(8,128)(2,1)S(1)} %pad_maximum_fusion.refs_0_), channel_id=1, source_target_pairs={{0,1},{1,0},{2,3},{3,2},{4,5},{5,4},{6,7},{7,6},{8,9},{9,8},{10,11... | collective-permute-start | bytes 786440 | tf_op jit(solution)/shard_map/ppermute | solution.py:371
  38.0 6.7 %copy-start.4 = (f32[3,256]{1,0:T(4,128)S(1)}, f32[3,256]{1,0:T(4,128)}, u32[]{:S(2)}) copy-start(f32[3,256]{1,0:T(4,128)} %colour_grad_ref.1) | copy-start | bytes 9220
  38.0 6.6 %collective-permute-start.7 = (bf16[4,256,128]{2,1,0:T(8,128)(2,1)S(1)}, bf16[4,256,128]{2,1,0:T(8,128)(2,1)S(1)}, u32[]{:S(2)}, u32[]{:S(2)}) collective-permute-start(bf16[4,256,128]{2,1,0:T(8,128)(2,1)S(1)} %collective-permute-done.3.refs_1_), channel_id=1, source_target_pairs={{0,1},{1,0},{2,3},{3,2},{4,5},{5,4},{6,7},{7,6},{8,9},{9,8},{10,11... | collective-permute-start | bytes 786440 | tf_op jit(solution)/shard_map/ppermute | solution.py:371
  41.4 3.2 %collective-permute-start.8 = (bf16[4,256,128]{2,1,0:T(8,128)(2,1)S(1)}, bf16[4,256,128]{2,1,0:T(8,128)(2,1)S(1)}, u32[]{:S(2)}, u32[]{:S(2)}) collective-permute-start(bf16[4,256,128]{2,1,0:T(8,128)(2,1)S(1)} %collective-permute-done.4.refs_2_), channel_id=1, source_target_pairs={{0,1},{1,0},{2,3},{3,2},{4,5},{5,4},{6,7},{7,6},{8,9},{9,8},{10,11... | collective-permute-start | bytes 786440 | tf_op jit(solution)/shard_map/ppermute | solution.py:371
  41.4 3.2 %collective-permute-start.9 = (bf16[4,256,128]{2,1,0:T(8,128)(2,1)S(1)}, bf16[4,256,128]{2,1,0:T(8,128)(2,1)S(1)}, u32[]{:S(2)}, u32[]{:S(2)}) collective-permute-start(bf16[4,256,128]{2,1,0:T(8,128)(2,1)S(1)} %collective-permute-done.5.refs_3_), channel_id=1, source_target_pairs={{0,1},{1,0},{2,3},{3,2},{4,5},{5,4},{6,7},{7,6},{8,9},{9,8},{10,11... | collective-permute-start | bytes 786440 | tf_op jit(solution)/shard_map/ppermute | solution.py:371

commit v2 on v1

--- a/solution.py
+++ b/solution.py
@@ -52,30 +52,10 @@
     return jnp.where(condition, 1.0, 0.0).astype(BF16)
 
 
-def order_kernel(
-    dims,
-    crossed_ref,
-    points_ref,
-    spacing_ref,
-    freq_ref,
-    hidden_w_ref,
-    head_w_ref,
-    slots_ref,
-    meta_ref,
-    rows_ref,
-    turned_ref,
-    small_ref,
-):
+def order_kernel(dims, samples_ref, crossed_ref, slots_ref, meta_ref, rows_ref):
     regions, rays, crossings, samples, tiles = dims
     lanes = crossings * samples
     width = meta_ref.shape[1]
-    turned_ref[...] = hidden_w_ref[...].astype(F32).T.astype(BF16)
-    freqs = freq_ref.shape[1]
-    small_ref[...] = jnp.zeros(small_ref.shape, BF16)
-    for region in range(regions):
-        small_ref[region, :4, :] = head_w_ref[...]
-        small_ref[region, 4:7, :freqs] = freq_ref[...]
-
     region_at = iota((regions, rays), 0)
     named = [jnp.where(crossed_ref[k : k + 1, :] == region_at, 1.0, 0.0) for k in range(crossings)]
     listed = functools.reduce(jnp.add, named)
@@ -95,7 +75,7 @@
     meta_ref[...] = jnp.concatenate([owner, used], axis=0).astype(jnp.int32)
 
     slot_row = jnp.concatenate(slot_rows, axis=1)
-    parts = [points_ref[d] * TURN for d in range(3)] + [spacing_ref[...]]
+    parts = [samples_ref[d] * TURN for d in range(3)] + [samples_ref[3]]
     lane_group = iota((rays, lanes), 1) // samples
     by_segment = []
     for k in range(crossings):
@@ -128,64 +108,39 @@
             rows_ref[half, pl.ds(4 + d, tiles, stride=8), :] = dense[d][half]
 
 
-def steps_used(meta, step):
-    return jnp.minimum(step, (meta[1, 0] - 1) // UNROLL)
-
-
-def feature_kernel(first, meta_ref, rows_ref, small_ref, *refs):
-    feature_ref = refs[-1]
-    used = meta_ref[1, 0]
-    step = first + pl.program_id(0)
-    rows = feature_ref.shape[0] // UNROLL
-    half = rows // 2
-
-    def phases(index):
-        small = small_ref[meta_ref[0, step * UNROLL + index]][:, :128].astype(F32)
-        freq = jnp.concatenate([small] * 3, axis=0).T[:half].astype(BF16)
-        return dot(freq, stacked(joined(rows_ref, pl.ds(index * 8, 8)), 0, 3))
-
-    def store(index, turns):
-        for at in range(0, half, 16):
-            part = turns[at : at + 16]
-            rest = part - ((part + ROUNDER) - ROUNDER)
-            square = rest * rest
-            sine = jnp.full_like(square, SIN_HALF[-1])
-            for c in SIN_HALF[-2::-1]:
-                sine = sine * square + c
-            sine = sine * rest
-            twice = sine * sine
-            left = jnp.maximum(2.0 - twice, 1e-30)
-            first = index * rows + at
-            feature_ref[first : first + 16, :] = (sine * (left * lax.rsqrt(left))).astype(BF16)
-            first = first + half
-            feature_ref[first : first + 16, :] = (1.0 - twice).astype(BF16)
-
-    @pl.when(step * UNROLL < used)
-    def _():
-        ahead = phases(0)
-        for index in range(UNROLL):
-            turns = ahead
-            if index + 1 < UNROLL:
-                ahead = phases(index + 1)
-            store(index, turns)
+def tile_rows(tile, height):
+    return pl.ds(pl.multiple_of(tile * height, height), height)
+
+
+def phases_of(tile, half, meta_ref, rows_ref, small_ref):
+    small = small_ref[meta_ref[0, tile]][:, :128].astype(F32)
+    freq = jnp.concatenate([small] * 3, axis=0).T[:half].astype(BF16)
+    return dot(freq, stacked(joined(rows_ref, tile_rows(tile, 8)), 0, 3))
+
+
+def store_features(turns, feature_ref, first):
+    half = turns.shape[0]
+    for at in range(0, half, 16):
+        part = turns[at : at + 16]
+        rest = part - ((part + ROUNDER) - ROUNDER)
+        square = rest * rest
+        sine = jnp.full_like(square, SIN_HALF[-1])
+        for c in SIN_HALF[-2::-1]:
+            sine = sine * square + c
+        sine = sine * rest
+        twice = sine * sine
+        left = jnp.maximum(2.0 - twice, 1e-30)
+        rows = slice(first + at, first + at + 16)
+        feature_ref[rows, :] = (sine * (left * lax.rsqrt(left))).astype(BF16)
+        rows = slice(first + half + at, first + half + at + 16)
+        feature_ref[rows, :] = (1.0 - twice).astype(BF16)
 
 
 def main_kernel(
-    dims,
-    stages,
-    parts,
-    meta_ref,
-    me_ref,
-    slots_ref,
-    rows_ref,
-    colour_grad_ref,
-    head_ref,
-    feature_ref,
-    *refs,
+    dims, stages, parts, meta_ref, me_ref, slots_ref, rows_ref, colour_grad_ref, small_ref, *refs
 ):
     part_refs = refs[:parts]
-    rendered_ref, head_grad_ref = refs[parts : parts + 2]
-    hidden_ref, raw_ref, grad_ref, weight_ref, slab_ref, weight_sems, slab_sems = refs[parts + 2 :]
+    rendered_ref, head_grad_ref, hidden_ref, raw_ref, weight_ref, slab_ref, sems = refs[parts:]
     regions, rays, crossings, samples, tiles = dims
     width = GROUP * samples
     halves, lanes = raw_ref.shape[0], raw_ref.shape[2]
@@ -196,57 +151,56 @@
     depth = slab_ref.shape[1] // UNROLL
     held = regions // parts
 
-    def fetch(step, slot):
-        at = pl.multiple_of(step * (UNROLL * depth), UNROLL * depth)
-        return pltpu.make_async_copy(
-            feature_ref.at[pl.ds(at, UNROLL * depth), :], slab_ref.at[slot], slab_sems.at[slot]
-        )
-
     copies = [
-        pltpu.make_async_copy(
-            part_refs[p], weight_ref.at[p * held : (p + 1) * held], weight_sems.at[p]
-        )
+        pltpu.make_async_copy(part_refs[p], weight_ref.at[p * held : (p + 1) * held], sems.at[p])
         for p in range(parts)
     ]
-    fetch(0, 0).start()
     for copy in copies:
         copy.start()
+
+    def phases(tile):
+        return phases_of(tile, depth // 2, meta_ref, rows_ref, small_ref)
+
+    ahead = phases(0)
+    for index in range(UNROLL):
+        turns = ahead
+        if index + 1 < UNROLL:
+            ahead = phases(index + 1)
+        store_features(turns, slab_ref.at[0], index * depth)
     for copy in copies:
         copy.wait()
 
-    def rows_of(tile, height):
-        return pl.ds(pl.multiple_of(tile * height, height), height)
-
-    def forward(step, _):
+    def work(step, more):
+        first = step * UNROLL
         slot = lax.rem(step, 2)
 
-        @pl.when(step + 1 < rounds)
-        def _():
-            fetch(step + 1, 1 - slot).start()
-
-        fetch(step, slot).wait()
-        first = step * UNROLL
-        named = [meta_ref[0, first + index] for index in range(UNROLL)]
-
         def layer(index):
-            weights = weight_ref[place(named[index] ^ me, stages)]
+            weights = weight_ref[place(meta_ref[0, first + index] ^ me, stages)]
             return dot(weights, slab_ref[slot, index * depth : (index + 1) * depth, :])
 
         ahead = layer(0)
+        turns_ahead = phases(first + UNROLL) if more else None
         for index in range(UNROLL):
-            result = ahead
+            result, turns = ahead, turns_ahead
             if index + 1 < UNROLL:
                 ahead = layer(index + 1)
+                turns_ahead = phases(first + UNROLL + index + 1) if more else None
             head(jnp.maximum(first - UNROLL, 0) + index)
-            hidden_ref[rows_of(first + index, units), :] = jnp.maximum(result.astype(BF16), 0)
+            if more:
+                store_features(turns, slab_ref.at[1 - slot], index * depth)
+            hidden_ref[tile_rows(first + index, units), :] = jnp.maximum(result.astype(BF16), 0)
+
+    def forward(step, _):
+        work(step, True)
         return 0
 
     def head(tile):
-        raw = dot(head_ref[meta_ref[0, tile]], hidden_ref[rows_of(tile, units), :])
+        raw = dot(small_ref[meta_ref[0, tile]], hidden_ref[tile_rows(tile, units), :])
         for half in range(halves):
-            raw_ref[half, rows_of(tile, 8), :] = raw[:, half * lanes : (half + 1) * lanes]
-
-    lax.fori_loop(0, rounds, forward, 0)
+            raw_ref[half, tile_rows(tile, 8), :] = raw[:, half * lanes : (half + 1) * lanes]
+
+    lax.fori_loop(0, rounds - 1, forward, 0)
+    work(rounds - 1, False)
     for index in range(UNROLL):
         head((rounds - 1) * UNROLL + index)
 
@@ -326,7 +280,7 @@
     for c in range(4):
         for half in range(halves):
             at = pl.ds(c, tiles, stride=8)
-            grad_ref[half, at, :] = raw_grad[c][:, half * lanes : (half + 1) * lanes]
+            raw_ref[half, at, :] = raw_grad[c][:, half * lanes : (half + 1) * lanes]
 
     head_grad_ref[...] = jnp.zeros(head_grad_ref.shape, F32)
 
@@ -334,8 +288,8 @@
         first = step * UNROLL
         products = []
         for index in range(UNROLL):
-            gradient = joined(grad_ref, rows_of(first + index, 8)).astype(BF16)
-            products.append(dot_nt(gradient, hidden_ref[rows_of(first + index, units), :])[:4])
+            gradient = joined(raw_ref, tile_rows(first + index, 8)).astype(BF16)
+            products.append(dot_nt(gradient, hidden_ref[tile_rows(first + index, units), :])[:4])
         for index in range(UNROLL):
             head_grad_ref[meta_ref[0, first + index]] += products[index]
         return 0
@@ -361,14 +315,12 @@
     return at
 
 
-def share_all(value, stages, count):
-    held = [value[None]]
-    for unit, size in stages:
-        sent = held if (unit, size) == stages[-1] else [jnp.concatenate(held, axis=0)]
-        held = list(sent)
-        for other in range(1, size):
-            pairs = [(i, i ^ (unit * other)) for i in range(count)]
-            held += [lax.ppermute(piece, "region", pairs) for piece in sent]
+def share(block, stage, count):
+    unit, size = stage
+    held = [block]
+    for other in range(1, size):
+        pairs = [(i, i ^ (unit * other)) for i in range(count)]
+        held.append(lax.ppermute(block, "region", pairs))
     return held
 
 
@@ -386,73 +338,47 @@
     dims = (regions, rays, crossings, samples, tiles)
     vmem, smem = pltpu.VMEM, pltpu.SMEM
     mib = 1024 * 1024
-    limit = 24 * mib
+    limit = 2 * tiles * width * hidden_units + 8 * halves * tiles * 8 * lanes
+    limit += 2 * regions * hidden_units * features + 4 * mib
+    limit += 2 * 2 * UNROLL * features * width + 4 * mib
+    small_limit = 24 * mib
+    params = pltpu.CompilerParams(vmem_limit_bytes=limit)
 
     me = lax.axis_index("region").astype(jnp.int32).reshape(1)
     meta_width = -(-tiles // 128) * 128
-    slots, meta, rows, turned, small = pl.pallas_call(
+    stages = exchange_stages(regions)
+    all_samples = jnp.concatenate([sample_points.transpose(1, 0, 2), sample_spacing[None]], axis=0)
+    weights = share(w_hidden[0].T[None], stages[0], regions)
+    slots, meta, rows = pl.pallas_call(
         functools.partial(order_kernel, dims),
         out_shape=(
             jax.ShapeDtypeStruct((crossings, rays), F32),
             jax.ShapeDtypeStruct((2, meta_width), jnp.int32),
             jax.ShapeDtypeStruct((halves, tiles * 8, lanes), F32),
-            jax.ShapeDtypeStruct((hidden_units, features), BF16),
-            jax.ShapeDtypeStruct((regions, 8, hidden_units), BF16),
         ),
-        in_specs=[pl.BlockSpec(memory_space=vmem)] * 6,
-        out_specs=[pl.BlockSpec(memory_space=vmem)] * 5,
-        compiler_params=pltpu.CompilerParams(vmem_limit_bytes=limit),
+        in_specs=[pl.BlockSpec(memory_space=vmem)] * 2,
+        out_specs=[pl.BlockSpec(memory_space=vmem)] * 3,
+        compiler_params=pltpu.CompilerParams(vmem_limit_bytes=small_limit),
         cost_estimate=pl.CostEstimate(flops=4 * 10**9, bytes_accessed=10**7, transcendentals=0),
         name="order",
-    )(
-        crossed.T,
-        sample_points.transpose(1, 0, 2),
-        sample_spacing,
-        freq[0],
-        w_hidden[0],
-        w_head[0],
-    )
-
-    stages = exchange_stages(regions)
+    )(all_samples, crossed.T)
+
+    small = jnp.pad(freq[0], ((0, 1), (0, hidden_units - freq.shape[2])))
+    small = jnp.concatenate([w_head[0], small], axis=0)
+    small = jnp.broadcast_to(small[None], (regions, 8, hidden_units))
+    block, small = lax.optimization_barrier((jnp.concatenate(weights, axis=0), small))
+    weights = share(block, stages[1], regions)
+    for stage in stages[2:-1]:
+        weights = share(jnp.concatenate(weights, axis=0), stage, regions)
+    own = share(weights[0], stages[-1], regions)
+    own[-1], small = lax.optimization_barrier((own[-1], small))
     all_small = lax.all_to_all(small, "region", split_axis=0, concat_axis=0, tiled=True)
-    weights = share_all(turned, stages, regions)
-
-    steps = tiles // UNROLL
-    split = steps * 7 // 10
+    all_small, *others = lax.optimization_barrier((all_small, *weights[1:]))
+    swapped = [own] + [share(block, stages[-1], regions) for block in others]
+    weights = [blocks[i] for i in range(stages[-1][1]) for blocks in swapped]
+
     whole = pl.BlockSpec(memory_space=vmem)
-    params = pltpu.CompilerParams(vmem_limit_bytes=limit)
-
-    def row_block(begin=0):
-        return pl.BlockSpec(
-            (halves, UNROLL * 8, lanes), lambda i, m: (0, steps_used(m, i + begin), 0)
-        )
-
-    def features_of(first, last, *before):
-        return pl.pallas_call(
-            functools.partial(feature_kernel, first),
-            out_shape=jax.ShapeDtypeStruct((tiles * features, width), BF16),
-            grid_spec=pltpu.PrefetchScalarGridSpec(
-                num_scalar_prefetch=1,
-                grid=(last - first + 1,),
-                in_specs=[row_block(first), whole]
-                + [pl.BlockSpec(memory_space=pl.ANY)] * len(before),
-                out_specs=pl.BlockSpec(
-                    (UNROLL * features, width),
-                    lambda i, m: (jnp.maximum(steps_used(m, i + first), first), 0),
-                ),
-            ),
-            input_output_aliases={3: 0} if before else {},
-            compiler_params=params,
-            cost_estimate=pl.CostEstimate(flops=10**10, bytes_accessed=10**7, transcendentals=0),
-            name="features",
-        )(meta, rows, all_small, *before)
-
-    feature = features_of(split, steps - 1, features_of(0, split - 1))
-
-    kept = 2 * tiles * hidden_units * width
-    kept += 4 * regions * hidden_units * features + 12 * halves * tiles * 8 * lanes
-    kept = min(60 * mib, kept + 4 * UNROLL * features * width + 8 * mib)
-    any_space = pl.BlockSpec(memory_space=pl.ANY)
+
     rendered, head_grad = pl.pallas_call(
         functools.partial(main_kernel, dims, stages, len(weights)),
         out_shape=(
@@ -461,22 +387,19 @@
         ),
         in_specs=[pl.BlockSpec(memory_space=smem)] * 2
         + [whole] * 4
-        + [any_space]
-        + [whole] * len(weights),
+        + [pl.BlockSpec(memory_space=pl.ANY)] * len(weights),
         out_specs=[whole] * 2,
         scratch_shapes=[
             pltpu.VMEM((tiles * hidden_units, width), BF16),
             pltpu.VMEM((halves, tiles * 8, lanes), F32),
-            pltpu.VMEM((halves, tiles * 8, lanes), F32),
             pltpu.VMEM((regions, hidden_units, features), BF16),
             pltpu.VMEM((2, UNROLL * features, width), BF16),
             pltpu.SemaphoreType.DMA((len(weights),)),
-            pltpu.SemaphoreType.DMA((2,)),
         ],
-        compiler_params=pltpu.CompilerParams(vmem_limit_bytes=kept),
+        compiler_params=params,
         cost_estimate=pl.CostEstimate(flops=2 * 10**10, bytes_accessed=3 * 10**7, transcendentals=0),
         name="render",
-    )(meta, me, slots, rows, colour_grad, all_small, feature, *weights)
+    )(meta, me, slots, rows, colour_grad, all_small, *weights)
 
     partial_sums = lax.all_to_all(head_grad, "region", split_axis=0, concat_axis=0, tiled=True)
     head_grad = jnp.sum(partial_sums, axis=0, keepdims=True)

time: 81 us -> 71.3 us (0.88); the launches traced: 80.1 us -> 72.2 us
  Pallas kernels: 36.8 us -> 26.6 us
  blocking collectives: 11.2 us -> 14.4 us
  local copies, waits for them, and re-layouts: 4.78 us -> 1.67 us
  waiting for transfers between devices: 9.52 us -> 11.7 us
  other arithmetic: 0.67 us -> 2.33 us
  starting transfers between devices: 16.4 us -> 14.8 us
    pallas_call x2 -> x0, Pallas kernels: 10.4 us -> none  [features_of(): pl.pallas_call(functools.partial(feature_kernel, first), out_shape=jax.Sh...]
    unnamed x14 -> x7, local copies, waits for them, and re-layouts: 4.78 us -> 1.01 us
    all_to_all x1, blocking collectives: 11.2 us -> 14.4 us  [on_device(): lax.all_to_all(head_grad, 'region', split_axis=0, concat_axis=0, tiled=True)]
    all_to_all x1, starting transfers between devices: 7.3 us -> 4.97 us  [on_device(): lax.all_to_all(small, 'region', split_axis=0, concat_axis=0, tiled=True)]
    ppermute x10, waiting for transfers between devices: 9.52 us -> 11.6 us  [share(): held.append(lax.ppermute(block, 'region', pairs))]
    concatenate x1 -> x3, other arithmetic: 0.04 us -> 1.69 us  [the longest x1 0.95 us: on_device(): jnp.concatenate([sample_points.transpose(1, 0, 2), sample_spacing[None]],...]
  transfers between devices with their start and end apart: 11 -> 11, of which waited for: 4 -> 4; matrix products, arithmetic and copies ran while one was open for 0% -> 2% of each run, Pallas kernels for 13% -> 3%
where the time goes in v2:
time: 71.3 us; the launch traced here: 72.2 us
  Pallas kernels  26.6 us (37%)
  starting transfers between devices  14.8 us (21%)
  blocking collectives  14.4 us (20%)
  waiting for transfers between devices  11.7 us (16%)
  other arithmetic  2.33 us (3%)
  local copies, waits for them, and re-layouts  1.67 us (2%)
  between operations  0.74 us (1%)
    pallas_call x1, Pallas kernels, on_device(): pl.pallas_call(functools.partial(main_kernel, dims, stages, len(weights))...  24.5 us
    all_to_all x1, blocking collectives, on_device(): lax.all_to_all(head_grad, 'region', split_axis=0, concat_axis=0, tiled=True)  14.4 us
    ppermute x10, waiting for transfers between devices, share(): held.append(lax.ppermute(block, 'region', pairs))  11.6 us
    ppermute x10, starting transfers between devices, share(): held.append(lax.ppermute(block, 'region', pairs))  9.78 us
    all_to_all x1, starting transfers between devices, on_device(): lax.all_to_all(small, 'region', split_axis=0, concat_axis=0, tiled=True)  4.97 us
    pallas_call x1, Pallas kernels, on_device(): pl.pallas_call(functools.partial(order_kernel, dims), out_shape=(jax.Shap...  2.09 us
  transfers between devices with their start and end apart: 11, of which 4 were waited for; matrix products, arithmetic and copies ran while one was open for 2% of the time, Pallas kernels for 3%

profile of v2, /device:TPU:0, one launch (start us, length us, event | category | flops | bytes accessed | tf_op | source)
XLA Modules:
  0.0 72.2 jit_solution(8030096851423554113)
XLA Ops:
  0.6 0.0 copy-start.2
  0.6 0.0 copy-start
  0.6 1.0 %copy.9 = bf16[1,128,256]{1,2,0:T(8,128)(2,1)S(1)} copy(bf16[1,128,256]{2,1,0:T(8,128)(2,1)} %param.12) | data formatting | bytes 131072 | tf_op args[5]
  1.7 5.1 %collective-permute-start.2 = (bf16[1,256,128]{2,1,0:T(8,128)(2,1)S(1)}, bf16[1,256,128]{2,1,0:T(8,128)(2,1)S(1)}, u32[]{:S(2)}, u32[]{:S(2)}) collective-permute-start(bf16[1,256,128]{2,1,0:T(8,128)(2,1)S(1)} %bitcast.14), channel_id=1, source_target_pairs={{0,24},{1,25},{2,26},{3,27},{4,28},{5,29},{6,30},{7,31},{8,16},{9,... | collective-permute-start | bytes 196616 | tf_op jit(solution)/shard_map/ppermute | solution.py:323
  6.8 0.0 collective-permute-start.1
  6.8 0.6 collective-permute-start
  7.4 0.7 fusion.1
  8.1 1.2 %collective-permute-done.2 = bf16[1,256,128]{2,1,0:T(8,128)(2,1)S(1)} collective-permute-done((bf16[1,256,128]{2,1,0:T(8,128)(2,1)S(1)}, bf16[1,256,128]{2,1,0:T(8,128)(2,1)S(1)}, u32[]{:S(2)}, u32[]{:S(2)}) %collective-permute-start.2) | collective-permute-done | bytes 65568 | tf_op jit(solution)/shard_map/ppermute | solution.py:323
  9.3 3.0 %collective-permute-done.1 = bf16[1,256,128]{2,1,0:T(8,128)(2,1)S(1)} collective-permute-done((bf16[1,256,128]{2,1,0:T(8,128)(2,1)S(1)}, bf16[1,256,128]{2,1,0:T(8,128)(2,1)S(1)}, u32[]{:S(2)}, u32[]{:S(2)}) %collective-permute-start.1) | collective-permute-done | bytes 65568 | tf_op jit(solution)/shard_map/ppermute | solution.py:323
  12.4 0.0 collective-permute-done
  12.4 0.7 broadcast_in_dim.17
  13.1 0.0 collective-permute-start.3
  13.1 1.5 %collective-permute-start.4 = (bf16[4,256,128]{2,1,0:T(8,128)(2,1)S(1)}, bf16[4,256,128]{2,1,0:T(8,128)(2,1)S(1)}, u32[]{:S(2)}, u32[]{:S(2)}) collective-permute-start(bf16[4,256,128]{2,1,0:T(8,128)(2,1)S(1)} %pad_maximum_fusion.1.refs_0_), channel_id=1, source_target_pairs={{0,2},{1,3},{2,0},{3,1},{4,6},{5,7},{6,4},{7,5},{8,10},{9,11},{10,... | collective-permute-start | bytes 786440 | tf_op jit(solution)/shard_map/ppermute | solution.py:323
  14.6 1.5 %collective-permute-start.5 = (bf16[4,256,128]{2,1,0:T(8,128)(2,1)S(1)}, bf16[4,256,128]{2,1,0:T(8,128)(2,1)S(1)}, u32[]{:S(2)}, u32[]{:S(2)}) collective-permute-start(bf16[4,256,128]{2,1,0:T(8,128)(2,1)S(1)} %pad_maximum_fusion.1.refs_0_), channel_id=1, source_target_pairs={{0,4},{1,5},{2,6},{3,7},{4,0},{5,1},{6,2},{7,3},{8,12},{9,13},{10,... | collective-permute-start | bytes 786440 | tf_op jit(solution)/shard_map/ppermute | solution.py:323
  16.1 0.5 collective-permute-start.6
  16.6 0.0 collective-permute-done.3.refs_4_
  16.6 5.0 %all-to-all-start = ((bf16[32,8,256]{2,1,0:T(8,128)(2,1)}), bf16[32,8,256]{2,1,0:T(8,128)(2,1)S(1)}, u32[]{:S(2)}, u32[]{:S(2)}) async-start(bf16[32,8,256]{2,1,0:T(8,128)(2,1)} %broadcast_in_dim.17), calls=%async_computation | async-start | bytes 262144 | tf_op jit(solution)/shard_map/all_to_all | solution.py:375
  21.5 0.0 copy-done.2
  21.6 0.9 %pad_maximum_fusion.samples_ref = f32[4,256,128]{2,1,0:T(8,128)S(1)} fusion(f32[1,256,128]{2,1,0:T(8,128)} %bitcast.18, f32[3,256,128]{2,1,0:T(8,128)S(1)} %bitcast.13), kind=kLoop, calls=%fused_computation | loop fusion | flops 131072 | bytes 1048576 | tf_op jit(solution)/shard_map/concatenate | solution.py:350
  22.5 0.0 collective-permute-done.4.refs_1_
  22.5 7.4 %collective-permute-done.5.refs_2_ = bf16[4,256,128]{2,1,0:T(8,128)(2,1)S(1)} collective-permute-done((bf16[4,256,128]{2,1,0:T(8,128)(2,1)S(1)}, bf16[4,256,128]{2,1,0:T(8,128)(2,1)S(1)}, u32[]{:S(2)}, u32[]{:S(2)}) %collective-permute-start.5) | collective-permute-done | bytes 262176 | tf_op jit(solution)/shard_map/ppermute | solution.py:323
  29.9 0.0 collective-permute-done.6.refs_3_
  29.9 0.1 all-to-all-done.small_ref
  30.0 0.0 collective-permute-start.7
  30.0 0.5 collective-permute-start.8
  30.5 0.0 collective-permute-start.9
  30.5 0.0 copy-done
  30.5 0.0 copy-start.1
  30.5 2.1 %order.1 = (f32[4,256]{1,0:T(4,128)S(1)}, s32[2,256]{1,0:T(2,128)S(1)}, f32[2,1280,128]{2,1,0:T(8,128)S(1)}) custom-call(f32[4,256,128]{2,1,0:T(8,128)S(1)} %pad_maximum_fusion.samples_ref, s32[4,256]{1,0:T(4,128)S(1)} %bitcast.12), custom_call_target="tpu_custom_call" | custom-call | flops 4000000000 | bytes 10000000 | tf_op jit(solution)/shard_map/order/pallas_call | solution.py:352
  32.6 0.0 collective-permute-done.7.refs_5_
  32.6 0.0 collective-permute-done.8.refs_6_
  32.6 0.0 collective-permute-done.9.refs_7_
  32.7 0.0 copy-done.1
  32.7 24.5 %render.1 = (f32[3,256]{1,0:T(4,128)}, f32[32,4,256]{2,1,0:T(4,128)S(1)}) custom-call(s32[2,256]{1,0:T(2,128)S(1)} %get-tuple-element.15.meta_ref, s32[1]{0:T(128)} %bitcast.3.me_ref, f32[4,256]{1,0:T(4,128)S(1)} %get-tuple-element.16.slots_ref, f32[2,1280,128]{2,1,0:T(8,128)S(1)} %get-tuple-element.17.rows_ref, f32[3,256]{1,0:T(4,128)S(1)} %copy-done.1, ...), custom_call_target="tpu_custom_call" | custom-call | flops 20000000000 | bytes 30000000 | tf_op jit(solution)/shard_map/render/pallas_call | solution.py:382
  57.1 14.4 %all_to_all.10 = f32[32,4,256]{2,1,0:T(4,128)S(1)} all-to-all(f32[32,4,256]{2,1,0:T(4,128)S(1)} %get-tuple-element.27), channel_id=1, replica_groups=mesh['region'=32] {'region'}, dimensions={0} | all-to-all | bytes 262144 | tf_op jit(solution)/shard_map/all_to_all | solution.py:404
  71.6 0.6 reduce_sum.9
  (1 shorter events, 0.0 us)
Async XLA Ops:
  0.6 20.9 %copy-start.2 = (f32[256,3,128]{2,0,1:T(8,128)S(1)}, f32[256,3,128]{2,0,1:T(8,128)}, u32[]{:S(2)}) copy-start(f32[256,3,128]{2,0,1:T(8,128)} %param.7) | copy-start | bytes 1179652
  0.6 29.9 %copy-start = (s32[256,4]{0,1:T(4,128)S(1)}, s32[256,4]{0,1:T(4,128)}, u32[]{:S(2)}) copy-start(s32[256,4]{0,1:T(4,128)} %param.9) | copy-start | bytes 12292
  1.7 7.7 %collective-permute-start.2 = (bf16[1,256,128]{2,1,0:T(8,128)(2,1)S(1)}, bf16[1,256,128]{2,1,0:T(8,128)(2,1)S(1)}, u32[]{:S(2)}, u32[]{:S(2)}) collective-permute-start(bf16[1,256,128]{2,1,0:T(8,128)(2,1)S(1)} %bitcast.14), channel_id=1, source_target_pairs={{0,24},{1,25},{2,26},{3,27},{4,28},{5,29},{6,30},{7,31},{8,16},{9,... | collective-permute-start | bytes 196616 | tf_op jit(solution)/shard_map/ppermute | solution.py:323
  6.8 5.6 %collective-permute-start.1 = (bf16[1,256,128]{2,1,0:T(8,128)(2,1)S(1)}, bf16[1,256,128]{2,1,0:T(8,128)(2,1)S(1)}, u32[]{:S(2)}, u32[]{:S(2)}) collective-permute-start(bf16[1,256,128]{2,1,0:T(8,128)(2,1)S(1)} %bitcast.15), channel_id=1, source_target_pairs={{0,16},{1,17},{2,18},{3,19},{4,20},{5,21},{6,22},{7,23},{8,24},{9,... | collective-permute-start | bytes 196616 | tf_op jit(solution)/shard_map/ppermute | solution.py:323
  6.8 5.6 %collective-permute-start = (bf16[1,256,128]{2,1,0:T(8,128)(2,1)S(1)}, bf16[1,256,128]{2,1,0:T(8,128)(2,1)S(1)}, u32[]{:S(2)}, u32[]{:S(2)}) collective-permute-start(bf16[1,256,128]{2,1,0:T(8,128)(2,1)S(1)} %bitcast.16), channel_id=1, source_target_pairs={{0,8},{1,9},{2,10},{3,11},{4,12},{5,13},{6,14},{7,15},{8,0},{9,1},... | collective-permute-start | bytes 196616 | tf_op jit(solution)/shard_map/ppermute | solution.py:323
  13.1 3.5 %collective-permute-start.3 = (bf16[4,256,128]{2,1,0:T(8,128)(2,1)S(1)}, bf16[4,256,128]{2,1,0:T(8,128)(2,1)S(1)}, u32[]{:S(2)}, u32[]{:S(2)}) collective-permute-start(bf16[4,256,128]{2,1,0:T(8,128)(2,1)S(1)} %pad_maximum_fusion.1.refs_0_), channel_id=1, source_target_pairs={{0,1},{1,0},{2,3},{3,2},{4,5},{5,4},{6,7},{7,6},{8,9},{9,8},{10,11... | collective-permute-start | bytes 786440 | tf_op jit(solution)/shard_map/ppermute | solution.py:323
  13.1 9.4 %collective-permute-start.4 = (bf16[4,256,128]{2,1,0:T(8,128)(2,1)S(1)}, bf16[4,256,128]{2,1,0:T(8,128)(2,1)S(1)}, u32[]{:S(2)}, u32[]{:S(2)}) collective-permute-start(bf16[4,256,128]{2,1,0:T(8,128)(2,1)S(1)} %pad_maximum_fusion.1.refs_0_), channel_id=1, source_target_pairs={{0,2},{1,3},{2,0},{3,1},{4,6},{5,7},{6,4},{7,5},{8,10},{9,11},{10,... | collective-permute-start | bytes 786440 | tf_op jit(solution)/shard_map/ppermute | solution.py:323
  14.6 15.3 %collective-permute-start.5 = (bf16[4,256,128]{2,1,0:T(8,128)(2,1)S(1)}, bf16[4,256,128]{2,1,0:T(8,128)(2,1)S(1)}, u32[]{:S(2)}, u32[]{:S(2)}) collective-permute-start(bf16[4,256,128]{2,1,0:T(8,128)(2,1)S(1)} %pad_maximum_fusion.1.refs_0_), channel_id=1, source_target_pairs={{0,4},{1,5},{2,6},{3,7},{4,0},{5,1},{6,2},{7,3},{8,12},{9,13},{10,... | collective-permute-start | bytes 786440 | tf_op jit(solution)/shard_map/ppermute | solution.py:323
  16.1 13.8 %collective-permute-start.6 = (bf16[4,256,128]{2,1,0:T(8,128)(2,1)S(1)}, bf16[4,256,128]{2,1,0:T(8,128)(2,1)S(1)}, u32[]{:S(2)}, u32[]{:S(2)}) collective-permute-start(bf16[4,256,128]{2,1,0:T(8,128)(2,1)S(1)} %pad_maximum_fusion.1.refs_0_), channel_id=1, source_target_pairs={{0,6},{1,7},{2,4},{3,5},{4,2},{5,3},{6,0},{7,1},{8,14},{9,15},{10,... | collective-permute-start | bytes 786440 | tf_op jit(solution)/shard_map/ppermute | solution.py:323
  16.6 13.4 %all-to-all-start = ((bf16[32,8,256]{2,1,0:T(8,128)(2,1)}), bf16[32,8,256]{2,1,0:T(8,128)(2,1)S(1)}, u32[]{:S(2)}, u32[]{:S(2)}) async-start(bf16[32,8,256]{2,1,0:T(8,128)(2,1)} %broadcast_in_dim.17), calls=%async_computation | async-start | bytes 262144 | tf_op jit(solution)/shard_map/all_to_all | solution.py:375
  30.0 2.6 %collective-permute-start.7 = (bf16[4,256,128]{2,1,0:T(8,128)(2,1)S(1)}, bf16[4,256,128]{2,1,0:T(8,128)(2,1)S(1)}, u32[]{:S(2)}, u32[]{:S(2)}) collective-permute-start(bf16[4,256,128]{2,1,0:T(8,128)(2,1)S(1)} %collective-permute-done.4.refs_1_), channel_id=1, source_target_pairs={{0,1},{1,0},{2,3},{3,2},{4,5},{5,4},{6,7},{7,6},{8,9},{9,8},{10,11... | collective-permute-start | bytes 786440 | tf_op jit(solution)/shard_map/ppermute | solution.py:323
  30.0 2.6 %collective-permute-start.8 = (bf16[4,256,128]{2,1,0:T(8,128)(2,1)S(1)}, bf16[4,256,128]{2,1,0:T(8,128)(2,1)S(1)}, u32[]{:S(2)}, u32[]{:S(2)}) collective-permute-start(bf16[4,256,128]{2,1,0:T(8,128)(2,1)S(1)} %collective-permute-done.5.refs_2_), channel_id=1, source_target_pairs={{0,1},{1,0},{2,3},{3,2},{4,5},{5,4},{6,7},{7,6},{8,9},{9,8},{10,11... | collective-permute-start | bytes 786440 | tf_op jit(solution)/shard_map/ppermute | solution.py:323
  30.5 2.1 %collective-permute-start.9 = (bf16[4,256,128]{2,1,0:T(8,128)(2,1)S(1)}, bf16[4,256,128]{2,1,0:T(8,128)(2,1)S(1)}, u32[]{:S(2)}, u32[]{:S(2)}) collective-permute-start(bf16[4,256,128]{2,1,0:T(8,128)(2,1)S(1)} %collective-permute-done.6.refs_3_), channel_id=1, source_target_pairs={{0,1},{1,0},{2,3},{3,2},{4,5},{5,4},{6,7},{7,6},{8,9},{9,8},{10,11... | collective-permute-start | bytes 786440 | tf_op jit(solution)/shard_map/ppermute | solution.py:323
  30.5 2.1 %copy-start.1 = (f32[3,256]{1,0:T(4,128)S(1)}, f32[3,256]{1,0:T(4,128)}, u32[]{:S(2)}) copy-start(f32[3,256]{1,0:T(4,128)} %colour_grad_ref.1) | copy-start | bytes 9220

commit v3 on v2

--- a/solution.py
+++ b/solution.py
@@ -137,7 +137,17 @@
 
 
 def main_kernel(
-    dims, stages, parts, meta_ref, me_ref, slots_ref, rows_ref, colour_grad_ref, small_ref, *refs
+    dims,
+    stages,
+    parts,
+    moves,
+    meta_ref,
+    me_ref,
+    slots_ref,
+    rows_ref,
+    colour_grad_ref,
+    small_ref,
+    *refs,
 ):
     part_refs = refs[:parts]
     rendered_ref, head_grad_ref, hidden_ref, raw_ref, weight_ref, slab_ref, sems = refs[parts:]
@@ -149,12 +159,11 @@
     rounds = (used + (UNROLL - 1)) // UNROLL
     units = hidden_ref.shape[0] // tiles
     depth = slab_ref.shape[1] // UNROLL
-    held = regions // parts
-
-    copies = [
-        pltpu.make_async_copy(part_refs[p], weight_ref.at[p * held : (p + 1) * held], sems.at[p])
-        for p in range(parts)
-    ]
+
+    copies = []
+    for at, (part, row, to, count) in enumerate(moves):
+        source = part_refs[part].at[row : row + count]
+        copies.append(pltpu.make_async_copy(source, weight_ref.at[to : to + count], sems.at[at]))
     for copy in copies:
         copy.start()
 
@@ -348,7 +357,9 @@
     meta_width = -(-tiles // 128) * 128
     stages = exchange_stages(regions)
     all_samples = jnp.concatenate([sample_points.transpose(1, 0, 2), sample_spacing[None]], axis=0)
-    weights = share(w_hidden[0].T[None], stages[0], regions)
+    own = w_hidden[0].T[None]
+    first = share(own, stages[0], regions)
+    own_second = share(own, stages[1], regions)
     slots, meta, rows = pl.pallas_call(
         functools.partial(order_kernel, dims),
         out_shape=(
@@ -366,21 +377,44 @@
     small = jnp.pad(freq[0], ((0, 1), (0, hidden_units - freq.shape[2])))
     small = jnp.concatenate([w_head[0], small], axis=0)
     small = jnp.broadcast_to(small[None], (regions, 8, hidden_units))
-    block, small = lax.optimization_barrier((jnp.concatenate(weights, axis=0), small))
-    weights = share(block, stages[1], regions)
-    for stage in stages[2:-1]:
-        weights = share(jnp.concatenate(weights, axis=0), stage, regions)
-    own = share(weights[0], stages[-1], regions)
-    own[-1], small = lax.optimization_barrier((own[-1], small))
+    others = jnp.concatenate(first[1:], axis=0)
+    second = share(others, stages[1], regions)
+    parts = [block for pair in zip(own_second, second) for block in pair]
+    last = stages[-1]
+    if len(stages) > 3:
+        parts = [jnp.concatenate(parts, axis=0)]
+        for stage in stages[2:-1]:
+            parts = share(jnp.concatenate(parts, axis=0), stage, regions)
+        groups = [[i] for i in range(len(parts))]
+    else:
+        groups = [[0, 1], [2, 4, 6], [3], [5], [7]]
+    held = [part.shape[0] for part in parts]
+    places = [sum(held[:i]) for i in range(len(parts))]
+
+    def swap(group):
+        return share(jnp.concatenate([parts[i] for i in group], axis=0), last, regions)[1:]
+
+    swapped = [swap(groups[0])]
+    swapped[0][0], small = lax.optimization_barrier((swapped[0][0], small))
     all_small = lax.all_to_all(small, "region", split_axis=0, concat_axis=0, tiled=True)
-    all_small, *others = lax.optimization_barrier((all_small, *weights[1:]))
-    swapped = [own] + [share(block, stages[-1], regions) for block in others]
-    weights = [blocks[i] for i in range(stages[-1][1]) for blocks in swapped]
+    late = sorted(i for group in groups[2:] for i in group)
+    all_small, *tied = lax.optimization_barrier((all_small, *[parts[i] for i in late]))
+    for i, part in zip(late, tied):
+        parts[i] = part
+    swapped += [swap(group) for group in groups[1:]]
+    weights, moves = list(parts), [(i, 0, places[i], held[i]) for i in range(len(parts))]
+    for blocks, group in zip(swapped, groups):
+        for other, block in enumerate(blocks, 1):
+            row = 0
+            for i in group:
+                moves.append((len(weights), row, other * sum(held) + places[i], held[i]))
+                row += held[i]
+            weights.append(block)
 
     whole = pl.BlockSpec(memory_space=vmem)
 
     rendered, head_grad = pl.pallas_call(
-        functools.partial(main_kernel, dims, stages, len(weights)),
+        functools.partial(main_kernel, dims, stages, len(weights), moves),
         out_shape=(
             jax.ShapeDtypeStruct((3, rays), F32),
             jax.ShapeDtypeStruct((regions, 4, hidden_units), F32),
@@ -394,7 +428,7 @@
             pltpu.VMEM((halves, tiles * 8, lanes), F32),
             pltpu.VMEM((regions, hidden_units, features), BF16),
             pltpu.VMEM((2, UNROLL * features, width), BF16),
-            pltpu.SemaphoreType.DMA((len(weights),)),
+            pltpu.SemaphoreType.DMA((len(moves),)),
         ],
         compiler_params=params,
         cost_estimate=pl.CostEstimate(flops=2 * 10**10, bytes_accessed=3 * 10**7, transcendentals=0),

time: 71.3 us -> 76.2 us (1.069); the launches traced: 72.2 us -> 76 us
  starting transfers between devices: 14.8 us -> 19.7 us
  Pallas kernels: 26.6 us -> 29.2 us
  blocking collectives: 14.4 us -> 12 us
  other arithmetic: 2.33 us -> 1.45 us
    ppermute x10 -> x14, starting transfers between devices: 9.78 us -> 14.8 us  [share(): held.append(lax.ppermute(block, 'region', pairs))]
    pallas_call x1, Pallas kernels: 24.5 us -> 27.1 us  [on_device(): pl.pallas_call(functools.partial(main_kernel, dims, stages, len(weights),...]
    all_to_all x1, blocking collectives: 14.4 us -> 12 us  [on_device(): lax.all_to_all(head_grad, 'region', split_axis=0, concat_axis=0, tiled=True)]
    concatenate x1, other arithmetic: 0.95 us -> 0.04 us  [on_device(): jnp.concatenate([sample_points.transpose(1, 0, 2), sample_spacing[None]],...]
    ppermute x10 -> x14, waiting for transfers between devices: 11.6 us -> 11.1 us  [share(): held.append(lax.ppermute(block, 'region', pairs))]
  transfers between devices with their start and end apart: 11 -> 15, of which waited for: 4 -> 4; matrix products, arithmetic and copies ran while one was open for 2% -> 2% of each run, Pallas kernels for 3% -> 3%
where the time goes in v3:
time: 76.2 us; the launch traced here: 76 us
  Pallas kernels  29.2 us (38%)
  starting transfers between devices  19.7 us (26%)
  blocking collectives  12 us (16%)
  waiting for transfers between devices  11.1 us (15%)
  local copies, waits for them, and re-layouts  1.72 us (2%)
  other arithmetic  1.45 us (2%)
  between operations  0.8 us (1%)
    pallas_call x1, Pallas kernels, on_device(): pl.pallas_call(functools.partial(main_kernel, dims, stages, len(weights),...  27.1 us
    ppermute x14, starting transfers between devices, share(): held.append(lax.ppermute(block, 'region', pairs))  14.8 us
    all_to_all x1, blocking collectives, on_device(): lax.all_to_all(head_grad, 'region', split_axis=0, concat_axis=0, tiled=True)  12 us
    ppermute x14, waiting for transfers between devices, share(): held.append(lax.ppermute(block, 'region', pairs))  11.1 us
    all_to_all x1, starting transfers between devices, on_device(): lax.all_to_all(small, 'region', split_axis=0, concat_axis=0, tiled=True)  4.97 us
    pallas_call x1, Pallas kernels, on_device(): pl.pallas_call(functools.partial(order_kernel, dims), out_shape=(jax.Shap...  2.09 us
  transfers between devices with their start and end apart: 15, of which 4 were waited for; matrix products, arithmetic and copies ran while one was open for 2% of the time, Pallas kernels for 3%

profile of v3, /device:TPU:0, one launch (start us, length us, event | category | flops | bytes accessed | tf_op | source)
XLA Modules:
  0.0 76.0 jit_solution(5930839758432660107)
XLA Ops:
  0.6 0.0 copy-start.3
  0.6 0.0 copy-start.2
  0.6 1.0 %copy.9 = bf16[1,128,256]{1,2,0:T(8,128)(2,1)S(1)} copy(bf16[1,128,256]{2,1,0:T(8,128)(2,1)} %param.12) | data formatting | bytes 131072 | tf_op args[5]
  1.7 0.0 copy-start
  1.7 5.1 %collective-permute-start.2 = (bf16[1,256,128]{2,1,0:T(8,128)(2,1)S(1)}, bf16[1,256,128]{2,1,0:T(8,128)(2,1)S(1)}, u32[]{:S(2)}, u32[]{:S(2)}) collective-permute-start(bf16[1,256,128]{2,1,0:T(8,128)(2,1)S(1)} %bitcast.12), channel_id=1, source_target_pairs={{0,24},{1,25},{2,26},{3,27},{4,28},{5,29},{6,30},{7,31},{8,16},{9,... | collective-permute-start | bytes 196616 | tf_op jit(solution)/shard_map/ppermute | solution.py:332
  6.8 0.0 collective-permute-start.1
  6.8 0.6 collective-permute-start
  7.4 1.6 %collective-permute-start.7 = (bf16[1,256,128]{2,1,0:T(8,128)(2,1)S(1)}, bf16[1,256,128]{2,1,0:T(8,128)(2,1)S(1)}, u32[]{:S(2)}, u32[]{:S(2)}) collective-permute-start(bf16[1,256,128]{2,1,0:T(8,128)(2,1)S(1)} %bitcast.15), channel_id=1, source_target_pairs={{0,2},{1,3},{2,0},{3,1},{4,6},{5,7},{6,4},{7,5},{8,10},{9,11},{10,... | collective-permute-start | bytes 196616 | tf_op jit(solution)/shard_map/ppermute | solution.py:332
  9.1 1.5 %collective-permute-start.8 = (bf16[1,256,128]{2,1,0:T(8,128)(2,1)S(1)}, bf16[1,256,128]{2,1,0:T(8,128)(2,1)S(1)}, u32[]{:S(2)}, u32[]{:S(2)}) collective-permute-start(bf16[1,256,128]{2,1,0:T(8,128)(2,1)S(1)} %bitcast.16), channel_id=1, source_target_pairs={{0,4},{1,5},{2,6},{3,7},{4,0},{5,1},{6,2},{7,3},{8,12},{9,13},{10,... | collective-permute-start | bytes 196616 | tf_op jit(solution)/shard_map/ppermute | solution.py:332
  10.6 0.0 collective-permute-done.2
  10.6 1.6 %collective-permute-start.9 = (bf16[1,256,128]{2,1,0:T(8,128)(2,1)S(1)}, bf16[1,256,128]{2,1,0:T(8,128)(2,1)S(1)}, u32[]{:S(2)}, u32[]{:S(2)}) collective-permute-start(bf16[1,256,128]{2,1,0:T(8,128)(2,1)S(1)} %bitcast.17), channel_id=1, source_target_pairs={{0,6},{1,7},{2,4},{3,5},{4,2},{5,3},{6,0},{7,1},{8,14},{9,15},{10,... | collective-permute-start | bytes 196616 | tf_op jit(solution)/shard_map/ppermute | solution.py:332
  12.2 0.2 collective-permute-done.1
  12.4 0.0 collective-permute-done
  12.4 0.1 collective-permute-start.3
  12.5 0.7 fusion.1
  13.3 0.8 %collective-permute-done.3.refs_8_ = bf16[4,256,128]{2,1,0:T(8,128)(2,1)S(1)} collective-permute-done((bf16[4,256,128]{2,1,0:T(8,128)(2,1)S(1)}, bf16[4,256,128]{2,1,0:T(8,128)(2,1)S(1)}, u32[]{:S(2)}, u32[]{:S(2)}) %collective-permute-start.3) | collective-permute-done | bytes 262176 | tf_op jit(solution)/shard_map/ppermute | solution.py:332
  14.0 0.7 broadcast_in_dim.17
  14.7 5.0 %all-to-all-start = ((bf16[32,8,256]{2,1,0:T(8,128)(2,1)}), bf16[32,8,256]{2,1,0:T(8,128)(2,1)S(1)}, u32[]{:S(2)}, u32[]{:S(2)}) async-start(bf16[32,8,256]{2,1,0:T(8,128)(2,1)} %broadcast_in_dim.17), calls=%async_computation | async-start | bytes 262144 | tf_op jit(solution)/shard_map/all_to_all | solution.py:399
  19.7 1.8 %collective-permute-start.4 = (bf16[3,256,128]{2,1,0:T(8,128)(2,1)S(1)}, bf16[3,256,128]{2,1,0:T(8,128)(2,1)S(1)}, u32[]{:S(2)}, u32[]{:S(2)}) collective-permute-start(bf16[3,256,128]{2,1,0:T(8,128)(2,1)S(1)} %constant_dynamic-update-slice_fusion.refs_1_), channel_id=1, source_target_pairs={{0,2},{1,3},{2,0},{3,1},{4,6},{5,7},{6,4},{7,5},{8,10},{9,11},{10,... | collective-permute-start | bytes 589832 | tf_op jit(solution)/shard_map/ppermute | solution.py:332
  21.5 1.5 %collective-permute-start.5 = (bf16[3,256,128]{2,1,0:T(8,128)(2,1)S(1)}, bf16[3,256,128]{2,1,0:T(8,128)(2,1)S(1)}, u32[]{:S(2)}, u32[]{:S(2)}) collective-permute-start(bf16[3,256,128]{2,1,0:T(8,128)(2,1)S(1)} %constant_dynamic-update-slice_fusion.refs_1_), channel_id=1, source_target_pairs={{0,4},{1,5},{2,6},{3,7},{4,0},{5,1},{6,2},{7,3},{8,12},{9,13},{10,... | collective-permute-start | bytes 589832 | tf_op jit(solution)/shard_map/ppermute | solution.py:332
  23.0 0.0 collective-permute-done.7.refs_2_
  23.0 0.3 collective-permute-start.6
  23.3 0.0 copy-done.3
  23.3 0.0 copy-done.2
  23.3 0.0 collective-permute-done.8.refs_4_
  23.3 0.0 collective-permute-done.9.refs_6_
  23.4 0.1 collective-permute-start.10
  23.4 5.2 %collective-permute-done.4.refs_3_ = bf16[3,256,128]{2,1,0:T(8,128)(2,1)S(1)} collective-permute-done((bf16[3,256,128]{2,1,0:T(8,128)(2,1)S(1)}, bf16[3,256,128]{2,1,0:T(8,128)(2,1)S(1)}, u32[]{:S(2)}, u32[]{:S(2)}) %collective-permute-start.4) | collective-permute-done | bytes 196640 | tf_op jit(solution)/shard_map/ppermute | solution.py:332
  28.6 4.8 %collective-permute-done.5.refs_5_ = bf16[3,256,128]{2,1,0:T(8,128)(2,1)S(1)} collective-permute-done((bf16[3,256,128]{2,1,0:T(8,128)(2,1)S(1)}, bf16[3,256,128]{2,1,0:T(8,128)(2,1)S(1)}, u32[]{:S(2)}, u32[]{:S(2)}) %collective-permute-start.5) | collective-permute-done | bytes 196640 | tf_op jit(solution)/shard_map/ppermute | solution.py:332
  33.5 0.0 collective-permute-done.6.refs_7_
  33.5 0.0 all-to-all-done.small_ref
  33.5 0.0 collective-permute-start.11
  33.5 0.5 collective-permute-start.12
  34.0 0.1 collective-permute-start.13
  34.1 0.0 copy-done
  34.1 0.0 copy-start.1
  34.1 2.1 %order.1 = (f32[4,256]{1,0:T(4,128)S(1)}, s32[2,256]{1,0:T(2,128)S(1)}, f32[2,1280,128]{2,1,0:T(8,128)S(1)}) custom-call(f32[4,256,128]{2,1,0:T(8,128)S(1)} %pad_maximum_fusion.samples_ref, s32[4,256]{1,0:T(4,128)S(1)} %bitcast.20), custom_call_target="tpu_custom_call" | custom-call | flops 4000000000 | bytes 10000000 | tf_op jit(solution)/shard_map/order/pallas_call | solution.py:363
  36.2 0.0 collective-permute-done.10.refs_9_
  36.2 0.0 collective-permute-done.11.refs_10_
  36.2 0.0 collective-permute-done.12.refs_11_
  36.2 0.0 collective-permute-done.13.refs_12_
  36.2 0.0 copy-done.1
  36.2 27.1 %render.1 = (f32[3,256]{1,0:T(4,128)}, f32[32,4,256]{2,1,0:T(4,128)S(1)}) custom-call(s32[2,256]{1,0:T(2,128)S(1)} %get-tuple-element.13.meta_ref, s32[1]{0:T(128)} %bitcast.3.me_ref, f32[4,256]{1,0:T(4,128)S(1)} %get-tuple-element.14.slots_ref, f32[2,1280,128]{2,1,0:T(8,128)S(1)} %get-tuple-element.15.rows_ref, f32[3,256]{1,0:T(4,128)S(1)} %copy-done.1, ...), custom_call_target="tpu_custom_call" | custom-call | flops 20000000000 | bytes 30000000 | tf_op jit(solution)/shard_map/render/pallas_call | solution.py:416
  63.3 12.0 %all_to_all.10 = f32[32,4,256]{2,1,0:T(4,128)S(1)} all-to-all(f32[32,4,256]{2,1,0:T(4,128)S(1)} %get-tuple-element.23), channel_id=1, replica_groups=mesh['region'=32] {'region'}, dimensions={0} | all-to-all | bytes 262144 | tf_op jit(solution)/shard_map/all_to_all | solution.py:438
  75.3 0.6 reduce_sum.9
  (6 shorter events, 0.1 us)
Async XLA Ops:
  0.6 22.6 %copy-start.3 = (f32[256,128]{1,0:T(8,128)S(1)}, f32[256,128]{1,0:T(8,128)}, u32[]{:S(2)}) copy-start(f32[256,128]{1,0:T(8,128)} %param.8) | copy-start | bytes 393220
  0.6 22.6 %copy-start.2 = (f32[256,3,128]{2,0,1:T(8,128)S(1)}, f32[256,3,128]{2,0,1:T(8,128)}, u32[]{:S(2)}) copy-start(f32[256,3,128]{2,0,1:T(8,128)} %param.7) | copy-start | bytes 1179652
  1.7 32.4 %copy-start = (s32[256,4]{0,1:T(4,128)S(1)}, s32[256,4]{0,1:T(4,128)}, u32[]{:S(2)}) copy-start(s32[256,4]{0,1:T(4,128)} %param.9) | copy-start | bytes 12292
  1.7 8.9 %collective-permute-start.2 = (bf16[1,256,128]{2,1,0:T(8,128)(2,1)S(1)}, bf16[1,256,128]{2,1,0:T(8,128)(2,1)S(1)}, u32[]{:S(2)}, u32[]{:S(2)}) collective-permute-start(bf16[1,256,128]{2,1,0:T(8,128)(2,1)S(1)} %bitcast.12), channel_id=1, source_target_pairs={{0,24},{1,25},{2,26},{3,27},{4,28},{5,29},{6,30},{7,31},{8,16},{9,... | collective-permute-start | bytes 196616 | tf_op jit(solution)/shard_map/ppermute | solution.py:332
  6.8 5.6 %collective-permute-start.1 = (bf16[1,256,128]{2,1,0:T(8,128)(2,1)S(1)}, bf16[1,256,128]{2,1,0:T(8,128)(2,1)S(1)}, u32[]{:S(2)}, u32[]{:S(2)}) collective-permute-start(bf16[1,256,128]{2,1,0:T(8,128)(2,1)S(1)} %bitcast.13), channel_id=1, source_target_pairs={{0,16},{1,17},{2,18},{3,19},{4,20},{5,21},{6,22},{7,23},{8,24},{9,... | collective-permute-start | bytes 196616 | tf_op jit(solution)/shard_map/ppermute | solution.py:332
  6.8 5.6 %collective-permute-start = (bf16[1,256,128]{2,1,0:T(8,128)(2,1)S(1)}, bf16[1,256,128]{2,1,0:T(8,128)(2,1)S(1)}, u32[]{:S(2)}, u32[]{:S(2)}) collective-permute-start(bf16[1,256,128]{2,1,0:T(8,128)(2,1)S(1)} %bitcast.14), channel_id=1, source_target_pairs={{0,8},{1,9},{2,10},{3,11},{4,12},{5,13},{6,14},{7,15},{8,0},{9,1},... | collective-permute-start | bytes 196616 | tf_op jit(solution)/shard_map/ppermute | solution.py:332
  7.4 15.6 %collective-permute-start.7 = (bf16[1,256,128]{2,1,0:T(8,128)(2,1)S(1)}, bf16[1,256,128]{2,1,0:T(8,128)(2,1)S(1)}, u32[]{:S(2)}, u32[]{:S(2)}) collective-permute-start(bf16[1,256,128]{2,1,0:T(8,128)(2,1)S(1)} %bitcast.15), channel_id=1, source_target_pairs={{0,2},{1,3},{2,0},{3,1},{4,6},{5,7},{6,4},{7,5},{8,10},{9,11},{10,... | collective-permute-start | bytes 196616 | tf_op jit(solution)/shard_map/ppermute | solution.py:332
  9.1 14.2 %collective-permute-start.8 = (bf16[1,256,128]{2,1,0:T(8,128)(2,1)S(1)}, bf16[1,256,128]{2,1,0:T(8,128)(2,1)S(1)}, u32[]{:S(2)}, u32[]{:S(2)}) collective-permute-start(bf16[1,256,128]{2,1,0:T(8,128)(2,1)S(1)} %bitcast.16), channel_id=1, source_target_pairs={{0,4},{1,5},{2,6},{3,7},{4,0},{5,1},{6,2},{7,3},{8,12},{9,13},{10,... | collective-permute-start | bytes 196616 | tf_op jit(solution)/shard_map/ppermute | solution.py:332
  10.6 12.7 %collective-permute-start.9 = (bf16[1,256,128]{2,1,0:T(8,128)(2,1)S(1)}, bf16[1,256,128]{2,1,0:T(8,128)(2,1)S(1)}, u32[]{:S(2)}, u32[]{:S(2)}) collective-permute-start(bf16[1,256,128]{2,1,0:T(8,128)(2,1)S(1)} %bitcast.17), channel_id=1, source_target_pairs={{0,6},{1,7},{2,4},{3,5},{4,2},{5,3},{6,0},{7,1},{8,14},{9,15},{10,... | collective-permute-start | bytes 196616 | tf_op jit(solution)/shard_map/ppermute | solution.py:332
  12.4 1.6 %collective-permute-start.3 = (bf16[4,256,128]{2,1,0:T(8,128)(2,1)S(1)}, bf16[4,256,128]{2,1,0:T(8,128)(2,1)S(1)}, u32[]{:S(2)}, u32[]{:S(2)}) collective-permute-start(bf16[4,256,128]{2,1,0:T(8,128)(2,1)S(1)} %pad_maximum_fusion.1), channel_id=1, source_target_pairs={{0,1},{1,0},{2,3},{3,2},{4,5},{5,4},{6,7},{7,6},{8,9},{9,8},{10,11... | collective-permute-start | bytes 786440 | tf_op jit(solution)/shard_map/ppermute | solution.py:332
  14.7 18.8 %all-to-all-start = ((bf16[32,8,256]{2,1,0:T(8,128)(2,1)}), bf16[32,8,256]{2,1,0:T(8,128)(2,1)S(1)}, u32[]{:S(2)}, u32[]{:S(2)}) async-start(bf16[32,8,256]{2,1,0:T(8,128)(2,1)} %broadcast_in_dim.17), calls=%async_computation | async-start | bytes 262144 | tf_op jit(solution)/shard_map/all_to_all | solution.py:399
  19.7 8.9 %collective-permute-start.4 = (bf16[3,256,128]{2,1,0:T(8,128)(2,1)S(1)}, bf16[3,256,128]{2,1,0:T(8,128)(2,1)S(1)}, u32[]{:S(2)}, u32[]{:S(2)}) collective-permute-start(bf16[3,256,128]{2,1,0:T(8,128)(2,1)S(1)} %constant_dynamic-update-slice_fusion.refs_1_), channel_id=1, source_target_pairs={{0,2},{1,3},{2,0},{3,1},{4,6},{5,7},{6,4},{7,5},{8,10},{9,11},{10,... | collective-permute-start | bytes 589832 | tf_op jit(solution)/shard_map/ppermute | solution.py:332
  21.5 11.9 %collective-permute-start.5 = (bf16[3,256,128]{2,1,0:T(8,128)(2,1)S(1)}, bf16[3,256,128]{2,1,0:T(8,128)(2,1)S(1)}, u32[]{:S(2)}, u32[]{:S(2)}) collective-permute-start(bf16[3,256,128]{2,1,0:T(8,128)(2,1)S(1)} %constant_dynamic-update-slice_fusion.refs_1_), channel_id=1, source_target_pairs={{0,4},{1,5},{2,6},{3,7},{4,0},{5,1},{6,2},{7,3},{8,12},{9,13},{10,... | collective-permute-start | bytes 589832 | tf_op jit(solution)/shard_map/ppermute | solution.py:332
  23.0 10.5 %collective-permute-start.6 = (bf16[3,256,128]{2,1,0:T(8,128)(2,1)S(1)}, bf16[3,256,128]{2,1,0:T(8,128)(2,1)S(1)}, u32[]{:S(2)}, u32[]{:S(2)}) collective-permute-start(bf16[3,256,128]{2,1,0:T(8,128)(2,1)S(1)} %constant_dynamic-update-slice_fusion.refs_1_), channel_id=1, source_target_pairs={{0,6},{1,7},{2,4},{3,5},{4,2},{5,3},{6,0},{7,1},{8,14},{9,15},{10,... | collective-permute-start | bytes 589832 | tf_op jit(solution)/shard_map/ppermute | solution.py:332
  23.4 12.8 %collective-permute-start.10 = (bf16[3,256,128]{2,1,0:T(8,128)(2,1)S(1)}, bf16[3,256,128]{2,1,0:T(8,128)(2,1)S(1)}, u32[]{:S(2)}, u32[]{:S(2)}) collective-permute-start(bf16[3,256,128]{2,1,0:T(8,128)(2,1)S(1)} %pad_maximum_fusion.2), channel_id=1, source_target_pairs={{0,1},{1,0},{2,3},{3,2},{4,5},{5,4},{6,7},{7,6},{8,9},{9,8},{10,11... | collective-permute-start | bytes 589832 | tf_op jit(solution)/shard_map/ppermute | solution.py:332
  33.5 2.7 %collective-permute-start.11 = (bf16[3,256,128]{2,1,0:T(8,128)(2,1)S(1)}, bf16[3,256,128]{2,1,0:T(8,128)(2,1)S(1)}, u32[]{:S(2)}, u32[]{:S(2)}) collective-permute-start(bf16[3,256,128]{2,1,0:T(8,128)(2,1)S(1)} %collective-permute-done.4.refs_3_), channel_id=1, source_target_pairs={{0,1},{1,0},{2,3},{3,2},{4,5},{5,4},{6,7},{7,6},{8,9},{9,8},{10,11... | collective-permute-start | bytes 589832 | tf_op jit(solution)/shard_map/ppermute | solution.py:332
  33.5 2.7 %collective-permute-start.12 = (bf16[3,256,128]{2,1,0:T(8,128)(2,1)S(1)}, bf16[3,256,128]{2,1,0:T(8,128)(2,1)S(1)}, u32[]{:S(2)}, u32[]{:S(2)}) collective-permute-start(bf16[3,256,128]{2,1,0:T(8,128)(2,1)S(1)} %collective-permute-done.5.refs_5_), channel_id=1, source_target_pairs={{0,1},{1,0},{2,3},{3,2},{4,5},{5,4},{6,7},{7,6},{8,9},{9,8},{10,11... | collective-permute-start | bytes 589832 | tf_op jit(solution)/shard_map/ppermute | solution.py:332
  34.0 2.2 %collective-permute-start.13 = (bf16[3,256,128]{2,1,0:T(8,128)(2,1)S(1)}, bf16[3,256,128]{2,1,0:T(8,128)(2,1)S(1)}, u32[]{:S(2)}, u32[]{:S(2)}) collective-permute-start(bf16[3,256,128]{2,1,0:T(8,128)(2,1)S(1)} %collective-permute-done.6.refs_7_), channel_id=1, source_target_pairs={{0,1},{1,0},{2,3},{3,2},{4,5},{5,4},{6,7},{7,6},{8,9},{9,8},{10,11... | collective-permute-start | bytes 589832 | tf_op jit(solution)/shard_map/ppermute | solution.py:332
  34.1 2.1 %copy-start.1 = (f32[3,256]{1,0:T(4,128)S(1)}, f32[3,256]{1,0:T(4,128)}, u32[]{:S(2)}) copy-start(f32[3,256]{1,0:T(4,128)} %colour_grad_ref.1) | copy-start | bytes 9220

commit v4 on v2

--- a/solution.py
+++ b/solution.py
@@ -137,10 +137,22 @@
 
 
 def main_kernel(
-    dims, stages, parts, meta_ref, me_ref, slots_ref, rows_ref, colour_grad_ref, small_ref, *refs
+    dims,
+    stages,
+    meta_ref,
+    me_ref,
+    slots_ref,
+    rows_ref,
+    colour_grad_ref,
+    small_ref,
+    near_ref,
+    far_ref,
+    rendered_ref,
+    head_grad_ref,
+    hidden_ref,
+    raw_ref,
+    slab_ref,
 ):
-    part_refs = refs[:parts]
-    rendered_ref, head_grad_ref, hidden_ref, raw_ref, weight_ref, slab_ref, sems = refs[parts:]
     regions, rays, crossings, samples, tiles = dims
     width = GROUP * samples
     halves, lanes = raw_ref.shape[0], raw_ref.shape[2]
@@ -149,14 +161,6 @@
     rounds = (used + (UNROLL - 1)) // UNROLL
     units = hidden_ref.shape[0] // tiles
     depth = slab_ref.shape[1] // UNROLL
-    held = regions // parts
-
-    copies = [
-        pltpu.make_async_copy(part_refs[p], weight_ref.at[p * held : (p + 1) * held], sems.at[p])
-        for p in range(parts)
-    ]
-    for copy in copies:
-        copy.start()
 
     def phases(tile):
         return phases_of(tile, depth // 2, meta_ref, rows_ref, small_ref)
@@ -167,16 +171,20 @@
         if index + 1 < UNROLL:
             ahead = phases(index + 1)
         store_features(turns, slab_ref.at[0], index * depth)
-    for copy in copies:
-        copy.wait()
+
+    def weights_of(region):
+        at = place(region ^ me, stages)
+        held = near_ref.shape[0]
+        is_near = at < held
+        at = jnp.where(is_near, at, at - held)
+        return jnp.where(is_near, near_ref[at], far_ref[at])
 
     def work(step, more):
         first = step * UNROLL
         slot = lax.rem(step, 2)
 
         def layer(index):
-            weights = weight_ref[place(meta_ref[0, first + index] ^ me, stages)]
-            return dot(weights, slab_ref[slot, index * depth : (index + 1) * depth, :])
+            return dot(weights_of(meta_ref[0, first + index]), slab_ref[slot, index * depth : (index + 1) * depth, :])
 
         ahead = layer(0)
         turns_ahead = phases(first + UNROLL) if more else None
@@ -308,8 +316,10 @@
 
 
 def place(offset, stages):
-    at, scale = 0, 1
-    for unit, size in stages:
+    a, b = [(offset // unit) % size for unit, size in stages[:2]]
+    at = jnp.where(b == 0, a, jnp.where(a == 0, 3 + b, 3 + 3 * b + a))
+    scale = 16
+    for unit, size in stages[2:]:
         at = at + ((offset // unit) % size) * scale
         scale = scale * size
     return at
@@ -348,7 +358,24 @@
     meta_width = -(-tiles // 128) * 128
     stages = exchange_stages(regions)
     all_samples = jnp.concatenate([sample_points.transpose(1, 0, 2), sample_spacing[None]], axis=0)
-    weights = share(w_hidden[0].T[None], stages[0], regions)
+    own = w_hidden[0].T[None]
+    first = share(own, stages[0], regions)
+    own_second = share(own, stages[1], regions)
+    small = jnp.pad(freq[0], ((0, 1), (0, hidden_units - freq.shape[2])))
+    small = jnp.concatenate([w_head[0], small], axis=0)
+    small = jnp.broadcast_to(small[None], (regions, 8, hidden_units))
+    others, small, listed = lax.optimization_barrier(
+        (jnp.concatenate(first[1:], axis=0), small, crossed.T)
+    )
+    second = share(others, stages[1], regions)
+    second[1], small = lax.optimization_barrier((second[1], small))
+    all_small = lax.all_to_all(small, "region", split_axis=0, concat_axis=0, tiled=True)
+    all_small, *second[2:] = lax.optimization_barrier((all_small, *second[2:]))
+    near = jnp.concatenate([own, others, *own_second[1:], *second[1:]], axis=0)
+    for stage in stages[2:-1]:
+        near = jnp.concatenate(share(near, stage, regions), axis=0)
+    near, far = share(near, stages[-1], regions)
+
     slots, meta, rows = pl.pallas_call(
         functools.partial(order_kernel, dims),
         out_shape=(
@@ -361,45 +388,28 @@
         compiler_params=pltpu.CompilerParams(vmem_limit_bytes=small_limit),
         cost_estimate=pl.CostEstimate(flops=4 * 10**9, bytes_accessed=10**7, transcendentals=0),
         name="order",
-    )(all_samples, crossed.T)
-
-    small = jnp.pad(freq[0], ((0, 1), (0, hidden_units - freq.shape[2])))
-    small = jnp.concatenate([w_head[0], small], axis=0)
-    small = jnp.broadcast_to(small[None], (regions, 8, hidden_units))
-    block, small = lax.optimization_barrier((jnp.concatenate(weights, axis=0), small))
-    weights = share(block, stages[1], regions)
-    for stage in stages[2:-1]:
-        weights = share(jnp.concatenate(weights, axis=0), stage, regions)
-    own = share(weights[0], stages[-1], regions)
-    own[-1], small = lax.optimization_barrier((own[-1], small))
-    all_small = lax.all_to_all(small, "region", split_axis=0, concat_axis=0, tiled=True)
-    all_small, *others = lax.optimization_barrier((all_small, *weights[1:]))
-    swapped = [own] + [share(block, stages[-1], regions) for block in others]
-    weights = [blocks[i] for i in range(stages[-1][1]) for blocks in swapped]
+    )(all_samples, listed)
 
     whole = pl.BlockSpec(memory_space=vmem)
 
     rendered, head_grad = pl.pallas_call(
-        functools.partial(main_kernel, dims, stages, len(weights)),
+        functools.partial(main_kernel, dims, stages),
         out_shape=(
             jax.ShapeDtypeStruct((3, rays), F32),
             jax.ShapeDtypeStruct((regions, 4, hidden_units), F32),
         ),
         in_specs=[pl.BlockSpec(memory_space=smem)] * 2
-        + [whole] * 4
-        + [pl.BlockSpec(memory_space=pl.ANY)] * len(weights),
+        + [whole] * 6,
         out_specs=[whole] * 2,
         scratch_shapes=[
             pltpu.VMEM((tiles * hidden_units, width), BF16),
             pltpu.VMEM((halves, tiles * 8, lanes), F32),
-            pltpu.VMEM((regions, hidden_units, features), BF16),
             pltpu.VMEM((2, UNROLL * features, width), BF16),
-            pltpu.SemaphoreType.DMA((len(weights),)),
         ],
         compiler_params=params,
         cost_estimate=pl.CostEstimate(flops=2 * 10**10, bytes_accessed=3 * 10**7, transcendentals=0),
         name="render",
-    )(meta, me, slots, rows, colour_grad, all_small, *weights)
+    )(meta, me, slots, rows, colour_grad, all_small, near, far)
 
     partial_sums = lax.all_to_all(head_grad, "region", split_axis=0, concat_axis=0, tiled=True)
     head_grad = jnp.sum(partial_sums, axis=0, keepdims=True)

time: 71.3 us -> 73.7 us (1.034); the launches traced: 72.2 us -> 72.8 us
  blocking collectives: 14.4 us -> 9.99 us
  waiting for transfers between devices: 11.7 us -> 14.4 us
  starting transfers between devices: 14.8 us -> 17.3 us
  other arithmetic: 2.33 us -> 1.4 us
    all_to_all x1, waiting for transfers between devices: 0.08 us -> 8.1 us  [on_device(): lax.all_to_all(small, 'region', split_axis=0, concat_axis=0, tiled=True)]
    ppermute x10, waiting for transfers between devices: 11.6 us -> 6.25 us  [share(): held.append(lax.ppermute(block, 'region', pairs))]
    all_to_all x1, blocking collectives: 14.4 us -> 9.99 us  [on_device(): lax.all_to_all(head_grad, 'region', split_axis=0, concat_axis=0, tiled=True)]
    ppermute x10, starting transfers between devices: 9.78 us -> 13.1 us  [share(): held.append(lax.ppermute(block, 'region', pairs))]
    concatenate x1, other arithmetic: 0.95 us -> 0.03 us  [on_device(): jnp.concatenate([sample_points.transpose(1, 0, 2), sample_spacing[None]],...]
  transfers between devices with their start and end apart: 11 -> 11, of which waited for: 4 -> 5; matrix products, arithmetic and copies ran while one was open for 2% -> 2% of each run, Pallas kernels for 3% -> 3%
where the time goes in v4:
time: 73.7 us; the launch traced here: 72.8 us
  Pallas kernels  27.2 us (37%)
  starting transfers between devices  17.3 us (23%)
  waiting for transfers between devices  14.4 us (20%)
  blocking collectives  9.99 us (14%)
  local copies, waits for them, and re-layouts  1.8 us (2%)
  other arithmetic  1.4 us (2%)
  between operations  0.79 us (1%)
    pallas_call x1, Pallas kernels, on_device(): pl.pallas_call(functools.partial(main_kernel, dims, stages), out_shape=(j...  25.1 us
    ppermute x10, starting transfers between devices, share(): held.append(lax.ppermute(block, 'region', pairs))  13.1 us
    all_to_all x1, blocking collectives, on_device(): lax.all_to_all(head_grad, 'region', split_axis=0, concat_axis=0, tiled=True)  9.99 us
    all_to_all x1, waiting for transfers between devices, on_device(): lax.all_to_all(small, 'region', split_axis=0, concat_axis=0, tiled=True)  8.1 us
    ppermute x10, waiting for transfers between devices, share(): held.append(lax.ppermute(block, 'region', pairs))  6.25 us
    all_to_all x1, starting transfers between devices, on_device(): lax.all_to_all(small, 'region', split_axis=0, concat_axis=0, tiled=True)  4.27 us
    pallas_call x1, Pallas kernels, on_device(): pl.pallas_call(functools.partial(order_kernel, dims), out_shape=(jax.Shap...  2.1 us
  transfers between devices with their start and end apart: 11, of which 5 were waited for; matrix products, arithmetic and copies ran while one was open for 2% of the time, Pallas kernels for 3%

profile of v4, /device:TPU:0, one launch (start us, length us, event | category | flops | bytes accessed | tf_op | source)
XLA Modules:
  0.0 72.8 jit_solution(13257590853490987436)
XLA Ops:
  0.6 0.9 %copy.9 = bf16[1,128,256]{1,2,0:T(8,128)(2,1)S(1)} copy(bf16[1,128,256]{2,1,0:T(8,128)(2,1)} %param.12) | data formatting | bytes 131072 | tf_op args[5]
  1.6 3.1 %collective-permute-start = (bf16[1,256,128]{2,1,0:T(8,128)(2,1)S(1)}, bf16[1,256,128]{2,1,0:T(8,128)(2,1)S(1)}, u32[]{:S(2)}, u32[]{:S(2)}) collective-permute-start(bf16[1,256,128]{2,1,0:T(8,128)(2,1)S(1)} %bitcast.15), channel_id=1, source_target_pairs={{0,8},{1,9},{2,10},{3,11},{4,12},{5,13},{6,14},{7,15},{8,0},{9,1},... | collective-permute-start | bytes 196616 | tf_op jit(solution)/shard_map/ppermute | solution.py:333
  4.7 2.6 %collective-permute-start.1 = (bf16[1,256,128]{2,1,0:T(8,128)(2,1)S(1)}, bf16[1,256,128]{2,1,0:T(8,128)(2,1)S(1)}, u32[]{:S(2)}, u32[]{:S(2)}) collective-permute-start(bf16[1,256,128]{2,1,0:T(8,128)(2,1)S(1)} %bitcast.16), channel_id=1, source_target_pairs={{0,16},{1,17},{2,18},{3,19},{4,20},{5,21},{6,22},{7,23},{8,24},{9,... | collective-permute-start | bytes 196616 | tf_op jit(solution)/shard_map/ppermute | solution.py:333
  7.3 0.0 collective-permute-start.2
  7.3 1.7 %collective-permute-start.6 = (bf16[1,256,128]{2,1,0:T(8,128)(2,1)S(1)}, bf16[1,256,128]{2,1,0:T(8,128)(2,1)S(1)}, u32[]{:S(2)}, u32[]{:S(2)}) collective-permute-start(bf16[1,256,128]{2,1,0:T(8,128)(2,1)S(1)} %bitcast.18), channel_id=1, source_target_pairs={{0,2},{1,3},{2,0},{3,1},{4,6},{5,7},{6,4},{7,5},{8,10},{9,11},{10,... | collective-permute-start | bytes 196616 | tf_op jit(solution)/shard_map/ppermute | solution.py:333
  9.0 1.5 %collective-permute-start.7 = (bf16[1,256,128]{2,1,0:T(8,128)(2,1)S(1)}, bf16[1,256,128]{2,1,0:T(8,128)(2,1)S(1)}, u32[]{:S(2)}, u32[]{:S(2)}) collective-permute-start(bf16[1,256,128]{2,1,0:T(8,128)(2,1)S(1)} %bitcast.19), channel_id=1, source_target_pairs={{0,4},{1,5},{2,6},{3,7},{4,0},{5,1},{6,2},{7,3},{8,12},{9,13},{10,... | collective-permute-start | bytes 196616 | tf_op jit(solution)/shard_map/ppermute | solution.py:333
  10.5 0.7 fusion.1
  11.2 0.0 copy-start.2
  11.2 0.0 copy-start.3
  11.2 0.0 collective-permute-done
  11.2 0.3 collective-permute-start.8
  11.6 0.4 collective-permute-done.1
  11.9 1.4 %collective-permute-done.2 = bf16[1,256,128]{2,1,0:T(8,128)(2,1)S(1)} collective-permute-done((bf16[1,256,128]{2,1,0:T(8,128)(2,1)S(1)}, bf16[1,256,128]{2,1,0:T(8,128)(2,1)S(1)}, u32[]{:S(2)}, u32[]{:S(2)}) %collective-permute-start.2) | collective-permute-done | bytes 65568 | tf_op jit(solution)/shard_map/ppermute | solution.py:333
  13.4 0.7 broadcast_in_dim.17
  14.0 1.5 %collective-permute-start.3 = (bf16[3,256,128]{2,1,0:T(8,128)(2,1)S(1)}, bf16[3,256,128]{2,1,0:T(8,128)(2,1)S(1)}, u32[]{:S(2)}, u32[]{:S(2)}) collective-permute-start(bf16[3,256,128]{2,1,0:T(8,128)(2,1)S(1)} %pad_maximum_fusion.1), channel_id=1, source_target_pairs={{0,2},{1,3},{2,0},{3,1},{4,6},{5,7},{6,4},{7,5},{8,10},{9,11},{10,... | collective-permute-start | bytes 589832 | tf_op jit(solution)/shard_map/ppermute | solution.py:333
  15.5 1.5 %collective-permute-start.4 = (bf16[3,256,128]{2,1,0:T(8,128)(2,1)S(1)}, bf16[3,256,128]{2,1,0:T(8,128)(2,1)S(1)}, u32[]{:S(2)}, u32[]{:S(2)}) collective-permute-start(bf16[3,256,128]{2,1,0:T(8,128)(2,1)S(1)} %pad_maximum_fusion.1), channel_id=1, source_target_pairs={{0,4},{1,5},{2,6},{3,7},{4,0},{5,1},{6,2},{7,3},{8,12},{9,13},{10,... | collective-permute-start | bytes 589832 | tf_op jit(solution)/shard_map/ppermute | solution.py:333
  17.1 0.0 collective-permute-done.6
  17.1 0.5 collective-permute-start.5
  17.6 4.2 %collective-permute-done.3 = bf16[3,256,128]{2,1,0:T(8,128)(2,1)S(1)} collective-permute-done((bf16[3,256,128]{2,1,0:T(8,128)(2,1)S(1)}, bf16[3,256,128]{2,1,0:T(8,128)(2,1)S(1)}, u32[]{:S(2)}, u32[]{:S(2)}) %collective-permute-start.3) | collective-permute-done | bytes 196640 | tf_op jit(solution)/shard_map/ppermute | solution.py:333
  21.8 4.3 %all-to-all-start = ((bf16[32,8,256]{2,1,0:T(8,128)(2,1)}), bf16[32,8,256]{2,1,0:T(8,128)(2,1)S(1)}, u32[]{:S(2)}, u32[]{:S(2)}) async-start(bf16[32,8,256]{2,1,0:T(8,128)(2,1)} %broadcast_in_dim.17), calls=%async_computation | async-start | bytes 262144 | tf_op jit(solution)/shard_map/all_to_all | solution.py:372
  26.1 0.0 copy-start
  26.1 0.0 collective-permute-done.7
  26.2 0.0 collective-permute-done.8
  26.2 0.0 collective-permute-done.4
  26.2 0.0 collective-permute-done.5
  26.2 8.1 %all-to-all-done.small_ref = bf16[32,8,256]{2,1,0:T(8,128)(2,1)S(1)} async-done(((bf16[32,8,256]{2,1,0:T(8,128)(2,1)}), bf16[32,8,256]{2,1,0:T(8,128)(2,1)S(1)}, u32[]{:S(2)}, u32[]{:S(2)}) %all-to-all-start) | async-done | bytes 131104 | tf_op jit(solution)/shard_map/all_to_all | solution.py:372
  34.4 0.3 collective-permute-start.9
  34.7 0.0 copy-done.2
  34.7 0.0 copy-done.3
  34.7 0.0 copy-done
  34.7 0.0 copy-start.1
  34.8 2.1 %order.1 = (f32[4,256]{1,0:T(4,128)S(1)}, s32[2,256]{1,0:T(2,128)S(1)}, f32[2,1280,128]{2,1,0:T(8,128)S(1)}) custom-call(f32[4,256,128]{2,1,0:T(8,128)S(1)} %pad_maximum_fusion.samples_ref, s32[4,256]{1,0:T(4,128)S(1)} %bitcast.13), custom_call_target="tpu_custom_call" | custom-call | flops 4000000000 | bytes 10000000 | tf_op jit(solution)/shard_map/order/pallas_call | solution.py:379
  36.9 0.3 collective-permute-done.9.far_ref
  37.1 0.0 copy-done.1
  37.1 25.1 %render.1 = (f32[3,256]{1,0:T(4,128)}, f32[32,4,256]{2,1,0:T(4,128)S(1)}) custom-call(s32[2,256]{1,0:T(2,128)S(1)} %get-tuple-element.16.meta_ref, s32[1]{0:T(128)} %bitcast.10.me_ref, f32[4,256]{1,0:T(4,128)S(1)} %get-tuple-element.17.slots_ref, f32[2,1280,128]{2,1,0:T(8,128)S(1)} %get-tuple-element.18.rows_ref, f32[3,256]{1,0:T(4,128)S(1)} %copy-done.1, ...), custom_call_target="tpu_custom_call" | custom-call | flops 20000000000 | bytes 30000000 | tf_op jit(solution)/shard_map/render/pallas_call | solution.py:395
  62.2 10.0 %all_to_all.10 = f32[32,4,256]{2,1,0:T(4,128)S(1)} all-to-all(f32[32,4,256]{2,1,0:T(4,128)S(1)} %get-tuple-element.27), channel_id=1, replica_groups=mesh['region'=32] {'region'}, dimensions={0} | all-to-all | bytes 262144 | tf_op jit(solution)/shard_map/all_to_all | solution.py:414
  72.2 0.6 reduce_sum.9
  (10 shorter events, 0.2 us)
Async XLA Ops:
  1.6 9.6 %collective-permute-start = (bf16[1,256,128]{2,1,0:T(8,128)(2,1)S(1)}, bf16[1,256,128]{2,1,0:T(8,128)(2,1)S(1)}, u32[]{:S(2)}, u32[]{:S(2)}) collective-permute-start(bf16[1,256,128]{2,1,0:T(8,128)(2,1)S(1)} %bitcast.15), channel_id=1, source_target_pairs={{0,8},{1,9},{2,10},{3,11},{4,12},{5,13},{6,14},{7,15},{8,0},{9,1},... | collective-permute-start | bytes 196616 | tf_op jit(solution)/shard_map/ppermute | solution.py:333
  4.7 7.3 %collective-permute-start.1 = (bf16[1,256,128]{2,1,0:T(8,128)(2,1)S(1)}, bf16[1,256,128]{2,1,0:T(8,128)(2,1)S(1)}, u32[]{:S(2)}, u32[]{:S(2)}) collective-permute-start(bf16[1,256,128]{2,1,0:T(8,128)(2,1)S(1)} %bitcast.16), channel_id=1, source_target_pairs={{0,16},{1,17},{2,18},{3,19},{4,20},{5,21},{6,22},{7,23},{8,24},{9,... | collective-permute-start | bytes 196616 | tf_op jit(solution)/shard_map/ppermute | solution.py:333
  7.3 6.1 %collective-permute-start.2 = (bf16[1,256,128]{2,1,0:T(8,128)(2,1)S(1)}, bf16[1,256,128]{2,1,0:T(8,128)(2,1)S(1)}, u32[]{:S(2)}, u32[]{:S(2)}) collective-permute-start(bf16[1,256,128]{2,1,0:T(8,128)(2,1)S(1)} %bitcast.17), channel_id=1, source_target_pairs={{0,24},{1,25},{2,26},{3,27},{4,28},{5,29},{6,30},{7,31},{8,16},{9,... | collective-permute-start | bytes 196616 | tf_op jit(solution)/shard_map/ppermute | solution.py:333
  7.3 9.8 %collective-permute-start.6 = (bf16[1,256,128]{2,1,0:T(8,128)(2,1)S(1)}, bf16[1,256,128]{2,1,0:T(8,128)(2,1)S(1)}, u32[]{:S(2)}, u32[]{:S(2)}) collective-permute-start(bf16[1,256,128]{2,1,0:T(8,128)(2,1)S(1)} %bitcast.18), channel_id=1, source_target_pairs={{0,2},{1,3},{2,0},{3,1},{4,6},{5,7},{6,4},{7,5},{8,10},{9,11},{10,... | collective-permute-start | bytes 196616 | tf_op jit(solution)/shard_map/ppermute | solution.py:333
  9.0 17.2 %collective-permute-start.7 = (bf16[1,256,128]{2,1,0:T(8,128)(2,1)S(1)}, bf16[1,256,128]{2,1,0:T(8,128)(2,1)S(1)}, u32[]{:S(2)}, u32[]{:S(2)}) collective-permute-start(bf16[1,256,128]{2,1,0:T(8,128)(2,1)S(1)} %bitcast.19), channel_id=1, source_target_pairs={{0,4},{1,5},{2,6},{3,7},{4,0},{5,1},{6,2},{7,3},{8,12},{9,13},{10,... | collective-permute-start | bytes 196616 | tf_op jit(solution)/shard_map/ppermute | solution.py:333
  11.2 23.5 %copy-start.2 = (f32[256,3,128]{2,0,1:T(8,128)S(1)}, f32[256,3,128]{2,0,1:T(8,128)}, u32[]{:S(2)}) copy-start(f32[256,3,128]{2,0,1:T(8,128)} %param.7) | copy-start | bytes 1179652
  11.2 23.5 %copy-start.3 = (f32[256,128]{1,0:T(8,128)S(1)}, f32[256,128]{1,0:T(8,128)}, u32[]{:S(2)}) copy-start(f32[256,128]{1,0:T(8,128)} %param.8) | copy-start | bytes 393220
  11.2 14.9 %collective-permute-start.8 = (bf16[1,256,128]{2,1,0:T(8,128)(2,1)S(1)}, bf16[1,256,128]{2,1,0:T(8,128)(2,1)S(1)}, u32[]{:S(2)}, u32[]{:S(2)}) collective-permute-start(bf16[1,256,128]{2,1,0:T(8,128)(2,1)S(1)} %bitcast.20), channel_id=1, source_target_pairs={{0,6},{1,7},{2,4},{3,5},{4,2},{5,3},{6,0},{7,1},{8,14},{9,15},{10,... | collective-permute-start | bytes 196616 | tf_op jit(solution)/shard_map/ppermute | solution.py:333
  14.0 7.8 %collective-permute-start.3 = (bf16[3,256,128]{2,1,0:T(8,128)(2,1)S(1)}, bf16[3,256,128]{2,1,0:T(8,128)(2,1)S(1)}, u32[]{:S(2)}, u32[]{:S(2)}) collective-permute-start(bf16[3,256,128]{2,1,0:T(8,128)(2,1)S(1)} %pad_maximum_fusion.1), channel_id=1, source_target_pairs={{0,2},{1,3},{2,0},{3,1},{4,6},{5,7},{6,4},{7,5},{8,10},{9,11},{10,... | collective-permute-start | bytes 589832 | tf_op jit(solution)/shard_map/ppermute | solution.py:333
  15.5 10.7 %collective-permute-start.4 = (bf16[3,256,128]{2,1,0:T(8,128)(2,1)S(1)}, bf16[3,256,128]{2,1,0:T(8,128)(2,1)S(1)}, u32[]{:S(2)}, u32[]{:S(2)}) collective-permute-start(bf16[3,256,128]{2,1,0:T(8,128)(2,1)S(1)} %pad_maximum_fusion.1), channel_id=1, source_target_pairs={{0,4},{1,5},{2,6},{3,7},{4,0},{5,1},{6,2},{7,3},{8,12},{9,13},{10,... | collective-permute-start | bytes 589832 | tf_op jit(solution)/shard_map/ppermute | solution.py:333
  17.1 9.1 %collective-permute-start.5 = (bf16[3,256,128]{2,1,0:T(8,128)(2,1)S(1)}, bf16[3,256,128]{2,1,0:T(8,128)(2,1)S(1)}, u32[]{:S(2)}, u32[]{:S(2)}) collective-permute-start(bf16[3,256,128]{2,1,0:T(8,128)(2,1)S(1)} %pad_maximum_fusion.1), channel_id=1, source_target_pairs={{0,6},{1,7},{2,4},{3,5},{4,2},{5,3},{6,0},{7,1},{8,14},{9,15},{10,... | collective-permute-start | bytes 589832 | tf_op jit(solution)/shard_map/ppermute | solution.py:333
  21.8 12.5 %all-to-all-start = ((bf16[32,8,256]{2,1,0:T(8,128)(2,1)}), bf16[32,8,256]{2,1,0:T(8,128)(2,1)S(1)}, u32[]{:S(2)}, u32[]{:S(2)}) async-start(bf16[32,8,256]{2,1,0:T(8,128)(2,1)} %broadcast_in_dim.17), calls=%async_computation | async-start | bytes 262144 | tf_op jit(solution)/shard_map/all_to_all | solution.py:372
  26.1 8.6 %copy-start = (s32[256,4]{0,1:T(4,128)S(1)}, s32[256,4]{0,1:T(4,128)}, u32[]{:S(2)}) copy-start(s32[256,4]{0,1:T(4,128)} %param.9) | copy-start | bytes 12292
  34.4 2.7 %collective-permute-start.9 = (bf16[16,256,128]{2,1,0:T(8,128)(2,1)S(1)}, bf16[16,256,128]{2,1,0:T(8,128)(2,1)S(1)}, u32[]{:S(2)}, u32[]{:S(2)}) collective-permute-start(bf16[16,256,128]{2,1,0:T(8,128)(2,1)S(1)} %constant_dynamic-update-slice_fusion.near_ref), channel_id=1, source_target_pairs={{0,1},{1,0},{2,3},{3,2},{4,5},{5,4},{6,7},{7,6},{8,9},{9,8},{10,11... | collective-permute-start | bytes 3145736 | tf_op jit(solution)/shard_map/ppermute | solution.py:333
  34.7 2.4 %copy-start.1 = (f32[3,256]{1,0:T(4,128)S(1)}, f32[3,256]{1,0:T(4,128)}, u32[]{:S(2)}) copy-start(f32[3,256]{1,0:T(4,128)} %colour_grad_ref.1) | copy-start | bytes 9220

commit v5 on v4

--- a/solution.py
+++ b/solution.py
@@ -112,8 +112,7 @@
     return pl.ds(pl.multiple_of(tile * height, height), height)
 
 
-def phases_of(tile, half, meta_ref, rows_ref, small_ref):
-    small = small_ref[meta_ref[0, tile]][:, :128].astype(F32)
+def phases_of(tile, half, small, rows_ref):
     freq = jnp.concatenate([small] * 3, axis=0).T[:half].astype(BF16)
     return dot(freq, stacked(joined(rows_ref, tile_rows(tile, 8)), 0, 3))
 
@@ -139,20 +138,16 @@
 def main_kernel(
     dims,
     stages,
+    parts,
     meta_ref,
     me_ref,
     slots_ref,
     rows_ref,
     colour_grad_ref,
-    small_ref,
-    near_ref,
-    far_ref,
-    rendered_ref,
-    head_grad_ref,
-    hidden_ref,
-    raw_ref,
-    slab_ref,
+    *refs,
 ):
+    part_refs = refs[:parts]
+    rendered_ref, head_grad_ref, hidden_ref, raw_ref, weight_ref, slab_ref, sems = refs[parts:]
     regions, rays, crossings, samples, tiles = dims
     width = GROUP * samples
     halves, lanes = raw_ref.shape[0], raw_ref.shape[2]
@@ -162,8 +157,27 @@
     units = hidden_ref.shape[0] // tiles
     depth = slab_ref.shape[1] // UNROLL
 
+    copies, at = [], 0
+    for p in range(parts):
+        count = part_refs[p].shape[0]
+        copies.append(
+            pltpu.make_async_copy(part_refs[p], weight_ref.at[at : at + count], sems.at[p])
+        )
+        at += count
+    for copy in copies:
+        copy.start()
+    for copy in copies:
+        copy.wait()
+
+    def at_of(tile):
+        return place(meta_ref[0, tile] ^ me, stages)
+
+    def small_of(tile):
+        both = weight_ref[at_of(tile), units:, :].astype(F32)
+        return both[:8], both[8:]
+
     def phases(tile):
-        return phases_of(tile, depth // 2, meta_ref, rows_ref, small_ref)
+        return phases_of(tile, depth // 2, small_of(tile)[0], rows_ref)
 
     ahead = phases(0)
     for index in range(UNROLL):
@@ -172,19 +186,13 @@
             ahead = phases(index + 1)
         store_features(turns, slab_ref.at[0], index * depth)
 
-    def weights_of(region):
-        at = place(region ^ me, stages)
-        held = near_ref.shape[0]
-        is_near = at < held
-        at = jnp.where(is_near, at, at - held)
-        return jnp.where(is_near, near_ref[at], far_ref[at])
-
     def work(step, more):
         first = step * UNROLL
         slot = lax.rem(step, 2)
 
         def layer(index):
-            return dot(weights_of(meta_ref[0, first + index]), slab_ref[slot, index * depth : (index + 1) * depth, :])
+            weights = weight_ref[at_of(first + index), :units, :]
+            return dot(weights, slab_ref[slot, index * depth : (index + 1) * depth, :])
 
         ahead = layer(0)
         turns_ahead = phases(first + UNROLL) if more else None
@@ -203,7 +211,8 @@
         return 0
 
     def head(tile):
-        raw = dot(small_ref[meta_ref[0, tile]], hidden_ref[tile_rows(tile, units), :])
+        head_w = jnp.concatenate(small_of(tile), axis=1).astype(BF16)
+        raw = dot(head_w, hidden_ref[tile_rows(tile, units), :])
         for half in range(halves):
             raw_ref[half, tile_rows(tile, 8), :] = raw[:, half * lanes : (half + 1) * lanes]
 
@@ -358,24 +367,14 @@
     meta_width = -(-tiles // 128) * 128
     stages = exchange_stages(regions)
     all_samples = jnp.concatenate([sample_points.transpose(1, 0, 2), sample_spacing[None]], axis=0)
-    own = w_hidden[0].T[None]
+    small = jnp.pad(freq[0], ((0, 1), (0, hidden_units - freq.shape[2])))
+    small = jnp.concatenate([w_head[0], small], axis=0)
+    halves_of_small = [small[:, i : i + features] for i in range(0, hidden_units, features)]
+    own = jnp.concatenate([w_hidden[0].T, *halves_of_small], axis=0)[None]
     first = share(own, stages[0], regions)
     own_second = share(own, stages[1], regions)
-    small = jnp.pad(freq[0], ((0, 1), (0, hidden_units - freq.shape[2])))
-    small = jnp.concatenate([w_head[0], small], axis=0)
-    small = jnp.broadcast_to(small[None], (regions, 8, hidden_units))
-    others, small, listed = lax.optimization_barrier(
-        (jnp.concatenate(first[1:], axis=0), small, crossed.T)
-    )
+    others, listed = lax.optimization_barrier((jnp.concatenate(first[1:], axis=0), crossed.T))
     second = share(others, stages[1], regions)
-    second[1], small = lax.optimization_barrier((second[1], small))
-    all_small = lax.all_to_all(small, "region", split_axis=0, concat_axis=0, tiled=True)
-    all_small, *second[2:] = lax.optimization_barrier((all_small, *second[2:]))
-    near = jnp.concatenate([own, others, *own_second[1:], *second[1:]], axis=0)
-    for stage in stages[2:-1]:
-        near = jnp.concatenate(share(near, stage, regions), axis=0)
-    near, far = share(near, stages[-1], regions)
-
     slots, meta, rows = pl.pallas_call(
         functools.partial(order_kernel, dims),
         out_shape=(
@@ -390,26 +389,41 @@
         name="order",
     )(all_samples, listed)
 
+    early = jnp.concatenate([own, others, *own_second[1:]], axis=0)
+    if len(stages) > 3:
+        near = jnp.concatenate([early, *second[1:]], axis=0)
+        for stage in stages[2:-1]:
+            near = jnp.concatenate(share(near, stage, regions), axis=0)
+        weights = share(near, stages[-1], regions)
+    else:
+        early, far = share(early, stages[-1], regions)
+        far, slots, *second = lax.optimization_barrier((far, slots, *second[1:]))
+        late, far_late = share(jnp.concatenate(second, axis=0), stages[-1], regions)
+        weights = [early, late, far, far_late]
+
     whole = pl.BlockSpec(memory_space=vmem)
 
     rendered, head_grad = pl.pallas_call(
-        functools.partial(main_kernel, dims, stages),
+        functools.partial(main_kernel, dims, stages, len(weights)),
         out_shape=(
             jax.ShapeDtypeStruct((3, rays), F32),
             jax.ShapeDtypeStruct((regions, 4, hidden_units), F32),
         ),
         in_specs=[pl.BlockSpec(memory_space=smem)] * 2
-        + [whole] * 6,
+        + [whole] * 3
+        + [pl.BlockSpec(memory_space=pl.ANY)] * len(weights),
         out_specs=[whole] * 2,
         scratch_shapes=[
             pltpu.VMEM((tiles * hidden_units, width), BF16),
             pltpu.VMEM((halves, tiles * 8, lanes), F32),
+            pltpu.VMEM((regions,) + own.shape[1:], BF16),
             pltpu.VMEM((2, UNROLL * features, width), BF16),
+            pltpu.SemaphoreType.DMA((len(weights),)),
         ],
         compiler_params=params,
         cost_estimate=pl.CostEstimate(flops=2 * 10**10, bytes_accessed=3 * 10**7, transcendentals=0),
         name="render",
-    )(meta, me, slots, rows, colour_grad, all_small, near, far)
+    )(meta, me, slots, rows, colour_grad, *weights)
 
     partial_sums = lax.all_to_all(head_grad, "region", split_axis=0, concat_axis=0, tiled=True)
     head_grad = jnp.sum(partial_sums, axis=0, keepdims=True)

time: 73.7 us -> 70.6 us (0.958)
  starting transfers between devices: 17.3 us -> 12.9 us
  blocking collectives: 9.99 us -> 12.9 us
  waiting for transfers between devices: 14.4 us -> 13.6 us
    all_to_all x1 -> x0, waiting for transfers between devices: 8.1 us -> none  [on_device(): lax.all_to_all(small, 'region', split_axis=0, concat_axis=0, tiled=True)]
    ppermute x10 -> x11, waiting for transfers between devices: 6.25 us -> 13.6 us  [share(): held.append(lax.ppermute(block, 'region', pairs))]
    all_to_all x1 -> x0, starting transfers between devices: 4.27 us -> none  [on_device(): lax.all_to_all(small, 'region', split_axis=0, concat_axis=0, tiled=True)]
    all_to_all x1, blocking collectives: 9.99 us -> 12.9 us  [on_device(): lax.all_to_all(head_grad, 'region', split_axis=0, concat_axis=0, tiled=True)]
    ppermute x10 -> x11, starting transfers between devices: 13.1 us -> 12.9 us  [share(): held.append(lax.ppermute(block, 'region', pairs))]
  transfers between devices with their start and end apart: 11 -> 11, of which waited for: 5 -> 7; matrix products, arithmetic and copies ran while one was open for 2% -> 0% of each run, Pallas kernels for 3% -> 3%
where the time goes in v5:
time: 70.6 us; the launch traced here: 70.4 us
  Pallas kernels  27.6 us (39%)
  waiting for transfers between devices  13.6 us (19%)
  starting transfers between devices  12.9 us (18%)
  blocking collectives  12.9 us (18%)
  other arithmetic  1.48 us (2%)
  local copies, waits for them, and re-layouts  1.12 us (2%)
  between operations  0.79 us (1%)
    pallas_call x1, Pallas kernels, on_device(): pl.pallas_call(functools.partial(main_kernel, dims, stages, len(weights))...  25.5 us
    ppermute x11, waiting for transfers between devices, share(): held.append(lax.ppermute(block, 'region', pairs))  13.6 us
    all_to_all x1, blocking collectives, on_device(): lax.all_to_all(head_grad, 'region', split_axis=0, concat_axis=0, tiled=True)  12.9 us
    ppermute x11, starting transfers between devices, share(): held.append(lax.ppermute(block, 'region', pairs))  12.9 us
    pallas_call x1, Pallas kernels, on_device(): pl.pallas_call(functools.partial(order_kernel, dims), out_shape=(jax.Shap...  2.09 us
  transfers between devices with their start and end apart: 11, of which 7 were waited for; matrix products, arithmetic and copies ran while one was open for 0% of the time, Pallas kernels for 3%

profile of v5, /device:TPU:0, one launch (start us, length us, event | category | flops | bytes accessed | tf_op | source)
XLA Modules:
  0.0 70.4 jit_solution(8773584421630867255)
XLA Ops:
  0.6 0.0 copy-start.2
  0.6 0.0 copy-start.3
  0.7 0.8 %fusion.1 = bf16[8,256]{1,0:T(8,128)(2,1)S(1)} fusion(bf16[3,64]{1,0:T(4,128)(2,1)} %bitcast.21, bf16[4,256]{1,0:T(4,128)(2,1)} %bitcast.20), kind=kLoop, calls=%fused_computation.13 | loop fusion | flops 12288 | bytes 6528 | tf_op jit(solution)/shard_map/concatenate | solution.py:371
  1.4 0.9 %copy.9 = bf16[1,128,256]{1,2,0:T(8,128)(2,1)S(1)} copy(bf16[1,128,256]{2,1,0:T(8,128)(2,1)} %param.12) | data formatting | bytes 131072 | tf_op args[5]
  2.4 0.0 copy-start
  2.4 3.1 %collective-permute-start = (bf16[1,272,128]{2,1,0:T(8,128)(2,1)S(1)}, bf16[1,272,128]{2,1,0:T(8,128)(2,1)S(1)}, u32[]{:S(2)}, u32[]{:S(2)}) collective-permute-start(bf16[1,272,128]{2,1,0:T(8,128)(2,1)S(1)} %maximum_bitcast_fusion), channel_id=1, source_target_pairs={{0,8},{1,9},{2,10},{3,11},{4,12},{5,13},{6,14},{7,15},{8,0},{9,1},... | collective-permute-start | bytes 208904 | tf_op jit(solution)/shard_map/ppermute | solution.py:342
  5.5 2.6 %collective-permute-start.1 = (bf16[1,272,128]{2,1,0:T(8,128)(2,1)S(1)}, bf16[1,272,128]{2,1,0:T(8,128)(2,1)S(1)}, u32[]{:S(2)}, u32[]{:S(2)}) collective-permute-start(bf16[1,272,128]{2,1,0:T(8,128)(2,1)S(1)} %maximum_bitcast_fusion), channel_id=1, source_target_pairs={{0,16},{1,17},{2,18},{3,19},{4,20},{5,21},{6,22},{7,23},{8,24},{9,... | collective-permute-start | bytes 208904 | tf_op jit(solution)/shard_map/ppermute | solution.py:342
  8.1 0.0 collective-permute-start.2
  8.1 1.7 %collective-permute-start.3 = (bf16[1,272,128]{2,1,0:T(8,128)(2,1)S(1)}, bf16[1,272,128]{2,1,0:T(8,128)(2,1)S(1)}, u32[]{:S(2)}, u32[]{:S(2)}) collective-permute-start(bf16[1,272,128]{2,1,0:T(8,128)(2,1)S(1)} %maximum_bitcast_fusion), channel_id=1, source_target_pairs={{0,2},{1,3},{2,0},{3,1},{4,6},{5,7},{6,4},{7,5},{8,10},{9,11},{10,... | collective-permute-start | bytes 208904 | tf_op jit(solution)/shard_map/ppermute | solution.py:342
  9.8 1.5 %collective-permute-start.4 = (bf16[1,272,128]{2,1,0:T(8,128)(2,1)S(1)}, bf16[1,272,128]{2,1,0:T(8,128)(2,1)S(1)}, u32[]{:S(2)}, u32[]{:S(2)}) collective-permute-start(bf16[1,272,128]{2,1,0:T(8,128)(2,1)S(1)} %maximum_bitcast_fusion), channel_id=1, source_target_pairs={{0,4},{1,5},{2,6},{3,7},{4,0},{5,1},{6,2},{7,3},{8,12},{9,13},{10,... | collective-permute-start | bytes 208904 | tf_op jit(solution)/shard_map/ppermute | solution.py:342
  11.3 0.0 collective-permute-done
  11.3 0.3 collective-permute-start.5
  11.7 1.4 %collective-permute-done.1 = bf16[1,272,128]{2,1,0:T(8,128)(2,1)S(1)} collective-permute-done((bf16[1,272,128]{2,1,0:T(8,128)(2,1)S(1)}, bf16[1,272,128]{2,1,0:T(8,128)(2,1)S(1)}, u32[]{:S(2)}, u32[]{:S(2)}) %collective-permute-start.1) | collective-permute-done | bytes 69664 | tf_op jit(solution)/shard_map/ppermute | solution.py:342
  13.0 1.3 %collective-permute-done.2 = bf16[1,272,128]{2,1,0:T(8,128)(2,1)S(1)} collective-permute-done((bf16[1,272,128]{2,1,0:T(8,128)(2,1)S(1)}, bf16[1,272,128]{2,1,0:T(8,128)(2,1)S(1)}, u32[]{:S(2)}, u32[]{:S(2)}) %collective-permute-start.2) | collective-permute-done | bytes 69664 | tf_op jit(solution)/shard_map/ppermute | solution.py:342
  14.4 0.0 collective-permute-done.3
  14.4 0.5 collective-permute-done.4
  14.9 1.7 %collective-permute-done.5 = bf16[1,272,128]{2,1,0:T(8,128)(2,1)S(1)} collective-permute-done((bf16[1,272,128]{2,1,0:T(8,128)(2,1)S(1)}, bf16[1,272,128]{2,1,0:T(8,128)(2,1)S(1)}, u32[]{:S(2)}, u32[]{:S(2)}) %collective-permute-start.5) | collective-permute-done | bytes 69664 | tf_op jit(solution)/shard_map/ppermute | solution.py:342
  16.6 0.1 collective-permute-start.6
  16.7 0.0 copy-done.2
  16.7 0.0 copy-done.3
  16.8 0.0 copy-start.1
  16.8 0.6 collective-permute-start.7
  17.4 0.3 collective-permute-start.8
  17.7 2.6 %collective-permute-start.9 = (bf16[3,272,128]{2,1,0:T(8,128)(2,1)S(1)}, bf16[3,272,128]{2,1,0:T(8,128)(2,1)S(1)}, u32[]{:S(2)}, u32[]{:S(2)}) collective-permute-start(bf16[3,272,128]{2,1,0:T(8,128)(2,1)S(1)} %pad_maximum_fusion.1), channel_id=1, source_target_pairs={{0,6},{1,7},{2,4},{3,5},{4,2},{5,3},{6,0},{7,1},{8,14},{9,15},{10,... | collective-permute-start | bytes 626696 | tf_op jit(solution)/shard_map/ppermute | solution.py:342
  20.3 0.0 copy-done
  20.3 2.1 %order.1 = (f32[4,256]{1,0:T(4,128)S(1)}, s32[2,256]{1,0:T(2,128)S(1)}, f32[2,1280,128]{2,1,0:T(8,128)S(1)}) custom-call(f32[4,256,128]{2,1,0:T(8,128)S(1)} %pad_maximum_fusion.samples_ref, s32[4,256]{1,0:T(4,128)S(1)} %bitcast.14), custom_call_target="tpu_custom_call" | custom-call | flops 4000000000 | bytes 10000000 | tf_op jit(solution)/shard_map/order/pallas_call | solution.py:378
  22.4 2.4 %collective-permute-done.7 = bf16[3,272,128]{2,1,0:T(8,128)(2,1)S(1)} collective-permute-done((bf16[3,272,128]{2,1,0:T(8,128)(2,1)S(1)}, bf16[3,272,128]{2,1,0:T(8,128)(2,1)S(1)}, u32[]{:S(2)}, u32[]{:S(2)}) %collective-permute-start.7) | collective-permute-done | bytes 208928 | tf_op jit(solution)/shard_map/ppermute | solution.py:342
  24.8 4.3 %collective-permute-done.8 = bf16[3,272,128]{2,1,0:T(8,128)(2,1)S(1)} collective-permute-done((bf16[3,272,128]{2,1,0:T(8,128)(2,1)S(1)}, bf16[3,272,128]{2,1,0:T(8,128)(2,1)S(1)}, u32[]{:S(2)}, u32[]{:S(2)}) %collective-permute-start.8) | collective-permute-done | bytes 208928 | tf_op jit(solution)/shard_map/ppermute | solution.py:342
  29.1 0.0 collective-permute-done.9
  29.1 0.0 collective-permute-done.6.refs_2_
  29.2 0.1 collective-permute-start.10
  29.3 2.0 %collective-permute-done.10.refs_3_ = bf16[9,272,128]{2,1,0:T(8,128)(2,1)S(1)} collective-permute-done((bf16[9,272,128]{2,1,0:T(8,128)(2,1)S(1)}, bf16[9,272,128]{2,1,0:T(8,128)(2,1)S(1)}, u32[]{:S(2)}, u32[]{:S(2)}) %collective-permute-start.10) | collective-permute-done | bytes 626720 | tf_op jit(solution)/shard_map/ppermute | solution.py:342
  31.3 0.0 copy-done.1
  31.3 25.5 %render.1 = (f32[3,256]{1,0:T(4,128)}, f32[32,4,256]{2,1,0:T(4,128)S(1)}) custom-call(s32[2,256]{1,0:T(2,128)S(1)} %get-tuple-element.15.meta_ref, s32[1]{0:T(128)} %bitcast.8.me_ref, f32[4,256]{1,0:T(4,128)S(1)} %get-tuple-element.18.slots_ref, f32[2,1280,128]{2,1,0:T(8,128)S(1)} %get-tuple-element.19.rows_ref, f32[3,256]{1,0:T(4,128)S(1)} %copy-done.1, ...), custom_call_target="tpu_custom_call" | custom-call | flops 20000000000 | bytes 30000000 | tf_op jit(solution)/shard_map/render/pallas_call | solution.py:406
  56.9 12.9 %all_to_all.5 = f32[32,4,256]{2,1,0:T(4,128)S(1)} all-to-all(f32[32,4,256]{2,1,0:T(4,128)S(1)} %get-tuple-element.25), channel_id=1, replica_groups=mesh['region'=32] {'region'}, dimensions={0} | all-to-all | bytes 262144 | tf_op jit(solution)/shard_map/all_to_all | solution.py:428
  69.8 0.6 reduce_sum.9
  (12 shorter events, 0.2 us)
Async XLA Ops:
  0.6 16.1 %copy-start.2 = (f32[256,3,128]{2,0,1:T(8,128)S(1)}, f32[256,3,128]{2,0,1:T(8,128)}, u32[]{:S(2)}) copy-start(f32[256,3,128]{2,0,1:T(8,128)} %param.7) | copy-start | bytes 1179652
  0.6 16.1 %copy-start.3 = (f32[256,128]{1,0:T(8,128)S(1)}, f32[256,128]{1,0:T(8,128)}, u32[]{:S(2)}) copy-start(f32[256,128]{1,0:T(8,128)} %param.8) | copy-start | bytes 393220
  2.4 18.0 %copy-start = (s32[256,4]{0,1:T(4,128)S(1)}, s32[256,4]{0,1:T(4,128)}, u32[]{:S(2)}) copy-start(s32[256,4]{0,1:T(4,128)} %param.9) | copy-start | bytes 12292
  2.4 8.9 %collective-permute-start = (bf16[1,272,128]{2,1,0:T(8,128)(2,1)S(1)}, bf16[1,272,128]{2,1,0:T(8,128)(2,1)S(1)}, u32[]{:S(2)}, u32[]{:S(2)}) collective-permute-start(bf16[1,272,128]{2,1,0:T(8,128)(2,1)S(1)} %maximum_bitcast_fusion), channel_id=1, source_target_pairs={{0,8},{1,9},{2,10},{3,11},{4,12},{5,13},{6,14},{7,15},{8,0},{9,1},... | collective-permute-start | bytes 208904 | tf_op jit(solution)/shard_map/ppermute | solution.py:342
  5.5 7.5 %collective-permute-start.1 = (bf16[1,272,128]{2,1,0:T(8,128)(2,1)S(1)}, bf16[1,272,128]{2,1,0:T(8,128)(2,1)S(1)}, u32[]{:S(2)}, u32[]{:S(2)}) collective-permute-start(bf16[1,272,128]{2,1,0:T(8,128)(2,1)S(1)} %maximum_bitcast_fusion), channel_id=1, source_target_pairs={{0,16},{1,17},{2,18},{3,19},{4,20},{5,21},{6,22},{7,23},{8,24},{9,... | collective-permute-start | bytes 208904 | tf_op jit(solution)/shard_map/ppermute | solution.py:342
  8.1 6.2 %collective-permute-start.2 = (bf16[1,272,128]{2,1,0:T(8,128)(2,1)S(1)}, bf16[1,272,128]{2,1,0:T(8,128)(2,1)S(1)}, u32[]{:S(2)}, u32[]{:S(2)}) collective-permute-start(bf16[1,272,128]{2,1,0:T(8,128)(2,1)S(1)} %maximum_bitcast_fusion), channel_id=1, source_target_pairs={{0,24},{1,25},{2,26},{3,27},{4,28},{5,29},{6,30},{7,31},{8,16},{9,... | collective-permute-start | bytes 208904 | tf_op jit(solution)/shard_map/ppermute | solution.py:342
  8.1 6.3 %collective-permute-start.3 = (bf16[1,272,128]{2,1,0:T(8,128)(2,1)S(1)}, bf16[1,272,128]{2,1,0:T(8,128)(2,1)S(1)}, u32[]{:S(2)}, u32[]{:S(2)}) collective-permute-start(bf16[1,272,128]{2,1,0:T(8,128)(2,1)S(1)} %maximum_bitcast_fusion), channel_id=1, source_target_pairs={{0,2},{1,3},{2,0},{3,1},{4,6},{5,7},{6,4},{7,5},{8,10},{9,11},{10,... | collective-permute-start | bytes 208904 | tf_op jit(solution)/shard_map/ppermute | solution.py:342
  9.8 5.1 %collective-permute-start.4 = (bf16[1,272,128]{2,1,0:T(8,128)(2,1)S(1)}, bf16[1,272,128]{2,1,0:T(8,128)(2,1)S(1)}, u32[]{:S(2)}, u32[]{:S(2)}) collective-permute-start(bf16[1,272,128]{2,1,0:T(8,128)(2,1)S(1)} %maximum_bitcast_fusion), channel_id=1, source_target_pairs={{0,4},{1,5},{2,6},{3,7},{4,0},{5,1},{6,2},{7,3},{8,12},{9,13},{10,... | collective-permute-start | bytes 208904 | tf_op jit(solution)/shard_map/ppermute | solution.py:342
  11.3 5.3 %collective-permute-start.5 = (bf16[1,272,128]{2,1,0:T(8,128)(2,1)S(1)}, bf16[1,272,128]{2,1,0:T(8,128)(2,1)S(1)}, u32[]{:S(2)}, u32[]{:S(2)}) collective-permute-start(bf16[1,272,128]{2,1,0:T(8,128)(2,1)S(1)} %maximum_bitcast_fusion), channel_id=1, source_target_pairs={{0,6},{1,7},{2,4},{3,5},{4,2},{5,3},{6,0},{7,1},{8,14},{9,15},{10,... | collective-permute-start | bytes 208904 | tf_op jit(solution)/shard_map/ppermute | solution.py:342
  16.6 12.5 %collective-permute-start.6 = (bf16[7,272,128]{2,1,0:T(8,128)(2,1)S(1)}, bf16[7,272,128]{2,1,0:T(8,128)(2,1)S(1)}, u32[]{:S(2)}, u32[]{:S(2)}) collective-permute-start(bf16[7,272,128]{2,1,0:T(8,128)(2,1)S(1)} %constant_dynamic-update-slice_fusion.refs_0_), channel_id=1, source_target_pairs={{0,1},{1,0},{2,3},{3,2},{4,5},{5,4},{6,7},{7,6},{8,9},{9,8},{10,11... | collective-permute-start | bytes 1462280 | tf_op jit(solution)/shard_map/ppermute | solution.py:342
  16.8 14.6 %copy-start.1 = (f32[3,256]{1,0:T(4,128)S(1)}, f32[3,256]{1,0:T(4,128)}, u32[]{:S(2)}) copy-start(f32[3,256]{1,0:T(4,128)} %colour_grad_ref.1) | copy-start | bytes 9220
  16.8 8.0 %collective-permute-start.7 = (bf16[3,272,128]{2,1,0:T(8,128)(2,1)S(1)}, bf16[3,272,128]{2,1,0:T(8,128)(2,1)S(1)}, u32[]{:S(2)}, u32[]{:S(2)}) collective-permute-start(bf16[3,272,128]{2,1,0:T(8,128)(2,1)S(1)} %pad_maximum_fusion.1), channel_id=1, source_target_pairs={{0,2},{1,3},{2,0},{3,1},{4,6},{5,7},{6,4},{7,5},{8,10},{9,11},{10,... | collective-permute-start | bytes 626696 | tf_op jit(solution)/shard_map/ppermute | solution.py:342
  17.4 11.7 %collective-permute-start.8 = (bf16[3,272,128]{2,1,0:T(8,128)(2,1)S(1)}, bf16[3,272,128]{2,1,0:T(8,128)(2,1)S(1)}, u32[]{:S(2)}, u32[]{:S(2)}) collective-permute-start(bf16[3,272,128]{2,1,0:T(8,128)(2,1)S(1)} %pad_maximum_fusion.1), channel_id=1, source_target_pairs={{0,4},{1,5},{2,6},{3,7},{4,0},{5,1},{6,2},{7,3},{8,12},{9,13},{10,... | collective-permute-start | bytes 626696 | tf_op jit(solution)/shard_map/ppermute | solution.py:342
  17.7 11.4 %collective-permute-start.9 = (bf16[3,272,128]{2,1,0:T(8,128)(2,1)S(1)}, bf16[3,272,128]{2,1,0:T(8,128)(2,1)S(1)}, u32[]{:S(2)}, u32[]{:S(2)}) collective-permute-start(bf16[3,272,128]{2,1,0:T(8,128)(2,1)S(1)} %pad_maximum_fusion.1), channel_id=1, source_target_pairs={{0,6},{1,7},{2,4},{3,5},{4,2},{5,3},{6,0},{7,1},{8,14},{9,15},{10,... | collective-permute-start | bytes 626696 | tf_op jit(solution)/shard_map/ppermute | solution.py:342
  29.2 2.1 %collective-permute-start.10 = (bf16[9,272,128]{2,1,0:T(8,128)(2,1)S(1)}, bf16[9,272,128]{2,1,0:T(8,128)(2,1)S(1)}, u32[]{:S(2)}, u32[]{:S(2)}) collective-permute-start(bf16[9,272,128]{2,1,0:T(8,128)(2,1)S(1)} %constant_dynamic-update-slice_fusion.5.refs_1_), channel_id=1, source_target_pairs={{0,1},{1,0},{2,3},{3,2},{4,5},{5,4},{6,7},{7,6},{8,9},{9,8},{10,11... | collective-permute-start | bytes 1880072 | tf_op jit(solution)/shard_map/ppermute | solution.py:342

commit v6 on v5

--- a/solution.py
+++ b/solution.py
@@ -112,11 +112,6 @@
     return pl.ds(pl.multiple_of(tile * height, height), height)
 
 
-def phases_of(tile, half, small, rows_ref):
-    freq = jnp.concatenate([small] * 3, axis=0).T[:half].astype(BF16)
-    return dot(freq, stacked(joined(rows_ref, tile_rows(tile, 8)), 0, 3))
-
-
 def store_features(turns, feature_ref, first):
     half = turns.shape[0]
     for at in range(0, half, 16):
@@ -147,7 +142,8 @@
     *refs,
 ):
     part_refs = refs[:parts]
-    rendered_ref, head_grad_ref, hidden_ref, raw_ref, weight_ref, slab_ref, sems = refs[parts:]
+    rendered_ref, head_grad_ref, hidden_ref, raw_ref, weight_ref = refs[parts : parts + 5]
+    freq_ref, head_ref, slab_ref, sems = refs[parts + 5 :]
     regions, rays, crossings, samples, tiles = dims
     width = GROUP * samples
     halves, lanes = raw_ref.shape[0], raw_ref.shape[2]
@@ -157,27 +153,34 @@
     units = hidden_ref.shape[0] // tiles
     depth = slab_ref.shape[1] // UNROLL
 
-    copies, at = [], 0
-    for p in range(parts):
-        count = part_refs[p].shape[0]
-        copies.append(
-            pltpu.make_async_copy(part_refs[p], weight_ref.at[at : at + count], sems.at[p])
-        )
-        at += count
+    places = [0]
+    for part in part_refs:
+        places.append(places[-1] + part.shape[0])
+    copies = []
+    for p, part in enumerate(part_refs):
+        source, target = part.at[:, :units, :], weight_ref.at[places[p] : places[p + 1]]
+        copies.append(pltpu.make_async_copy(source, target, sems.at[p]))
     for copy in copies:
         copy.start()
-    for copy in copies:
-        copy.wait()
+
+    def table(part, start, index):
+        both = part[index, units:, :].astype(F32)
+        freq_ref[start + index, :, :24] = jnp.concatenate([both[:8]] * 3, axis=0).T[: depth // 2].astype(BF16)
+        head_ref[start + index] = jnp.concatenate([both[:8], both[8:]], axis=1).astype(BF16)
+
+    for start, part in zip(places, part_refs):
+        if part.shape[0] <= 16:
+            for index in range(part.shape[0]):
+                table(part, start, index)
+        else:
+            lax.fori_loop(0, part.shape[0], lambda i, _: (table(part, start, i), 0)[1], 0)
 
     def at_of(tile):
         return place(meta_ref[0, tile] ^ me, stages)
 
-    def small_of(tile):
-        both = weight_ref[at_of(tile), units:, :].astype(F32)
-        return both[:8], both[8:]
-
     def phases(tile):
-        return phases_of(tile, depth // 2, small_of(tile)[0], rows_ref)
+        points = stacked(joined(rows_ref, tile_rows(tile, 8)), 0, 3)
+        return dot(freq_ref[at_of(tile), :, :24], points)
 
     ahead = phases(0)
     for index in range(UNROLL):
@@ -185,13 +188,15 @@
         if index + 1 < UNROLL:
             ahead = phases(index + 1)
         store_features(turns, slab_ref.at[0], index * depth)
+    for copy in copies:
+        copy.wait()
 
     def work(step, more):
         first = step * UNROLL
         slot = lax.rem(step, 2)
 
         def layer(index):
-            weights = weight_ref[at_of(first + index), :units, :]
+            weights = weight_ref[at_of(first + index)]
             return dot(weights, slab_ref[slot, index * depth : (index + 1) * depth, :])
 
         ahead = layer(0)
@@ -211,8 +216,7 @@
         return 0
 
     def head(tile):
-        head_w = jnp.concatenate(small_of(tile), axis=1).astype(BF16)
-        raw = dot(head_w, hidden_ref[tile_rows(tile, units), :])
+        raw = dot(head_ref[at_of(tile)], hidden_ref[tile_rows(tile, units), :])
         for half in range(halves):
             raw_ref[half, tile_rows(tile, 8), :] = raw[:, half * lanes : (half + 1) * lanes]
 
@@ -358,7 +362,7 @@
     vmem, smem = pltpu.VMEM, pltpu.SMEM
     mib = 1024 * 1024
     limit = 2 * tiles * width * hidden_units + 8 * halves * tiles * 8 * lanes
-    limit += 2 * regions * hidden_units * features + 4 * mib
+    limit += 2 * regions * (2 * hidden_units + 16) * features + 4 * mib
     limit += 2 * 2 * UNROLL * features * width + 4 * mib
     small_limit = 24 * mib
     params = pltpu.CompilerParams(vmem_limit_bytes=limit)
@@ -410,13 +414,14 @@
             jax.ShapeDtypeStruct((regions, 4, hidden_units), F32),
         ),
         in_specs=[pl.BlockSpec(memory_space=smem)] * 2
-        + [whole] * 3
-        + [pl.BlockSpec(memory_space=pl.ANY)] * len(weights),
+        + [whole] * (3 + len(weights)),
         out_specs=[whole] * 2,
         scratch_shapes=[
             pltpu.VMEM((tiles * hidden_units, width), BF16),
             pltpu.VMEM((halves, tiles * 8, lanes), F32),
-            pltpu.VMEM((regions,) + own.shape[1:], BF16),
+            pltpu.VMEM((regions, hidden_units, features), BF16),
+            pltpu.VMEM((regions, features // 2, 128), BF16),
+            pltpu.VMEM((regions, 8, hidden_units), BF16),
             pltpu.VMEM((2, UNROLL * features, width), BF16),
             pltpu.SemaphoreType.DMA((len(weights),)),
         ],

time: 70.6 us -> 69.5 us (0.984)
  Pallas kernels: 27.6 us -> 26.4 us
    pallas_call x1, Pallas kernels: 25.5 us -> 24.3 us  [on_device(): pl.pallas_call(functools.partial(main_kernel, dims, stages, len(weights))...]
where the time goes in v6:
time: 69.5 us; the launch traced here: 69.3 us
  Pallas kernels  26.4 us (38%)
  waiting for transfers between devices  13.6 us (20%)
  starting transfers between devices  12.9 us (19%)
  blocking collectives  12.9 us (19%)
  other arithmetic  1.48 us (2%)
  local copies, waits for them, and re-layouts  1.12 us (2%)
  between operations  0.79 us (1%)
    pallas_call x1, Pallas kernels, on_device(): pl.pallas_call(functools.partial(main_kernel, dims, stages, len(weights))...  24.3 us
    ppermute x11, waiting for transfers between devices, share(): held.append(lax.ppermute(block, 'region', pairs))  13.6 us
    all_to_all x1, blocking collectives, on_device(): lax.all_to_all(head_grad, 'region', split_axis=0, concat_axis=0, tiled=True)  12.9 us
    ppermute x11, starting transfers between devices, share(): held.append(lax.ppermute(block, 'region', pairs))  12.9 us
    pallas_call x1, Pallas kernels, on_device(): pl.pallas_call(functools.partial(order_kernel, dims), out_shape=(jax.Shap...  2.09 us
  transfers between devices with their start and end apart: 11, of which 7 were waited for; matrix products, arithmetic and copies ran while one was open for 0% of the time, Pallas kernels for 3%

profile of v6, /device:TPU:0, one launch (start us, length us, event | category | flops | bytes accessed | tf_op | source)
XLA Modules:
  0.0 69.3 jit_solution(17190618301700914921)
XLA Ops:
  0.6 0.0 copy-start.2
  0.6 0.0 copy-start.3
  0.7 0.8 %fusion.1 = bf16[8,256]{1,0:T(8,128)(2,1)S(1)} fusion(bf16[3,64]{1,0:T(4,128)(2,1)} %bitcast.21, bf16[4,256]{1,0:T(4,128)(2,1)} %bitcast.20), kind=kLoop, calls=%fused_computation.13 | loop fusion | flops 12288 | bytes 6528 | tf_op jit(solution)/shard_map/concatenate | solution.py:375
  1.4 0.9 %copy.9 = bf16[1,128,256]{1,2,0:T(8,128)(2,1)S(1)} copy(bf16[1,128,256]{2,1,0:T(8,128)(2,1)} %param.12) | data formatting | bytes 131072 | tf_op args[5]
  2.4 0.0 copy-start
  2.4 3.1 %collective-permute-start = (bf16[1,272,128]{2,1,0:T(8,128)(2,1)S(1)}, bf16[1,272,128]{2,1,0:T(8,128)(2,1)S(1)}, u32[]{:S(2)}, u32[]{:S(2)}) collective-permute-start(bf16[1,272,128]{2,1,0:T(8,128)(2,1)S(1)} %maximum_bitcast_fusion), channel_id=1, source_target_pairs={{0,8},{1,9},{2,10},{3,11},{4,12},{5,13},{6,14},{7,15},{8,0},{9,1},... | collective-permute-start | bytes 208904 | tf_op jit(solution)/shard_map/ppermute | solution.py:346
  5.5 2.6 %collective-permute-start.1 = (bf16[1,272,128]{2,1,0:T(8,128)(2,1)S(1)}, bf16[1,272,128]{2,1,0:T(8,128)(2,1)S(1)}, u32[]{:S(2)}, u32[]{:S(2)}) collective-permute-start(bf16[1,272,128]{2,1,0:T(8,128)(2,1)S(1)} %maximum_bitcast_fusion), channel_id=1, source_target_pairs={{0,16},{1,17},{2,18},{3,19},{4,20},{5,21},{6,22},{7,23},{8,24},{9,... | collective-permute-start | bytes 208904 | tf_op jit(solution)/shard_map/ppermute | solution.py:346
  8.1 0.0 collective-permute-start.2
  8.1 1.7 %collective-permute-start.3 = (bf16[1,272,128]{2,1,0:T(8,128)(2,1)S(1)}, bf16[1,272,128]{2,1,0:T(8,128)(2,1)S(1)}, u32[]{:S(2)}, u32[]{:S(2)}) collective-permute-start(bf16[1,272,128]{2,1,0:T(8,128)(2,1)S(1)} %maximum_bitcast_fusion), channel_id=1, source_target_pairs={{0,2},{1,3},{2,0},{3,1},{4,6},{5,7},{6,4},{7,5},{8,10},{9,11},{10,... | collective-permute-start | bytes 208904 | tf_op jit(solution)/shard_map/ppermute | solution.py:346
  9.8 1.5 %collective-permute-start.4 = (bf16[1,272,128]{2,1,0:T(8,128)(2,1)S(1)}, bf16[1,272,128]{2,1,0:T(8,128)(2,1)S(1)}, u32[]{:S(2)}, u32[]{:S(2)}) collective-permute-start(bf16[1,272,128]{2,1,0:T(8,128)(2,1)S(1)} %maximum_bitcast_fusion), channel_id=1, source_target_pairs={{0,4},{1,5},{2,6},{3,7},{4,0},{5,1},{6,2},{7,3},{8,12},{9,13},{10,... | collective-permute-start | bytes 208904 | tf_op jit(solution)/shard_map/ppermute | solution.py:346
  11.3 0.0 collective-permute-done
  11.3 0.3 collective-permute-start.5
  11.7 1.4 %collective-permute-done.1 = bf16[1,272,128]{2,1,0:T(8,128)(2,1)S(1)} collective-permute-done((bf16[1,272,128]{2,1,0:T(8,128)(2,1)S(1)}, bf16[1,272,128]{2,1,0:T(8,128)(2,1)S(1)}, u32[]{:S(2)}, u32[]{:S(2)}) %collective-permute-start.1) | collective-permute-done | bytes 69664 | tf_op jit(solution)/shard_map/ppermute | solution.py:346
  13.0 1.3 %collective-permute-done.2 = bf16[1,272,128]{2,1,0:T(8,128)(2,1)S(1)} collective-permute-done((bf16[1,272,128]{2,1,0:T(8,128)(2,1)S(1)}, bf16[1,272,128]{2,1,0:T(8,128)(2,1)S(1)}, u32[]{:S(2)}, u32[]{:S(2)}) %collective-permute-start.2) | collective-permute-done | bytes 69664 | tf_op jit(solution)/shard_map/ppermute | solution.py:346
  14.4 0.0 collective-permute-done.3
  14.4 0.5 collective-permute-done.4
  14.9 1.7 %collective-permute-done.5 = bf16[1,272,128]{2,1,0:T(8,128)(2,1)S(1)} collective-permute-done((bf16[1,272,128]{2,1,0:T(8,128)(2,1)S(1)}, bf16[1,272,128]{2,1,0:T(8,128)(2,1)S(1)}, u32[]{:S(2)}, u32[]{:S(2)}) %collective-permute-start.5) | collective-permute-done | bytes 69664 | tf_op jit(solution)/shard_map/ppermute | solution.py:346
  16.6 0.1 collective-permute-start.6
  16.7 0.0 copy-done.2
  16.7 0.0 copy-done.3
  16.8 0.0 copy-start.1
  16.8 0.6 collective-permute-start.7
  17.4 0.3 collective-permute-start.8
  17.7 2.6 %collective-permute-start.9 = (bf16[3,272,128]{2,1,0:T(8,128)(2,1)S(1)}, bf16[3,272,128]{2,1,0:T(8,128)(2,1)S(1)}, u32[]{:S(2)}, u32[]{:S(2)}) collective-permute-start(bf16[3,272,128]{2,1,0:T(8,128)(2,1)S(1)} %pad_maximum_fusion.1), channel_id=1, source_target_pairs={{0,6},{1,7},{2,4},{3,5},{4,2},{5,3},{6,0},{7,1},{8,14},{9,15},{10,... | collective-permute-start | bytes 626696 | tf_op jit(solution)/shard_map/ppermute | solution.py:346
  20.3 0.0 copy-done
  20.3 2.1 %order.1 = (f32[4,256]{1,0:T(4,128)S(1)}, s32[2,256]{1,0:T(2,128)S(1)}, f32[2,1280,128]{2,1,0:T(8,128)S(1)}) custom-call(f32[4,256,128]{2,1,0:T(8,128)S(1)} %pad_maximum_fusion.samples_ref, s32[4,256]{1,0:T(4,128)S(1)} %bitcast.14), custom_call_target="tpu_custom_call" | custom-call | flops 4000000000 | bytes 10000000 | tf_op jit(solution)/shard_map/order/pallas_call | solution.py:382
  22.4 2.4 %collective-permute-done.7 = bf16[3,272,128]{2,1,0:T(8,128)(2,1)S(1)} collective-permute-done((bf16[3,272,128]{2,1,0:T(8,128)(2,1)S(1)}, bf16[3,272,128]{2,1,0:T(8,128)(2,1)S(1)}, u32[]{:S(2)}, u32[]{:S(2)}) %collective-permute-start.7) | collective-permute-done | bytes 208928 | tf_op jit(solution)/shard_map/ppermute | solution.py:346
  24.8 4.3 %collective-permute-done.8 = bf16[3,272,128]{2,1,0:T(8,128)(2,1)S(1)} collective-permute-done((bf16[3,272,128]{2,1,0:T(8,128)(2,1)S(1)}, bf16[3,272,128]{2,1,0:T(8,128)(2,1)S(1)}, u32[]{:S(2)}, u32[]{:S(2)}) %collective-permute-start.8) | collective-permute-done | bytes 208928 | tf_op jit(solution)/shard_map/ppermute | solution.py:346
  29.1 0.0 collective-permute-done.9
  29.1 0.0 collective-permute-done.6.refs_2_
  29.2 0.1 collective-permute-start.10
  29.3 2.0 %collective-permute-done.10.refs_3_ = bf16[9,272,128]{2,1,0:T(8,128)(2,1)S(1)} collective-permute-done((bf16[9,272,128]{2,1,0:T(8,128)(2,1)S(1)}, bf16[9,272,128]{2,1,0:T(8,128)(2,1)S(1)}, u32[]{:S(2)}, u32[]{:S(2)}) %collective-permute-start.10) | collective-permute-done | bytes 626720 | tf_op jit(solution)/shard_map/ppermute | solution.py:346
  31.3 0.0 copy-done.1
  31.3 24.3 %render.1 = (f32[3,256]{1,0:T(4,128)}, f32[32,4,256]{2,1,0:T(4,128)S(1)}) custom-call(s32[2,256]{1,0:T(2,128)S(1)} %get-tuple-element.15.meta_ref, s32[1]{0:T(128)} %bitcast.8.me_ref, f32[4,256]{1,0:T(4,128)S(1)} %get-tuple-element.18.slots_ref, f32[2,1280,128]{2,1,0:T(8,128)S(1)} %get-tuple-element.19.rows_ref, f32[3,256]{1,0:T(4,128)S(1)} %copy-done.1, ...), custom_call_target="tpu_custom_call" | custom-call | flops 20000000000 | bytes 30000000 | tf_op jit(solution)/shard_map/render/pallas_call | solution.py:410
  55.7 12.9 %all_to_all.5 = f32[32,4,256]{2,1,0:T(4,128)S(1)} all-to-all(f32[32,4,256]{2,1,0:T(4,128)S(1)} %get-tuple-element.25), channel_id=1, replica_groups=mesh['region'=32] {'region'}, dimensions={0} | all-to-all | bytes 262144 | tf_op jit(solution)/shard_map/all_to_all | solution.py:433
  68.6 0.6 reduce_sum.9
  (12 shorter events, 0.2 us)
Async XLA Ops:
  0.6 16.1 %copy-start.2 = (f32[256,3,128]{2,0,1:T(8,128)S(1)}, f32[256,3,128]{2,0,1:T(8,128)}, u32[]{:S(2)}) copy-start(f32[256,3,128]{2,0,1:T(8,128)} %param.7) | copy-start | bytes 1179652
  0.6 16.1 %copy-start.3 = (f32[256,128]{1,0:T(8,128)S(1)}, f32[256,128]{1,0:T(8,128)}, u32[]{:S(2)}) copy-start(f32[256,128]{1,0:T(8,128)} %param.8) | copy-start | bytes 393220
  2.4 18.0 %copy-start = (s32[256,4]{0,1:T(4,128)S(1)}, s32[256,4]{0,1:T(4,128)}, u32[]{:S(2)}) copy-start(s32[256,4]{0,1:T(4,128)} %param.9) | copy-start | bytes 12292
  2.4 8.9 %collective-permute-start = (bf16[1,272,128]{2,1,0:T(8,128)(2,1)S(1)}, bf16[1,272,128]{2,1,0:T(8,128)(2,1)S(1)}, u32[]{:S(2)}, u32[]{:S(2)}) collective-permute-start(bf16[1,272,128]{2,1,0:T(8,128)(2,1)S(1)} %maximum_bitcast_fusion), channel_id=1, source_target_pairs={{0,8},{1,9},{2,10},{3,11},{4,12},{5,13},{6,14},{7,15},{8,0},{9,1},... | collective-permute-start | bytes 208904 | tf_op jit(solution)/shard_map/ppermute | solution.py:346
  5.5 7.5 %collective-permute-start.1 = (bf16[1,272,128]{2,1,0:T(8,128)(2,1)S(1)}, bf16[1,272,128]{2,1,0:T(8,128)(2,1)S(1)}, u32[]{:S(2)}, u32[]{:S(2)}) collective-permute-start(bf16[1,272,128]{2,1,0:T(8,128)(2,1)S(1)} %maximum_bitcast_fusion), channel_id=1, source_target_pairs={{0,16},{1,17},{2,18},{3,19},{4,20},{5,21},{6,22},{7,23},{8,24},{9,... | collective-permute-start | bytes 208904 | tf_op jit(solution)/shard_map/ppermute | solution.py:346
  8.1 6.2 %collective-permute-start.2 = (bf16[1,272,128]{2,1,0:T(8,128)(2,1)S(1)}, bf16[1,272,128]{2,1,0:T(8,128)(2,1)S(1)}, u32[]{:S(2)}, u32[]{:S(2)}) collective-permute-start(bf16[1,272,128]{2,1,0:T(8,128)(2,1)S(1)} %maximum_bitcast_fusion), channel_id=1, source_target_pairs={{0,24},{1,25},{2,26},{3,27},{4,28},{5,29},{6,30},{7,31},{8,16},{9,... | collective-permute-start | bytes 208904 | tf_op jit(solution)/shard_map/ppermute | solution.py:346
  8.1 6.3 %collective-permute-start.3 = (bf16[1,272,128]{2,1,0:T(8,128)(2,1)S(1)}, bf16[1,272,128]{2,1,0:T(8,128)(2,1)S(1)}, u32[]{:S(2)}, u32[]{:S(2)}) collective-permute-start(bf16[1,272,128]{2,1,0:T(8,128)(2,1)S(1)} %maximum_bitcast_fusion), channel_id=1, source_target_pairs={{0,2},{1,3},{2,0},{3,1},{4,6},{5,7},{6,4},{7,5},{8,10},{9,11},{10,... | collective-permute-start | bytes 208904 | tf_op jit(solution)/shard_map/ppermute | solution.py:346
  9.8 5.1 %collective-permute-start.4 = (bf16[1,272,128]{2,1,0:T(8,128)(2,1)S(1)}, bf16[1,272,128]{2,1,0:T(8,128)(2,1)S(1)}, u32[]{:S(2)}, u32[]{:S(2)}) collective-permute-start(bf16[1,272,128]{2,1,0:T(8,128)(2,1)S(1)} %maximum_bitcast_fusion), channel_id=1, source_target_pairs={{0,4},{1,5},{2,6},{3,7},{4,0},{5,1},{6,2},{7,3},{8,12},{9,13},{10,... | collective-permute-start | bytes 208904 | tf_op jit(solution)/shard_map/ppermute | solution.py:346
  11.3 5.3 %collective-permute-start.5 = (bf16[1,272,128]{2,1,0:T(8,128)(2,1)S(1)}, bf16[1,272,128]{2,1,0:T(8,128)(2,1)S(1)}, u32[]{:S(2)}, u32[]{:S(2)}) collective-permute-start(bf16[1,272,128]{2,1,0:T(8,128)(2,1)S(1)} %maximum_bitcast_fusion), channel_id=1, source_target_pairs={{0,6},{1,7},{2,4},{3,5},{4,2},{5,3},{6,0},{7,1},{8,14},{9,15},{10,... | collective-permute-start | bytes 208904 | tf_op jit(solution)/shard_map/ppermute | solution.py:346
  16.6 12.5 %collective-permute-start.6 = (bf16[7,272,128]{2,1,0:T(8,128)(2,1)S(1)}, bf16[7,272,128]{2,1,0:T(8,128)(2,1)S(1)}, u32[]{:S(2)}, u32[]{:S(2)}) collective-permute-start(bf16[7,272,128]{2,1,0:T(8,128)(2,1)S(1)} %constant_dynamic-update-slice_fusion.refs_0_), channel_id=1, source_target_pairs={{0,1},{1,0},{2,3},{3,2},{4,5},{5,4},{6,7},{7,6},{8,9},{9,8},{10,11... | collective-permute-start | bytes 1462280 | tf_op jit(solution)/shard_map/ppermute | solution.py:346
  16.8 14.6 %copy-start.1 = (f32[3,256]{1,0:T(4,128)S(1)}, f32[3,256]{1,0:T(4,128)}, u32[]{:S(2)}) copy-start(f32[3,256]{1,0:T(4,128)} %colour_grad_ref.1) | copy-start | bytes 9220
  16.8 8.0 %collective-permute-start.7 = (bf16[3,272,128]{2,1,0:T(8,128)(2,1)S(1)}, bf16[3,272,128]{2,1,0:T(8,128)(2,1)S(1)}, u32[]{:S(2)}, u32[]{:S(2)}) collective-permute-start(bf16[3,272,128]{2,1,0:T(8,128)(2,1)S(1)} %pad_maximum_fusion.1), channel_id=1, source_target_pairs={{0,2},{1,3},{2,0},{3,1},{4,6},{5,7},{6,4},{7,5},{8,10},{9,11},{10,... | collective-permute-start | bytes 626696 | tf_op jit(solution)/shard_map/ppermute | solution.py:346
  17.4 11.7 %collective-permute-start.8 = (bf16[3,272,128]{2,1,0:T(8,128)(2,1)S(1)}, bf16[3,272,128]{2,1,0:T(8,128)(2,1)S(1)}, u32[]{:S(2)}, u32[]{:S(2)}) collective-permute-start(bf16[3,272,128]{2,1,0:T(8,128)(2,1)S(1)} %pad_maximum_fusion.1), channel_id=1, source_target_pairs={{0,4},{1,5},{2,6},{3,7},{4,0},{5,1},{6,2},{7,3},{8,12},{9,13},{10,... | collective-permute-start | bytes 626696 | tf_op jit(solution)/shard_map/ppermute | solution.py:346
  17.7 11.4 %collective-permute-start.9 = (bf16[3,272,128]{2,1,0:T(8,128)(2,1)S(1)}, bf16[3,272,128]{2,1,0:T(8,128)(2,1)S(1)}, u32[]{:S(2)}, u32[]{:S(2)}) collective-permute-start(bf16[3,272,128]{2,1,0:T(8,128)(2,1)S(1)} %pad_maximum_fusion.1), channel_id=1, source_target_pairs={{0,6},{1,7},{2,4},{3,5},{4,2},{5,3},{6,0},{7,1},{8,14},{9,15},{10,... | collective-permute-start | bytes 626696 | tf_op jit(solution)/shard_map/ppermute | solution.py:346
  29.2 2.1 %collective-permute-start.10 = (bf16[9,272,128]{2,1,0:T(8,128)(2,1)S(1)}, bf16[9,272,128]{2,1,0:T(8,128)(2,1)S(1)}, u32[]{:S(2)}, u32[]{:S(2)}) collective-permute-start(bf16[9,272,128]{2,1,0:T(8,128)(2,1)S(1)} %constant_dynamic-update-slice_fusion.5.refs_1_), channel_id=1, source_target_pairs={{0,1},{1,0},{2,3},{3,2},{4,5},{5,4},{6,7},{7,6},{8,9},{9,8},{10,11... | collective-permute-start | bytes 1880072 | tf_op jit(solution)/shard_map/ppermute | solution.py:346

commit v7 on v6

--- a/solution.py
+++ b/solution.py
@@ -393,7 +393,8 @@
         name="order",
     )(all_samples, listed)
 
-    early = jnp.concatenate([own, others, *own_second[1:]], axis=0)
+    slots, *own_second = lax.optimization_barrier((slots, *own_second[1:]))
+    early = jnp.concatenate([own, others, *own_second], axis=0)
     if len(stages) > 3:
         near = jnp.concatenate([early, *second[1:]], axis=0)
         for stage in stages[2:-1]:
@@ -401,9 +402,9 @@
         weights = share(near, stages[-1], regions)
     else:
         early, far = share(early, stages[-1], regions)
-        far, slots, *second = lax.optimization_barrier((far, slots, *second[1:]))
-        late, far_late = share(jnp.concatenate(second, axis=0), stages[-1], regions)
-        weights = [early, late, far, far_late]
+        far, second[1] = lax.optimization_barrier((far, second[1]))
+        late = [share(block, stages[-1], regions) for block in second[1:]]
+        weights = [early] + [block for block, _ in late] + [far] + [block for _, block in late]
 
     whole = pl.BlockSpec(memory_space=vmem)
 

time: 69.5 us -> 71.4 us (1.027)
  other arithmetic: 1.48 us -> 2.49 us
    concatenate x1, other arithmetic: 0.04 us -> 1.1 us  [on_device(): jnp.concatenate([sample_points.transpose(1, 0, 2), sample_spacing[None]],...]
    ppermute x11 -> x13, starting transfers between devices: 12.9 us -> 13.5 us  [share(): held.append(lax.ppermute(block, 'region', pairs))]
    ppermute x11 -> x13, waiting for transfers between devices: 13.6 us -> 13.8 us  [share(): held.append(lax.ppermute(block, 'region', pairs))]
  transfers between devices with their start and end apart: 11 -> 13, of which waited for: 7 -> 8; matrix products, arithmetic and copies ran while one was open for 0% -> 2% of each run, Pallas kernels for 3% -> 3%
where the time goes in v7:
time: 71.4 us; the launch traced here: 71.2 us
  Pallas kernels  26.9 us (38%)
  waiting for transfers between devices  13.8 us (19%)
  starting transfers between devices  13.5 us (19%)
  blocking collectives  12.7 us (18%)
  other arithmetic  2.49 us (3%)
  local copies, waits for them, and re-layouts  1.04 us (1%)
  between operations  0.77 us (1%)
    pallas_call x1, Pallas kernels, on_device(): pl.pallas_call(functools.partial(main_kernel, dims, stages, len(weights))...  24.8 us
    ppermute x13, waiting for transfers between devices, share(): held.append(lax.ppermute(block, 'region', pairs))  13.8 us
    ppermute x13, starting transfers between devices, share(): held.append(lax.ppermute(block, 'region', pairs))  13.5 us
    all_to_all x1, blocking collectives, on_device(): lax.all_to_all(head_grad, 'region', split_axis=0, concat_axis=0, tiled=True)  12.7 us
    pallas_call x1, Pallas kernels, on_device(): pl.pallas_call(functools.partial(order_kernel, dims), out_shape=(jax.Shap...  2.1 us
  transfers between devices with their start and end apart: 13, of which 8 were waited for; matrix products, arithmetic and copies ran while one was open for 2% of the time, Pallas kernels for 3%

profile of v7, /device:TPU:0, one launch (start us, length us, event | category | flops | bytes accessed | tf_op | source)
XLA Modules:
  0.0 71.2 jit_solution(17182712401398646249)
XLA Ops:
  0.6 0.0 copy-start
  0.6 0.7 %fusion.1 = bf16[8,256]{1,0:T(8,128)(2,1)S(1)} fusion(bf16[3,64]{1,0:T(4,128)(2,1)} %bitcast.21, bf16[4,256]{1,0:T(4,128)(2,1)} %bitcast.20), kind=kLoop, calls=%fused_computation.10 | loop fusion | flops 12288 | bytes 6528 | tf_op jit(solution)/shard_map/concatenate | solution.py:375
  1.4 0.9 %copy.9 = bf16[1,128,256]{1,2,0:T(8,128)(2,1)S(1)} copy(bf16[1,128,256]{2,1,0:T(8,128)(2,1)} %param.12) | data formatting | bytes 131072 | tf_op args[5]
  2.3 4.0 %collective-permute-start.5 = (bf16[1,272,128]{2,1,0:T(8,128)(2,1)S(1)}, bf16[1,272,128]{2,1,0:T(8,128)(2,1)S(1)}, u32[]{:S(2)}, u32[]{:S(2)}) collective-permute-start(bf16[1,272,128]{2,1,0:T(8,128)(2,1)S(1)} %maximum_bitcast_fusion), channel_id=1, source_target_pairs={{0,6},{1,7},{2,4},{3,5},{4,2},{5,3},{6,0},{7,1},{8,14},{9,15},{10,... | collective-permute-start | bytes 208904 | tf_op jit(solution)/shard_map/ppermute | solution.py:346
  6.3 0.5 collective-permute-start.4
  6.8 3.6 %collective-permute-start.2 = (bf16[1,272,128]{2,1,0:T(8,128)(2,1)S(1)}, bf16[1,272,128]{2,1,0:T(8,128)(2,1)S(1)}, u32[]{:S(2)}, u32[]{:S(2)}) collective-permute-start(bf16[1,272,128]{2,1,0:T(8,128)(2,1)S(1)} %maximum_bitcast_fusion), channel_id=1, source_target_pairs={{0,24},{1,25},{2,26},{3,27},{4,28},{5,29},{6,30},{7,31},{8,16},{9,... | collective-permute-start | bytes 208904 | tf_op jit(solution)/shard_map/ppermute | solution.py:346
  10.4 0.0 collective-permute-start.1
  10.4 0.8 %collective-permute-start = (bf16[1,272,128]{2,1,0:T(8,128)(2,1)S(1)}, bf16[1,272,128]{2,1,0:T(8,128)(2,1)S(1)}, u32[]{:S(2)}, u32[]{:S(2)}) collective-permute-start(bf16[1,272,128]{2,1,0:T(8,128)(2,1)S(1)} %maximum_bitcast_fusion), channel_id=1, source_target_pairs={{0,8},{1,9},{2,10},{3,11},{4,12},{5,13},{6,14},{7,15},{8,0},{9,1},... | collective-permute-start | bytes 208904 | tf_op jit(solution)/shard_map/ppermute | solution.py:346
  11.2 1.1 %pad_maximum_fusion.samples_ref = f32[4,256,128]{2,1,0:T(8,128)S(1)} fusion(f32[1,256,128]{2,1,0:T(8,128)} %bitcast.18, f32[3,256,128]{2,1,0:T(8,128)} %bitcast.17), kind=kLoop, calls=%fused_computation | loop fusion | flops 131072 | bytes 1048576 | tf_op jit(solution)/shard_map/concatenate | solution.py:373
  12.3 1.2 %collective-permute-done.2 = bf16[1,272,128]{2,1,0:T(8,128)(2,1)S(1)} collective-permute-done((bf16[1,272,128]{2,1,0:T(8,128)(2,1)S(1)}, bf16[1,272,128]{2,1,0:T(8,128)(2,1)S(1)}, u32[]{:S(2)}, u32[]{:S(2)}) %collective-permute-start.2) | collective-permute-done | bytes 69664 | tf_op jit(solution)/shard_map/ppermute | solution.py:346
  13.5 0.5 collective-permute-start.3
  14.0 1.9 %collective-permute-done.1 = bf16[1,272,128]{2,1,0:T(8,128)(2,1)S(1)} collective-permute-done((bf16[1,272,128]{2,1,0:T(8,128)(2,1)S(1)}, bf16[1,272,128]{2,1,0:T(8,128)(2,1)S(1)}, u32[]{:S(2)}, u32[]{:S(2)}) %collective-permute-start.1) | collective-permute-done | bytes 69664 | tf_op jit(solution)/shard_map/ppermute | solution.py:346
  15.9 0.1 collective-permute-done
  16.0 0.0 copy-done
  16.0 0.0 copy-start.1
  16.0 2.1 %order.1 = (f32[4,256]{1,0:T(4,128)S(1)}, s32[2,256]{1,0:T(2,128)S(1)}, f32[2,1280,128]{2,1,0:T(8,128)S(1)}) custom-call(f32[4,256,128]{2,1,0:T(8,128)S(1)} %pad_maximum_fusion.samples_ref, s32[4,256]{1,0:T(4,128)S(1)} %bitcast.14), custom_call_target="tpu_custom_call" | custom-call | flops 4000000000 | bytes 10000000 | tf_op jit(solution)/shard_map/order/pallas_call | solution.py:382
  18.1 0.0 collective-permute-done.5
  18.1 0.0 collective-permute-done.4
  18.1 0.0 collective-permute-done.3
  18.2 0.1 collective-permute-start.6
  18.3 1.6 %collective-permute-start.9 = (bf16[3,272,128]{2,1,0:T(8,128)(2,1)S(1)}, bf16[3,272,128]{2,1,0:T(8,128)(2,1)S(1)}, u32[]{:S(2)}, u32[]{:S(2)}) collective-permute-start(bf16[3,272,128]{2,1,0:T(8,128)(2,1)S(1)} %pad_maximum_fusion.1), channel_id=1, source_target_pairs={{0,6},{1,7},{2,4},{3,5},{4,2},{5,3},{6,0},{7,1},{8,14},{9,15},{10,... | collective-permute-start | bytes 626696 | tf_op jit(solution)/shard_map/ppermute | solution.py:346
  19.9 0.5 collective-permute-start.8
  20.4 1.5 %collective-permute-start.7 = (bf16[3,272,128]{2,1,0:T(8,128)(2,1)S(1)}, bf16[3,272,128]{2,1,0:T(8,128)(2,1)S(1)}, u32[]{:S(2)}, u32[]{:S(2)}) collective-permute-start(bf16[3,272,128]{2,1,0:T(8,128)(2,1)S(1)} %pad_maximum_fusion.1), channel_id=1, source_target_pairs={{0,2},{1,3},{2,0},{3,1},{4,6},{5,7},{6,4},{7,5},{8,10},{9,11},{10,... | collective-permute-start | bytes 626696 | tf_op jit(solution)/shard_map/ppermute | solution.py:346
  21.9 5.4 %collective-permute-done.9.refs_3_ = bf16[3,272,128]{2,1,0:T(8,128)(2,1)S(1)} collective-permute-done((bf16[3,272,128]{2,1,0:T(8,128)(2,1)S(1)}, bf16[3,272,128]{2,1,0:T(8,128)(2,1)S(1)}, u32[]{:S(2)}, u32[]{:S(2)}) %collective-permute-start.9) | collective-permute-done | bytes 208928 | tf_op jit(solution)/shard_map/ppermute | solution.py:346
  27.3 0.0 collective-permute-start.12
  27.3 4.0 %collective-permute-done.8.refs_2_ = bf16[3,272,128]{2,1,0:T(8,128)(2,1)S(1)} collective-permute-done((bf16[3,272,128]{2,1,0:T(8,128)(2,1)S(1)}, bf16[3,272,128]{2,1,0:T(8,128)(2,1)S(1)}, u32[]{:S(2)}, u32[]{:S(2)}) %collective-permute-start.8) | collective-permute-done | bytes 208928 | tf_op jit(solution)/shard_map/ppermute | solution.py:346
  31.3 0.0 collective-permute-start.11
  31.3 0.1 collective-permute-done.7.refs_1_
  31.4 0.0 collective-permute-done.6.refs_4_
  31.4 0.4 collective-permute-start.10
  31.8 0.0 collective-permute-done.12.refs_7_
  31.8 0.9 %collective-permute-done.11.refs_6_ = bf16[3,272,128]{2,1,0:T(8,128)(2,1)S(1)} collective-permute-done((bf16[3,272,128]{2,1,0:T(8,128)(2,1)S(1)}, bf16[3,272,128]{2,1,0:T(8,128)(2,1)S(1)}, u32[]{:S(2)}, u32[]{:S(2)}) %collective-permute-start.11) | collective-permute-done | bytes 208928 | tf_op jit(solution)/shard_map/ppermute | solution.py:346
  32.7 0.3 collective-permute-done.10.refs_5_
  33.0 0.0 copy-done.1
  33.0 24.8 %render.1 = (f32[3,256]{1,0:T(4,128)}, f32[32,4,256]{2,1,0:T(4,128)S(1)}) custom-call(s32[2,256]{1,0:T(2,128)S(1)} %get-tuple-element.16.meta_ref, s32[1]{0:T(128)} %bitcast.8.me_ref, f32[4,256]{1,0:T(4,128)S(1)} %get-tuple-element.18.slots_ref, f32[2,1280,128]{2,1,0:T(8,128)S(1)} %get-tuple-element.19.rows_ref, f32[3,256]{1,0:T(4,128)S(1)} %copy-done.1, ...), custom_call_target="tpu_custom_call" | custom-call | flops 20000000000 | bytes 30000000 | tf_op jit(solution)/shard_map/render/pallas_call | solution.py:411
  57.9 12.7 %all_to_all.5 = f32[32,4,256]{2,1,0:T(4,128)S(1)} all-to-all(f32[32,4,256]{2,1,0:T(4,128)S(1)} %get-tuple-element.27), channel_id=1, replica_groups=mesh['region'=32] {'region'}, dimensions={0} | all-to-all | bytes 262144 | tf_op jit(solution)/shard_map/all_to_all | solution.py:434
  70.5 0.6 reduce_sum.9
  (8 shorter events, 0.1 us)
Async XLA Ops:
  0.6 15.4 %copy-start = (s32[256,4]{0,1:T(4,128)S(1)}, s32[256,4]{0,1:T(4,128)}, u32[]{:S(2)}) copy-start(s32[256,4]{0,1:T(4,128)} %param.9) | copy-start | bytes 12292
  2.3 15.8 %collective-permute-start.5 = (bf16[1,272,128]{2,1,0:T(8,128)(2,1)S(1)}, bf16[1,272,128]{2,1,0:T(8,128)(2,1)S(1)}, u32[]{:S(2)}, u32[]{:S(2)}) collective-permute-start(bf16[1,272,128]{2,1,0:T(8,128)(2,1)S(1)} %maximum_bitcast_fusion), channel_id=1, source_target_pairs={{0,6},{1,7},{2,4},{3,5},{4,2},{5,3},{6,0},{7,1},{8,14},{9,15},{10,... | collective-permute-start | bytes 208904 | tf_op jit(solution)/shard_map/ppermute | solution.py:346
  6.3 11.8 %collective-permute-start.4 = (bf16[1,272,128]{2,1,0:T(8,128)(2,1)S(1)}, bf16[1,272,128]{2,1,0:T(8,128)(2,1)S(1)}, u32[]{:S(2)}, u32[]{:S(2)}) collective-permute-start(bf16[1,272,128]{2,1,0:T(8,128)(2,1)S(1)} %maximum_bitcast_fusion), channel_id=1, source_target_pairs={{0,4},{1,5},{2,6},{3,7},{4,0},{5,1},{6,2},{7,3},{8,12},{9,13},{10,... | collective-permute-start | bytes 208904 | tf_op jit(solution)/shard_map/ppermute | solution.py:346
  6.8 6.7 %collective-permute-start.2 = (bf16[1,272,128]{2,1,0:T(8,128)(2,1)S(1)}, bf16[1,272,128]{2,1,0:T(8,128)(2,1)S(1)}, u32[]{:S(2)}, u32[]{:S(2)}) collective-permute-start(bf16[1,272,128]{2,1,0:T(8,128)(2,1)S(1)} %maximum_bitcast_fusion), channel_id=1, source_target_pairs={{0,24},{1,25},{2,26},{3,27},{4,28},{5,29},{6,30},{7,31},{8,16},{9,... | collective-permute-start | bytes 208904 | tf_op jit(solution)/shard_map/ppermute | solution.py:346
  10.4 5.5 %collective-permute-start.1 = (bf16[1,272,128]{2,1,0:T(8,128)(2,1)S(1)}, bf16[1,272,128]{2,1,0:T(8,128)(2,1)S(1)}, u32[]{:S(2)}, u32[]{:S(2)}) collective-permute-start(bf16[1,272,128]{2,1,0:T(8,128)(2,1)S(1)} %maximum_bitcast_fusion), channel_id=1, source_target_pairs={{0,16},{1,17},{2,18},{3,19},{4,20},{5,21},{6,22},{7,23},{8,24},{9,... | collective-permute-start | bytes 208904 | tf_op jit(solution)/shard_map/ppermute | solution.py:346
  10.4 5.6 %collective-permute-start = (bf16[1,272,128]{2,1,0:T(8,128)(2,1)S(1)}, bf16[1,272,128]{2,1,0:T(8,128)(2,1)S(1)}, u32[]{:S(2)}, u32[]{:S(2)}) collective-permute-start(bf16[1,272,128]{2,1,0:T(8,128)(2,1)S(1)} %maximum_bitcast_fusion), channel_id=1, source_target_pairs={{0,8},{1,9},{2,10},{3,11},{4,12},{5,13},{6,14},{7,15},{8,0},{9,1},... | collective-permute-start | bytes 208904 | tf_op jit(solution)/shard_map/ppermute | solution.py:346
  13.5 4.7 %collective-permute-start.3 = (bf16[1,272,128]{2,1,0:T(8,128)(2,1)S(1)}, bf16[1,272,128]{2,1,0:T(8,128)(2,1)S(1)}, u32[]{:S(2)}, u32[]{:S(2)}) collective-permute-start(bf16[1,272,128]{2,1,0:T(8,128)(2,1)S(1)} %maximum_bitcast_fusion), channel_id=1, source_target_pairs={{0,2},{1,3},{2,0},{3,1},{4,6},{5,7},{6,4},{7,5},{8,10},{9,11},{10,... | collective-permute-start | bytes 208904 | tf_op jit(solution)/shard_map/ppermute | solution.py:346
  16.0 17.0 %copy-start.1 = (f32[3,256]{1,0:T(4,128)S(1)}, f32[3,256]{1,0:T(4,128)}, u32[]{:S(2)}) copy-start(f32[3,256]{1,0:T(4,128)} %colour_grad_ref.1) | copy-start | bytes 9220
  18.2 13.1 %collective-permute-start.6 = (bf16[7,272,128]{2,1,0:T(8,128)(2,1)S(1)}, bf16[7,272,128]{2,1,0:T(8,128)(2,1)S(1)}, u32[]{:S(2)}, u32[]{:S(2)}) collective-permute-start(bf16[7,272,128]{2,1,0:T(8,128)(2,1)S(1)} %constant_dynamic-update-slice_fusion.refs_0_), channel_id=1, source_target_pairs={{0,1},{1,0},{2,3},{3,2},{4,5},{5,4},{6,7},{7,6},{8,9},{9,8},{10,11... | collective-permute-start | bytes 1462280 | tf_op jit(solution)/shard_map/ppermute | solution.py:346
  18.3 9.0 %collective-permute-start.9 = (bf16[3,272,128]{2,1,0:T(8,128)(2,1)S(1)}, bf16[3,272,128]{2,1,0:T(8,128)(2,1)S(1)}, u32[]{:S(2)}, u32[]{:S(2)}) collective-permute-start(bf16[3,272,128]{2,1,0:T(8,128)(2,1)S(1)} %pad_maximum_fusion.1), channel_id=1, source_target_pairs={{0,6},{1,7},{2,4},{3,5},{4,2},{5,3},{6,0},{7,1},{8,14},{9,15},{10,... | collective-permute-start | bytes 626696 | tf_op jit(solution)/shard_map/ppermute | solution.py:346
  19.9 11.4 %collective-permute-start.8 = (bf16[3,272,128]{2,1,0:T(8,128)(2,1)S(1)}, bf16[3,272,128]{2,1,0:T(8,128)(2,1)S(1)}, u32[]{:S(2)}, u32[]{:S(2)}) collective-permute-start(bf16[3,272,128]{2,1,0:T(8,128)(2,1)S(1)} %pad_maximum_fusion.1), channel_id=1, source_target_pairs={{0,4},{1,5},{2,6},{3,7},{4,0},{5,1},{6,2},{7,3},{8,12},{9,13},{10,... | collective-permute-start | bytes 626696 | tf_op jit(solution)/shard_map/ppermute | solution.py:346
  20.4 11.0 %collective-permute-start.7 = (bf16[3,272,128]{2,1,0:T(8,128)(2,1)S(1)}, bf16[3,272,128]{2,1,0:T(8,128)(2,1)S(1)}, u32[]{:S(2)}, u32[]{:S(2)}) collective-permute-start(bf16[3,272,128]{2,1,0:T(8,128)(2,1)S(1)} %pad_maximum_fusion.1), channel_id=1, source_target_pairs={{0,2},{1,3},{2,0},{3,1},{4,6},{5,7},{6,4},{7,5},{8,10},{9,11},{10,... | collective-permute-start | bytes 626696 | tf_op jit(solution)/shard_map/ppermute | solution.py:346
  27.3 4.5 %collective-permute-start.12 = (bf16[3,272,128]{2,1,0:T(8,128)(2,1)S(1)}, bf16[3,272,128]{2,1,0:T(8,128)(2,1)S(1)}, u32[]{:S(2)}, u32[]{:S(2)}) collective-permute-start(bf16[3,272,128]{2,1,0:T(8,128)(2,1)S(1)} %collective-permute-done.9.refs_3_), channel_id=1, source_target_pairs={{0,1},{1,0},{2,3},{3,2},{4,5},{5,4},{6,7},{7,6},{8,9},{9,8},{10,11... | collective-permute-start | bytes 626696 | tf_op jit(solution)/shard_map/ppermute | solution.py:346
  31.3 1.5 %collective-permute-start.11 = (bf16[3,272,128]{2,1,0:T(8,128)(2,1)S(1)}, bf16[3,272,128]{2,1,0:T(8,128)(2,1)S(1)}, u32[]{:S(2)}, u32[]{:S(2)}) collective-permute-start(bf16[3,272,128]{2,1,0:T(8,128)(2,1)S(1)} %collective-permute-done.8.refs_2_), channel_id=1, source_target_pairs={{0,1},{1,0},{2,3},{3,2},{4,5},{5,4},{6,7},{7,6},{8,9},{9,8},{10,11... | collective-permute-start | bytes 626696 | tf_op jit(solution)/shard_map/ppermute | solution.py:346
  31.4 1.6 %collective-permute-start.10 = (bf16[3,272,128]{2,1,0:T(8,128)(2,1)S(1)}, bf16[3,272,128]{2,1,0:T(8,128)(2,1)S(1)}, u32[]{:S(2)}, u32[]{:S(2)}) collective-permute-start(bf16[3,272,128]{2,1,0:T(8,128)(2,1)S(1)} %collective-permute-done.7.refs_1_), channel_id=1, source_target_pairs={{0,1},{1,0},{2,3},{3,2},{4,5},{5,4},{6,7},{7,6},{8,9},{9,8},{10,11... | collective-permute-start | bytes 626696 | tf_op jit(solution)/shard_map/ppermute | solution.py:346

commit v8 on v6

--- a/solution.py
+++ b/solution.py
@@ -377,7 +377,9 @@
     own = jnp.concatenate([w_hidden[0].T, *halves_of_small], axis=0)[None]
     first = share(own, stages[0], regions)
     own_second = share(own, stages[1], regions)
-    others, listed = lax.optimization_barrier((jnp.concatenate(first[1:], axis=0), crossed.T))
+    others, listed, own_second[1] = lax.optimization_barrier(
+        (jnp.concatenate(first[1:], axis=0), crossed.T, own_second[1])
+    )
     second = share(others, stages[1], regions)
     slots, meta, rows = pl.pallas_call(
         functools.partial(order_kernel, dims),
@@ -393,16 +395,17 @@
         name="order",
     )(all_samples, listed)
 
-    early = jnp.concatenate([own, others, *own_second[1:]], axis=0)
+    early = jnp.concatenate([own, others], axis=0)
     if len(stages) > 3:
-        near = jnp.concatenate([early, *second[1:]], axis=0)
+        near = jnp.concatenate([early, *own_second[1:], *second[1:]], axis=0)
         for stage in stages[2:-1]:
             near = jnp.concatenate(share(near, stage, regions), axis=0)
         weights = share(near, stages[-1], regions)
     else:
         early, far = share(early, stages[-1], regions)
         far, slots, *second = lax.optimization_barrier((far, slots, *second[1:]))
-        late, far_late = share(jnp.concatenate(second, axis=0), stages[-1], regions)
+        late = jnp.concatenate([*own_second[1:], *second], axis=0)
+        late, far_late = share(late, stages[-1], regions)
         weights = [early, late, far, far_late]
 
     whole = pl.BlockSpec(memory_space=vmem)

time: 69.5 us -> 66.5 us (0.957)
  blocking collectives: 12.9 us -> 10.7 us
  waiting for transfers between devices: 13.6 us -> 11.8 us
  other arithmetic: 1.48 us -> 2.51 us
    all_to_all x1, blocking collectives: 12.9 us -> 10.7 us  [on_device(): lax.all_to_all(head_grad, 'region', split_axis=0, concat_axis=0, tiled=True)]
    ppermute x11, waiting for transfers between devices: 13.6 us -> 11.8 us  [share(): held.append(lax.ppermute(block, 'region', pairs))]
    concatenate x1, other arithmetic: 0.04 us -> 1.1 us  [on_device(): jnp.concatenate([sample_points.transpose(1, 0, 2), sample_spacing[None]],...]
  transfers between devices with their start and end apart: 11 -> 11, of which waited for: 7 -> 6; matrix products, arithmetic and copies ran while one was open for 0% -> 2% of each run, Pallas kernels for 3% -> 3%
where the time goes in v8:
time: 66.5 us; the launch traced here: 66.2 us
  Pallas kernels  26.4 us (40%)
  starting transfers between devices  12.9 us (19%)
  waiting for transfers between devices  11.8 us (18%)
  blocking collectives  10.7 us (16%)
  other arithmetic  2.51 us (4%)
  local copies, waits for them, and re-layouts  1.09 us (2%)
  between operations  0.78 us (1%)
    pallas_call x1, Pallas kernels, on_device(): pl.pallas_call(functools.partial(main_kernel, dims, stages, len(weights))...  24.3 us
    ppermute x11, starting transfers between devices, share(): held.append(lax.ppermute(block, 'region', pairs))  12.9 us
    ppermute x11, waiting for transfers between devices, share(): held.append(lax.ppermute(block, 'region', pairs))  11.8 us
    all_to_all x1, blocking collectives, on_device(): lax.all_to_all(head_grad, 'region', split_axis=0, concat_axis=0, tiled=True)  10.7 us
    pallas_call x1, Pallas kernels, on_device(): pl.pallas_call(functools.partial(order_kernel, dims), out_shape=(jax.Shap...  2.09 us
  transfers between devices with their start and end apart: 11, of which 6 were waited for; matrix products, arithmetic and copies ran while one was open for 2% of the time, Pallas kernels for 3%

profile of v8, /device:TPU:0, one launch (start us, length us, event | category | flops | bytes accessed | tf_op | source)
XLA Modules:
  0.0 66.2 jit_solution(7389552384115755645)
XLA Ops:
  0.6 0.0 copy-start
  0.6 0.7 %fusion.1 = bf16[8,256]{1,0:T(8,128)(2,1)S(1)} fusion(bf16[3,64]{1,0:T(4,128)(2,1)} %bitcast.18, bf16[4,256]{1,0:T(4,128)(2,1)} %bitcast.17), kind=kLoop, calls=%fused_computation.12 | loop fusion | flops 12288 | bytes 6528 | tf_op jit(solution)/shard_map/concatenate | solution.py:375
  1.4 0.9 %copy.9 = bf16[1,128,256]{1,2,0:T(8,128)(2,1)S(1)} copy(bf16[1,128,256]{2,1,0:T(8,128)(2,1)} %param.12) | data formatting | bytes 131072 | tf_op args[5]
  2.3 3.1 %collective-permute-start = (bf16[1,272,128]{2,1,0:T(8,128)(2,1)S(1)}, bf16[1,272,128]{2,1,0:T(8,128)(2,1)S(1)}, u32[]{:S(2)}, u32[]{:S(2)}) collective-permute-start(bf16[1,272,128]{2,1,0:T(8,128)(2,1)S(1)} %maximum_bitcast_fusion), channel_id=1, source_target_pairs={{0,8},{1,9},{2,10},{3,11},{4,12},{5,13},{6,14},{7,15},{8,0},{9,1},... | collective-permute-start | bytes 208904 | tf_op jit(solution)/shard_map/ppermute | solution.py:346
  5.4 2.6 %collective-permute-start.1 = (bf16[1,272,128]{2,1,0:T(8,128)(2,1)S(1)}, bf16[1,272,128]{2,1,0:T(8,128)(2,1)S(1)}, u32[]{:S(2)}, u32[]{:S(2)}) collective-permute-start(bf16[1,272,128]{2,1,0:T(8,128)(2,1)S(1)} %maximum_bitcast_fusion), channel_id=1, source_target_pairs={{0,16},{1,17},{2,18},{3,19},{4,20},{5,21},{6,22},{7,23},{8,24},{9,... | collective-permute-start | bytes 208904 | tf_op jit(solution)/shard_map/ppermute | solution.py:346
  8.0 0.0 collective-permute-start.2
  8.0 1.7 %collective-permute-start.3 = (bf16[1,272,128]{2,1,0:T(8,128)(2,1)S(1)}, bf16[1,272,128]{2,1,0:T(8,128)(2,1)S(1)}, u32[]{:S(2)}, u32[]{:S(2)}) collective-permute-start(bf16[1,272,128]{2,1,0:T(8,128)(2,1)S(1)} %maximum_bitcast_fusion), channel_id=1, source_target_pairs={{0,2},{1,3},{2,0},{3,1},{4,6},{5,7},{6,4},{7,5},{8,10},{9,11},{10,... | collective-permute-start | bytes 208904 | tf_op jit(solution)/shard_map/ppermute | solution.py:346
  9.7 1.5 %collective-permute-start.8 = (bf16[1,272,128]{2,1,0:T(8,128)(2,1)S(1)}, bf16[1,272,128]{2,1,0:T(8,128)(2,1)S(1)}, u32[]{:S(2)}, u32[]{:S(2)}) collective-permute-start(bf16[1,272,128]{2,1,0:T(8,128)(2,1)S(1)} %maximum_bitcast_fusion), channel_id=1, source_target_pairs={{0,4},{1,5},{2,6},{3,7},{4,0},{5,1},{6,2},{7,3},{8,12},{9,13},{10,... | collective-permute-start | bytes 208904 | tf_op jit(solution)/shard_map/ppermute | solution.py:346
  11.2 1.1 %pad_maximum_fusion.samples_ref = f32[4,256,128]{2,1,0:T(8,128)S(1)} fusion(f32[1,256,128]{2,1,0:T(8,128)} %bitcast.15, f32[3,256,128]{2,1,0:T(8,128)} %bitcast.13), kind=kLoop, calls=%fused_computation | loop fusion | flops 131072 | bytes 1048576 | tf_op jit(solution)/shard_map/concatenate | solution.py:373
  12.3 0.0 collective-permute-done
  12.4 0.3 collective-permute-start.9
  12.7 0.3 collective-permute-done.1
  12.9 1.3 %collective-permute-done.2 = bf16[1,272,128]{2,1,0:T(8,128)(2,1)S(1)} collective-permute-done((bf16[1,272,128]{2,1,0:T(8,128)(2,1)S(1)}, bf16[1,272,128]{2,1,0:T(8,128)(2,1)S(1)}, u32[]{:S(2)}, u32[]{:S(2)}) %collective-permute-start.2) | collective-permute-done | bytes 69664 | tf_op jit(solution)/shard_map/ppermute | solution.py:346
  14.3 0.0 collective-permute-done.3
  14.3 1.6 %collective-permute-start.5 = (bf16[3,272,128]{2,1,0:T(8,128)(2,1)S(1)}, bf16[3,272,128]{2,1,0:T(8,128)(2,1)S(1)}, u32[]{:S(2)}, u32[]{:S(2)}) collective-permute-start(bf16[3,272,128]{2,1,0:T(8,128)(2,1)S(1)} %pad_maximum_fusion.2), channel_id=1, source_target_pairs={{0,2},{1,3},{2,0},{3,1},{4,6},{5,7},{6,4},{7,5},{8,10},{9,11},{10,... | collective-permute-start | bytes 626696 | tf_op jit(solution)/shard_map/ppermute | solution.py:346
  15.9 1.5 %collective-permute-start.6 = (bf16[3,272,128]{2,1,0:T(8,128)(2,1)S(1)}, bf16[3,272,128]{2,1,0:T(8,128)(2,1)S(1)}, u32[]{:S(2)}, u32[]{:S(2)}) collective-permute-start(bf16[3,272,128]{2,1,0:T(8,128)(2,1)S(1)} %pad_maximum_fusion.2), channel_id=1, source_target_pairs={{0,4},{1,5},{2,6},{3,7},{4,0},{5,1},{6,2},{7,3},{8,12},{9,13},{10,... | collective-permute-start | bytes 626696 | tf_op jit(solution)/shard_map/ppermute | solution.py:346
  17.4 0.0 collective-permute-start.4
  17.4 0.0 copy-done
  17.4 2.1 %order.1 = (f32[4,256]{1,0:T(4,128)S(1)}, s32[2,256]{1,0:T(2,128)S(1)}, f32[2,1280,128]{2,1,0:T(8,128)S(1)}) custom-call(f32[4,256,128]{2,1,0:T(8,128)S(1)} %pad_maximum_fusion.samples_ref, s32[4,256]{1,0:T(4,128)S(1)} %bitcast.12), custom_call_target="tpu_custom_call" | custom-call | flops 4000000000 | bytes 10000000 | tf_op jit(solution)/shard_map/order/pallas_call | solution.py:384
  19.5 0.0 copy-start.1
  19.5 0.0 collective-permute-done.8
  19.5 0.5 collective-permute-start.7
  20.1 0.0 collective-permute-done.9
  20.1 0.1 collective-permute-done.5
  20.2 1.5 %collective-permute-done.6 = bf16[3,272,128]{2,1,0:T(8,128)(2,1)S(1)} collective-permute-done((bf16[3,272,128]{2,1,0:T(8,128)(2,1)S(1)}, bf16[3,272,128]{2,1,0:T(8,128)(2,1)S(1)}, u32[]{:S(2)}, u32[]{:S(2)}) %collective-permute-start.6) | collective-permute-done | bytes 208928 | tf_op jit(solution)/shard_map/ppermute | solution.py:346
  21.7 6.4 %collective-permute-done.7 = bf16[3,272,128]{2,1,0:T(8,128)(2,1)S(1)} collective-permute-done((bf16[3,272,128]{2,1,0:T(8,128)(2,1)S(1)}, bf16[3,272,128]{2,1,0:T(8,128)(2,1)S(1)}, u32[]{:S(2)}, u32[]{:S(2)}) %collective-permute-start.7) | collective-permute-done | bytes 208928 | tf_op jit(solution)/shard_map/ppermute | solution.py:346
  28.1 0.0 collective-permute-done.4.refs_2_
  28.2 0.1 collective-permute-start.10
  28.2 2.3 %collective-permute-done.10.refs_3_ = bf16[12,272,128]{2,1,0:T(8,128)(2,1)S(1)} collective-permute-done((bf16[12,272,128]{2,1,0:T(8,128)(2,1)S(1)}, bf16[12,272,128]{2,1,0:T(8,128)(2,1)S(1)}, u32[]{:S(2)}, u32[]{:S(2)}) %collective-permute-start.10) | collective-permute-done | bytes 835616 | tf_op jit(solution)/shard_map/ppermute | solution.py:346
  30.6 0.0 copy-done.1
  30.6 24.3 %render.1 = (f32[3,256]{1,0:T(4,128)}, f32[32,4,256]{2,1,0:T(4,128)S(1)}) custom-call(s32[2,256]{1,0:T(2,128)S(1)} %get-tuple-element.16.meta_ref, s32[1]{0:T(128)} %bitcast.8.me_ref, f32[4,256]{1,0:T(4,128)S(1)} %get-tuple-element.19.slots_ref, f32[2,1280,128]{2,1,0:T(8,128)S(1)} %get-tuple-element.20.rows_ref, f32[3,256]{1,0:T(4,128)S(1)} %copy-done.1, ...), custom_call_target="tpu_custom_call" | custom-call | flops 20000000000 | bytes 30000000 | tf_op jit(solution)/shard_map/render/pallas_call | solution.py:413
  54.9 10.7 %all_to_all.5 = f32[32,4,256]{2,1,0:T(4,128)S(1)} all-to-all(f32[32,4,256]{2,1,0:T(4,128)S(1)} %get-tuple-element.27), channel_id=1, replica_groups=mesh['region'=32] {'region'}, dimensions={0} | all-to-all | bytes 262144 | tf_op jit(solution)/shard_map/all_to_all | solution.py:436
  65.6 0.6 reduce_sum.9
  (10 shorter events, 0.2 us)
Async XLA Ops:
  0.6 16.7 %copy-start = (s32[256,4]{0,1:T(4,128)S(1)}, s32[256,4]{0,1:T(4,128)}, u32[]{:S(2)}) copy-start(s32[256,4]{0,1:T(4,128)} %param.9) | copy-start | bytes 12292
  2.3 10.0 %collective-permute-start = (bf16[1,272,128]{2,1,0:T(8,128)(2,1)S(1)}, bf16[1,272,128]{2,1,0:T(8,128)(2,1)S(1)}, u32[]{:S(2)}, u32[]{:S(2)}) collective-permute-start(bf16[1,272,128]{2,1,0:T(8,128)(2,1)S(1)} %maximum_bitcast_fusion), channel_id=1, source_target_pairs={{0,8},{1,9},{2,10},{3,11},{4,12},{5,13},{6,14},{7,15},{8,0},{9,1},... | collective-permute-start | bytes 208904 | tf_op jit(solution)/shard_map/ppermute | solution.py:346
  5.4 7.5 %collective-permute-start.1 = (bf16[1,272,128]{2,1,0:T(8,128)(2,1)S(1)}, bf16[1,272,128]{2,1,0:T(8,128)(2,1)S(1)}, u32[]{:S(2)}, u32[]{:S(2)}) collective-permute-start(bf16[1,272,128]{2,1,0:T(8,128)(2,1)S(1)} %maximum_bitcast_fusion), channel_id=1, source_target_pairs={{0,16},{1,17},{2,18},{3,19},{4,20},{5,21},{6,22},{7,23},{8,24},{9,... | collective-permute-start | bytes 208904 | tf_op jit(solution)/shard_map/ppermute | solution.py:346
  8.0 6.2 %collective-permute-start.2 = (bf16[1,272,128]{2,1,0:T(8,128)(2,1)S(1)}, bf16[1,272,128]{2,1,0:T(8,128)(2,1)S(1)}, u32[]{:S(2)}, u32[]{:S(2)}) collective-permute-start(bf16[1,272,128]{2,1,0:T(8,128)(2,1)S(1)} %maximum_bitcast_fusion), channel_id=1, source_target_pairs={{0,24},{1,25},{2,26},{3,27},{4,28},{5,29},{6,30},{7,31},{8,16},{9,... | collective-permute-start | bytes 208904 | tf_op jit(solution)/shard_map/ppermute | solution.py:346
  8.0 6.2 %collective-permute-start.3 = (bf16[1,272,128]{2,1,0:T(8,128)(2,1)S(1)}, bf16[1,272,128]{2,1,0:T(8,128)(2,1)S(1)}, u32[]{:S(2)}, u32[]{:S(2)}) collective-permute-start(bf16[1,272,128]{2,1,0:T(8,128)(2,1)S(1)} %maximum_bitcast_fusion), channel_id=1, source_target_pairs={{0,2},{1,3},{2,0},{3,1},{4,6},{5,7},{6,4},{7,5},{8,10},{9,11},{10,... | collective-permute-start | bytes 208904 | tf_op jit(solution)/shard_map/ppermute | solution.py:346
  9.7 9.8 %collective-permute-start.8 = (bf16[1,272,128]{2,1,0:T(8,128)(2,1)S(1)}, bf16[1,272,128]{2,1,0:T(8,128)(2,1)S(1)}, u32[]{:S(2)}, u32[]{:S(2)}) collective-permute-start(bf16[1,272,128]{2,1,0:T(8,128)(2,1)S(1)} %maximum_bitcast_fusion), channel_id=1, source_target_pairs={{0,4},{1,5},{2,6},{3,7},{4,0},{5,1},{6,2},{7,3},{8,12},{9,13},{10,... | collective-permute-start | bytes 208904 | tf_op jit(solution)/shard_map/ppermute | solution.py:346
  12.4 7.7 %collective-permute-start.9 = (bf16[1,272,128]{2,1,0:T(8,128)(2,1)S(1)}, bf16[1,272,128]{2,1,0:T(8,128)(2,1)S(1)}, u32[]{:S(2)}, u32[]{:S(2)}) collective-permute-start(bf16[1,272,128]{2,1,0:T(8,128)(2,1)S(1)} %maximum_bitcast_fusion), channel_id=1, source_target_pairs={{0,6},{1,7},{2,4},{3,5},{4,2},{5,3},{6,0},{7,1},{8,14},{9,15},{10,... | collective-permute-start | bytes 208904 | tf_op jit(solution)/shard_map/ppermute | solution.py:346
  14.3 5.9 %collective-permute-start.5 = (bf16[3,272,128]{2,1,0:T(8,128)(2,1)S(1)}, bf16[3,272,128]{2,1,0:T(8,128)(2,1)S(1)}, u32[]{:S(2)}, u32[]{:S(2)}) collective-permute-start(bf16[3,272,128]{2,1,0:T(8,128)(2,1)S(1)} %pad_maximum_fusion.2), channel_id=1, source_target_pairs={{0,2},{1,3},{2,0},{3,1},{4,6},{5,7},{6,4},{7,5},{8,10},{9,11},{10,... | collective-permute-start | bytes 626696 | tf_op jit(solution)/shard_map/ppermute | solution.py:346
  15.9 5.8 %collective-permute-start.6 = (bf16[3,272,128]{2,1,0:T(8,128)(2,1)S(1)}, bf16[3,272,128]{2,1,0:T(8,128)(2,1)S(1)}, u32[]{:S(2)}, u32[]{:S(2)}) collective-permute-start(bf16[3,272,128]{2,1,0:T(8,128)(2,1)S(1)} %pad_maximum_fusion.2), channel_id=1, source_target_pairs={{0,4},{1,5},{2,6},{3,7},{4,0},{5,1},{6,2},{7,3},{8,12},{9,13},{10,... | collective-permute-start | bytes 626696 | tf_op jit(solution)/shard_map/ppermute | solution.py:346
  17.4 10.7 %collective-permute-start.4 = (bf16[4,272,128]{2,1,0:T(8,128)(2,1)S(1)}, bf16[4,272,128]{2,1,0:T(8,128)(2,1)S(1)}, u32[]{:S(2)}, u32[]{:S(2)}) collective-permute-start(bf16[4,272,128]{2,1,0:T(8,128)(2,1)S(1)} %pad_maximum_fusion.1.refs_0_), channel_id=1, source_target_pairs={{0,1},{1,0},{2,3},{3,2},{4,5},{5,4},{6,7},{7,6},{8,9},{9,8},{10,11... | collective-permute-start | bytes 835592 | tf_op jit(solution)/shard_map/ppermute | solution.py:346
  19.5 11.1 %copy-start.1 = (f32[3,256]{1,0:T(4,128)S(1)}, f32[3,256]{1,0:T(4,128)}, u32[]{:S(2)}) copy-start(f32[3,256]{1,0:T(4,128)} %colour_grad_ref.1) | copy-start | bytes 9220
  19.5 8.5 %collective-permute-start.7 = (bf16[3,272,128]{2,1,0:T(8,128)(2,1)S(1)}, bf16[3,272,128]{2,1,0:T(8,128)(2,1)S(1)}, u32[]{:S(2)}, u32[]{:S(2)}) collective-permute-start(bf16[3,272,128]{2,1,0:T(8,128)(2,1)S(1)} %pad_maximum_fusion.2), channel_id=1, source_target_pairs={{0,6},{1,7},{2,4},{3,5},{4,2},{5,3},{6,0},{7,1},{8,14},{9,15},{10,... | collective-permute-start | bytes 626696 | tf_op jit(solution)/shard_map/ppermute | solution.py:346
  28.2 2.4 %collective-permute-start.10 = (bf16[12,272,128]{2,1,0:T(8,128)(2,1)S(1)}, bf16[12,272,128]{2,1,0:T(8,128)(2,1)S(1)}, u32[]{:S(2)}, u32[]{:S(2)}) collective-permute-start(bf16[12,272,128]{2,1,0:T(8,128)(2,1)S(1)} %constant_dynamic-update-slice_fusion.refs_1_), channel_id=1, source_target_pairs={{0,1},{1,0},{2,3},{3,2},{4,5},{5,4},{6,7},{7,6},{8,9},{9,8},{10,11... | collective-permute-start | bytes 2506760 | tf_op jit(solution)/shard_map/ppermute | solution.py:346

commit v9 on v8

--- a/solution.py
+++ b/solution.py
@@ -377,10 +377,11 @@
     own = jnp.concatenate([w_hidden[0].T, *halves_of_small], axis=0)[None]
     first = share(own, stages[0], regions)
     own_second = share(own, stages[1], regions)
-    others, listed, own_second[1] = lax.optimization_barrier(
-        (jnp.concatenate(first[1:], axis=0), crossed.T, own_second[1])
+    others, own_second[1] = lax.optimization_barrier(
+        (jnp.concatenate(first[1:], axis=0), own_second[1])
     )
     second = share(others, stages[1], regions)
+    second[1], listed = lax.optimization_barrier((second[1], crossed.T))
     slots, meta, rows = pl.pallas_call(
         functools.partial(order_kernel, dims),
         out_shape=(

time: 66.5 us -> 70.2 us (1.056)
  waiting for transfers between devices: 11.8 us -> 13.8 us
  blocking collectives: 10.7 us -> 12.3 us
    ppermute x11, waiting for transfers between devices: 11.8 us -> 13.8 us  [share(): held.append(lax.ppermute(block, 'region', pairs))]
    all_to_all x1, blocking collectives: 10.7 us -> 12.3 us  [on_device(): lax.all_to_all(head_grad, 'region', split_axis=0, concat_axis=0, tiled=True)]
where the time goes in v9:
time: 70.2 us; the launch traced here: 69.9 us
  Pallas kernels  26.4 us (38%)
  waiting for transfers between devices  13.8 us (20%)
  starting transfers between devices  13.1 us (19%)
  blocking collectives  12.3 us (18%)
  other arithmetic  2.51 us (4%)
  local copies, waits for them, and re-layouts  1.09 us (2%)
  between operations  0.78 us (1%)
    pallas_call x1, Pallas kernels, on_device(): pl.pallas_call(functools.partial(main_kernel, dims, stages, len(weights))...  24.3 us
    ppermute x11, waiting for transfers between devices, share(): held.append(lax.ppermute(block, 'region', pairs))  13.8 us
    ppermute x11, starting transfers between devices, share(): held.append(lax.ppermute(block, 'region', pairs))  13.1 us
    all_to_all x1, blocking collectives, on_device(): lax.all_to_all(head_grad, 'region', split_axis=0, concat_axis=0, tiled=True)  12.3 us
    pallas_call x1, Pallas kernels, on_device(): pl.pallas_call(functools.partial(order_kernel, dims), out_shape=(jax.Shap...  2.09 us
  transfers between devices with their start and end apart: 11, of which 6 were waited for; matrix products, arithmetic and copies ran while one was open for 2% of the time, Pallas kernels for 3%

profile of v9, /device:TPU:0, one launch (start us, length us, event | category | flops | bytes accessed | tf_op | source)
XLA Modules:
  0.0 69.9 jit_solution(6996845918369417150)
XLA Ops:
  0.6 0.7 %fusion.1 = bf16[8,256]{1,0:T(8,128)(2,1)S(1)} fusion(bf16[3,64]{1,0:T(4,128)(2,1)} %bitcast.18, bf16[4,256]{1,0:T(4,128)(2,1)} %bitcast.17), kind=kLoop, calls=%fused_computation.12 | loop fusion | flops 12288 | bytes 6528 | tf_op jit(solution)/shard_map/concatenate | solution.py:375
  1.3 0.9 %copy.9 = bf16[1,128,256]{1,2,0:T(8,128)(2,1)S(1)} copy(bf16[1,128,256]{2,1,0:T(8,128)(2,1)} %param.12) | data formatting | bytes 131072 | tf_op args[5]
  2.3 0.0 copy-start
  2.3 4.0 %collective-permute-start.9 = (bf16[1,272,128]{2,1,0:T(8,128)(2,1)S(1)}, bf16[1,272,128]{2,1,0:T(8,128)(2,1)S(1)}, u32[]{:S(2)}, u32[]{:S(2)}) collective-permute-start(bf16[1,272,128]{2,1,0:T(8,128)(2,1)S(1)} %maximum_bitcast_fusion), channel_id=1, source_target_pairs={{0,6},{1,7},{2,4},{3,5},{4,2},{5,3},{6,0},{7,1},{8,14},{9,15},{10,... | collective-permute-start | bytes 208904 | tf_op jit(solution)/shard_map/ppermute | solution.py:346
  6.3 0.5 collective-permute-start.8
  6.8 3.6 %collective-permute-start.2 = (bf16[1,272,128]{2,1,0:T(8,128)(2,1)S(1)}, bf16[1,272,128]{2,1,0:T(8,128)(2,1)S(1)}, u32[]{:S(2)}, u32[]{:S(2)}) collective-permute-start(bf16[1,272,128]{2,1,0:T(8,128)(2,1)S(1)} %maximum_bitcast_fusion), channel_id=1, source_target_pairs={{0,24},{1,25},{2,26},{3,27},{4,28},{5,29},{6,30},{7,31},{8,16},{9,... | collective-permute-start | bytes 208904 | tf_op jit(solution)/shard_map/ppermute | solution.py:346
  10.4 0.0 collective-permute-start.1
  10.4 0.8 %collective-permute-start = (bf16[1,272,128]{2,1,0:T(8,128)(2,1)S(1)}, bf16[1,272,128]{2,1,0:T(8,128)(2,1)S(1)}, u32[]{:S(2)}, u32[]{:S(2)}) collective-permute-start(bf16[1,272,128]{2,1,0:T(8,128)(2,1)S(1)} %maximum_bitcast_fusion), channel_id=1, source_target_pairs={{0,8},{1,9},{2,10},{3,11},{4,12},{5,13},{6,14},{7,15},{8,0},{9,1},... | collective-permute-start | bytes 208904 | tf_op jit(solution)/shard_map/ppermute | solution.py:346
  11.2 1.1 %pad_maximum_fusion.samples_ref = f32[4,256,128]{2,1,0:T(8,128)S(1)} fusion(f32[1,256,128]{2,1,0:T(8,128)} %bitcast.15, f32[3,256,128]{2,1,0:T(8,128)} %bitcast.13), kind=kLoop, calls=%fused_computation | loop fusion | flops 131072 | bytes 1048576 | tf_op jit(solution)/shard_map/concatenate | solution.py:373
  12.3 1.2 %collective-permute-done.2 = bf16[1,272,128]{2,1,0:T(8,128)(2,1)S(1)} collective-permute-done((bf16[1,272,128]{2,1,0:T(8,128)(2,1)S(1)}, bf16[1,272,128]{2,1,0:T(8,128)(2,1)S(1)}, u32[]{:S(2)}, u32[]{:S(2)}) %collective-permute-start.2) | collective-permute-done | bytes 69664 | tf_op jit(solution)/shard_map/ppermute | solution.py:346
  13.5 0.5 collective-permute-start.3
  14.0 1.9 %collective-permute-done.1 = bf16[1,272,128]{2,1,0:T(8,128)(2,1)S(1)} collective-permute-done((bf16[1,272,128]{2,1,0:T(8,128)(2,1)S(1)}, bf16[1,272,128]{2,1,0:T(8,128)(2,1)S(1)}, u32[]{:S(2)}, u32[]{:S(2)}) %collective-permute-start.1) | collective-permute-done | bytes 69664 | tf_op jit(solution)/shard_map/ppermute | solution.py:346
  15.9 0.1 collective-permute-done
  16.0 1.8 %collective-permute-done.3 = bf16[1,272,128]{2,1,0:T(8,128)(2,1)S(1)} collective-permute-done((bf16[1,272,128]{2,1,0:T(8,128)(2,1)S(1)}, bf16[1,272,128]{2,1,0:T(8,128)(2,1)S(1)}, u32[]{:S(2)}, u32[]{:S(2)}) %collective-permute-start.3) | collective-permute-done | bytes 69664 | tf_op jit(solution)/shard_map/ppermute | solution.py:346
  17.8 1.6 %collective-permute-start.7 = (bf16[3,272,128]{2,1,0:T(8,128)(2,1)S(1)}, bf16[3,272,128]{2,1,0:T(8,128)(2,1)S(1)}, u32[]{:S(2)}, u32[]{:S(2)}) collective-permute-start(bf16[3,272,128]{2,1,0:T(8,128)(2,1)S(1)} %pad_maximum_fusion.2), channel_id=1, source_target_pairs={{0,6},{1,7},{2,4},{3,5},{4,2},{5,3},{6,0},{7,1},{8,14},{9,15},{10,... | collective-permute-start | bytes 626696 | tf_op jit(solution)/shard_map/ppermute | solution.py:346
  19.4 0.5 collective-permute-start.6
  19.9 1.5 %collective-permute-start.4 = (bf16[3,272,128]{2,1,0:T(8,128)(2,1)S(1)}, bf16[3,272,128]{2,1,0:T(8,128)(2,1)S(1)}, u32[]{:S(2)}, u32[]{:S(2)}) collective-permute-start(bf16[3,272,128]{2,1,0:T(8,128)(2,1)S(1)} %pad_maximum_fusion.2), channel_id=1, source_target_pairs={{0,2},{1,3},{2,0},{3,1},{4,6},{5,7},{6,4},{7,5},{8,10},{9,11},{10,... | collective-permute-start | bytes 626696 | tf_op jit(solution)/shard_map/ppermute | solution.py:346
  21.4 0.0 collective-permute-done.8
  21.4 0.1 collective-permute-start.5
  21.5 0.0 collective-permute-done.9
  21.5 6.5 %collective-permute-done.4 = bf16[3,272,128]{2,1,0:T(8,128)(2,1)S(1)} collective-permute-done((bf16[3,272,128]{2,1,0:T(8,128)(2,1)S(1)}, bf16[3,272,128]{2,1,0:T(8,128)(2,1)S(1)}, u32[]{:S(2)}, u32[]{:S(2)}) %collective-permute-start.4) | collective-permute-done | bytes 208928 | tf_op jit(solution)/shard_map/ppermute | solution.py:346
  28.0 0.0 copy-done
  28.0 0.0 copy-start.1
  28.0 2.1 %order.1 = (f32[4,256]{1,0:T(4,128)S(1)}, s32[2,256]{1,0:T(2,128)S(1)}, f32[2,1280,128]{2,1,0:T(8,128)S(1)}) custom-call(f32[4,256,128]{2,1,0:T(8,128)S(1)} %pad_maximum_fusion.samples_ref, s32[4,256]{1,0:T(4,128)S(1)} %bitcast.12), custom_call_target="tpu_custom_call" | custom-call | flops 4000000000 | bytes 10000000 | tf_op jit(solution)/shard_map/order/pallas_call | solution.py:385
  30.1 0.0 collective-permute-done.7
  30.1 0.0 collective-permute-done.6
  30.1 0.0 collective-permute-done.5.refs_2_
  30.2 0.1 collective-permute-start.10
  30.3 2.3 %collective-permute-done.10.refs_3_ = bf16[12,272,128]{2,1,0:T(8,128)(2,1)S(1)} collective-permute-done((bf16[12,272,128]{2,1,0:T(8,128)(2,1)S(1)}, bf16[12,272,128]{2,1,0:T(8,128)(2,1)S(1)}, u32[]{:S(2)}, u32[]{:S(2)}) %collective-permute-start.10) | collective-permute-done | bytes 835616 | tf_op jit(solution)/shard_map/ppermute | solution.py:346
  32.7 0.0 copy-done.1
  32.7 24.3 %render.1 = (f32[3,256]{1,0:T(4,128)}, f32[32,4,256]{2,1,0:T(4,128)S(1)}) custom-call(s32[2,256]{1,0:T(2,128)S(1)} %get-tuple-element.18.meta_ref, s32[1]{0:T(128)} %bitcast.8.me_ref, f32[4,256]{1,0:T(4,128)S(1)} %get-tuple-element.21.slots_ref, f32[2,1280,128]{2,1,0:T(8,128)S(1)} %get-tuple-element.22.rows_ref, f32[3,256]{1,0:T(4,128)S(1)} %copy-done.1, ...), custom_call_target="tpu_custom_call" | custom-call | flops 20000000000 | bytes 30000000 | tf_op jit(solution)/shard_map/render/pallas_call | solution.py:414
  57.0 12.3 %all_to_all.5 = f32[32,4,256]{2,1,0:T(4,128)S(1)} all-to-all(f32[32,4,256]{2,1,0:T(4,128)S(1)} %get-tuple-element.29), channel_id=1, replica_groups=mesh['region'=32] {'region'}, dimensions={0} | all-to-all | bytes 262144 | tf_op jit(solution)/shard_map/all_to_all | solution.py:437
  69.3 0.6 reduce_sum.9
  (10 shorter events, 0.2 us)
Async XLA Ops:
  2.3 25.7 %copy-start = (s32[256,4]{0,1:T(4,128)S(1)}, s32[256,4]{0,1:T(4,128)}, u32[]{:S(2)}) copy-start(s32[256,4]{0,1:T(4,128)} %param.9) | copy-start | bytes 12292
  2.3 19.2 %collective-permute-start.9 = (bf16[1,272,128]{2,1,0:T(8,128)(2,1)S(1)}, bf16[1,272,128]{2,1,0:T(8,128)(2,1)S(1)}, u32[]{:S(2)}, u32[]{:S(2)}) collective-permute-start(bf16[1,272,128]{2,1,0:T(8,128)(2,1)S(1)} %maximum_bitcast_fusion), channel_id=1, source_target_pairs={{0,6},{1,7},{2,4},{3,5},{4,2},{5,3},{6,0},{7,1},{8,14},{9,15},{10,... | collective-permute-start | bytes 208904 | tf_op jit(solution)/shard_map/ppermute | solution.py:346
  6.3 15.1 %collective-permute-start.8 = (bf16[1,272,128]{2,1,0:T(8,128)(2,1)S(1)}, bf16[1,272,128]{2,1,0:T(8,128)(2,1)S(1)}, u32[]{:S(2)}, u32[]{:S(2)}) collective-permute-start(bf16[1,272,128]{2,1,0:T(8,128)(2,1)S(1)} %maximum_bitcast_fusion), channel_id=1, source_target_pairs={{0,4},{1,5},{2,6},{3,7},{4,0},{5,1},{6,2},{7,3},{8,12},{9,13},{10,... | collective-permute-start | bytes 208904 | tf_op jit(solution)/shard_map/ppermute | solution.py:346
  6.8 6.7 %collective-permute-start.2 = (bf16[1,272,128]{2,1,0:T(8,128)(2,1)S(1)}, bf16[1,272,128]{2,1,0:T(8,128)(2,1)S(1)}, u32[]{:S(2)}, u32[]{:S(2)}) collective-permute-start(bf16[1,272,128]{2,1,0:T(8,128)(2,1)S(1)} %maximum_bitcast_fusion), channel_id=1, source_target_pairs={{0,24},{1,25},{2,26},{3,27},{4,28},{5,29},{6,30},{7,31},{8,16},{9,... | collective-permute-start | bytes 208904 | tf_op jit(solution)/shard_map/ppermute | solution.py:346
  10.4 5.5 %collective-permute-start.1 = (bf16[1,272,128]{2,1,0:T(8,128)(2,1)S(1)}, bf16[1,272,128]{2,1,0:T(8,128)(2,1)S(1)}, u32[]{:S(2)}, u32[]{:S(2)}) collective-permute-start(bf16[1,272,128]{2,1,0:T(8,128)(2,1)S(1)} %maximum_bitcast_fusion), channel_id=1, source_target_pairs={{0,16},{1,17},{2,18},{3,19},{4,20},{5,21},{6,22},{7,23},{8,24},{9,... | collective-permute-start | bytes 208904 | tf_op jit(solution)/shard_map/ppermute | solution.py:346
  10.4 5.6 %collective-permute-start = (bf16[1,272,128]{2,1,0:T(8,128)(2,1)S(1)}, bf16[1,272,128]{2,1,0:T(8,128)(2,1)S(1)}, u32[]{:S(2)}, u32[]{:S(2)}) collective-permute-start(bf16[1,272,128]{2,1,0:T(8,128)(2,1)S(1)} %maximum_bitcast_fusion), channel_id=1, source_target_pairs={{0,8},{1,9},{2,10},{3,11},{4,12},{5,13},{6,14},{7,15},{8,0},{9,1},... | collective-permute-start | bytes 208904 | tf_op jit(solution)/shard_map/ppermute | solution.py:346
  13.5 4.3 %collective-permute-start.3 = (bf16[1,272,128]{2,1,0:T(8,128)(2,1)S(1)}, bf16[1,272,128]{2,1,0:T(8,128)(2,1)S(1)}, u32[]{:S(2)}, u32[]{:S(2)}) collective-permute-start(bf16[1,272,128]{2,1,0:T(8,128)(2,1)S(1)} %maximum_bitcast_fusion), channel_id=1, source_target_pairs={{0,2},{1,3},{2,0},{3,1},{4,6},{5,7},{6,4},{7,5},{8,10},{9,11},{10,... | collective-permute-start | bytes 208904 | tf_op jit(solution)/shard_map/ppermute | solution.py:346
  17.8 12.3 %collective-permute-start.7 = (bf16[3,272,128]{2,1,0:T(8,128)(2,1)S(1)}, bf16[3,272,128]{2,1,0:T(8,128)(2,1)S(1)}, u32[]{:S(2)}, u32[]{:S(2)}) collective-permute-start(bf16[3,272,128]{2,1,0:T(8,128)(2,1)S(1)} %pad_maximum_fusion.2), channel_id=1, source_target_pairs={{0,6},{1,7},{2,4},{3,5},{4,2},{5,3},{6,0},{7,1},{8,14},{9,15},{10,... | collective-permute-start | bytes 626696 | tf_op jit(solution)/shard_map/ppermute | solution.py:346
  19.4 10.7 %collective-permute-start.6 = (bf16[3,272,128]{2,1,0:T(8,128)(2,1)S(1)}, bf16[3,272,128]{2,1,0:T(8,128)(2,1)S(1)}, u32[]{:S(2)}, u32[]{:S(2)}) collective-permute-start(bf16[3,272,128]{2,1,0:T(8,128)(2,1)S(1)} %pad_maximum_fusion.2), channel_id=1, source_target_pairs={{0,4},{1,5},{2,6},{3,7},{4,0},{5,1},{6,2},{7,3},{8,12},{9,13},{10,... | collective-permute-start | bytes 626696 | tf_op jit(solution)/shard_map/ppermute | solution.py:346
  19.9 8.1 %collective-permute-start.4 = (bf16[3,272,128]{2,1,0:T(8,128)(2,1)S(1)}, bf16[3,272,128]{2,1,0:T(8,128)(2,1)S(1)}, u32[]{:S(2)}, u32[]{:S(2)}) collective-permute-start(bf16[3,272,128]{2,1,0:T(8,128)(2,1)S(1)} %pad_maximum_fusion.2), channel_id=1, source_target_pairs={{0,2},{1,3},{2,0},{3,1},{4,6},{5,7},{6,4},{7,5},{8,10},{9,11},{10,... | collective-permute-start | bytes 626696 | tf_op jit(solution)/shard_map/ppermute | solution.py:346
  21.4 8.7 %collective-permute-start.5 = (bf16[4,272,128]{2,1,0:T(8,128)(2,1)S(1)}, bf16[4,272,128]{2,1,0:T(8,128)(2,1)S(1)}, u32[]{:S(2)}, u32[]{:S(2)}) collective-permute-start(bf16[4,272,128]{2,1,0:T(8,128)(2,1)S(1)} %pad_maximum_fusion.1.refs_0_), channel_id=1, source_target_pairs={{0,1},{1,0},{2,3},{3,2},{4,5},{5,4},{6,7},{7,6},{8,9},{9,8},{10,11... | collective-permute-start | bytes 835592 | tf_op jit(solution)/shard_map/ppermute | solution.py:346
  28.0 4.7 %copy-start.1 = (f32[3,256]{1,0:T(4,128)S(1)}, f32[3,256]{1,0:T(4,128)}, u32[]{:S(2)}) copy-start(f32[3,256]{1,0:T(4,128)} %colour_grad_ref.1) | copy-start | bytes 9220
  30.2 2.4 %collective-permute-start.10 = (bf16[12,272,128]{2,1,0:T(8,128)(2,1)S(1)}, bf16[12,272,128]{2,1,0:T(8,128)(2,1)S(1)}, u32[]{:S(2)}, u32[]{:S(2)}) collective-permute-start(bf16[12,272,128]{2,1,0:T(8,128)(2,1)S(1)} %constant_dynamic-update-slice_fusion.refs_1_), channel_id=1, source_target_pairs={{0,1},{1,0},{2,3},{3,2},{4,5},{5,4},{6,7},{7,6},{8,9},{9,8},{10,11... | collective-permute-start | bytes 2506760 | tf_op jit(solution)/shard_map/ppermute | solution.py:346

commit v10 on v9

--- a/solution.py
+++ b/solution.py
@@ -381,7 +381,20 @@
         (jnp.concatenate(first[1:], axis=0), own_second[1])
     )
     second = share(others, stages[1], regions)
-    second[1], listed = lax.optimization_barrier((second[1], crossed.T))
+    listed = crossed.T
+    early = jnp.concatenate([own, others], axis=0)
+    if len(stages) > 3:
+        near = jnp.concatenate([early, *own_second[1:], *second[1:]], axis=0)
+        for stage in stages[2:-1]:
+            near = jnp.concatenate(share(near, stage, regions), axis=0)
+        weights = share(near, stages[-1], regions)
+    else:
+        early, far = share(early, stages[-1], regions)
+        far, listed, *second = lax.optimization_barrier((far, listed, *second[1:]))
+        late = jnp.concatenate([*own_second[1:], *second], axis=0)
+        late, far_late = share(late, stages[-1], regions)
+        weights = [early, late, far, far_late]
+
     slots, meta, rows = pl.pallas_call(
         functools.partial(order_kernel, dims),
         out_shape=(
@@ -395,19 +408,6 @@
         cost_estimate=pl.CostEstimate(flops=4 * 10**9, bytes_accessed=10**7, transcendentals=0),
         name="order",
     )(all_samples, listed)
-
-    early = jnp.concatenate([own, others], axis=0)
-    if len(stages) > 3:
-        near = jnp.concatenate([early, *own_second[1:], *second[1:]], axis=0)
-        for stage in stages[2:-1]:
-            near = jnp.concatenate(share(near, stage, regions), axis=0)
-        weights = share(near, stages[-1], regions)
-    else:
-        early, far = share(early, stages[-1], regions)
-        far, slots, *second = lax.optimization_barrier((far, slots, *second[1:]))
-        late = jnp.concatenate([*own_second[1:], *second], axis=0)
-        late, far_late = share(late, stages[-1], regions)
-        weights = [early, late, far, far_late]
 
     whole = pl.BlockSpec(memory_space=vmem)
 

time: 70.2 us -> 67.4 us (0.960)
  waiting for transfers between devices: 13.8 us -> 11.3 us
  other arithmetic: 2.51 us -> 1.44 us
    ppermute x11, waiting for transfers between devices: 13.8 us -> 11.3 us  [share(): held.append(lax.ppermute(block, 'region', pairs))]
    concatenate x1, other arithmetic: 1.1 us -> 0.04 us  [on_device(): jnp.concatenate([sample_points.transpose(1, 0, 2), sample_spacing[None]],...]
  transfers between devices with their start and end apart: 11 -> 11, of which waited for: 6 -> 6; matrix products, arithmetic and copies ran while one was open for 2% -> 0% of each run, Pallas kernels for 3% -> 3%
where the time goes in v10:
time: 67.4 us; the launch traced here: 67.2 us
  Pallas kernels  26.4 us (39%)
  starting transfers between devices  13.3 us (20%)
  blocking collectives  12.8 us (19%)
  waiting for transfers between devices  11.3 us (17%)
  other arithmetic  1.44 us (2%)
  local copies, waits for them, and re-layouts  1.1 us (2%)
  between operations  0.8 us (1%)
    pallas_call x1, Pallas kernels, on_device(): pl.pallas_call(functools.partial(main_kernel, dims, stages, len(weights))...  24.3 us
    ppermute x11, starting transfers between devices, share(): held.append(lax.ppermute(block, 'region', pairs))  13.3 us
    all_to_all x1, blocking collectives, on_device(): lax.all_to_all(head_grad, 'region', split_axis=0, concat_axis=0, tiled=True)  12.8 us
    ppermute x11, waiting for transfers between devices, share(): held.append(lax.ppermute(block, 'region', pairs))  11.3 us
    pallas_call x1, Pallas kernels, on_device(): pl.pallas_call(functools.partial(order_kernel, dims), out_shape=(jax.Shap...  2.09 us
  transfers between devices with their start and end apart: 11, of which 6 were waited for; matrix products, arithmetic and copies ran while one was open for 0% of the time, Pallas kernels for 3%

profile of v10, /device:TPU:0, one launch (start us, length us, event | category | flops | bytes accessed | tf_op | source)
XLA Modules:
  0.0 67.2 jit_solution(10567831052049822111)
XLA Ops:
  0.6 0.7 %fusion.1 = bf16[8,256]{1,0:T(8,128)(2,1)S(1)} fusion(bf16[3,64]{1,0:T(4,128)(2,1)} %bitcast.18, bf16[4,256]{1,0:T(4,128)(2,1)} %bitcast.17), kind=kLoop, calls=%fused_computation.12 | loop fusion | flops 12288 | bytes 6528 | tf_op jit(solution)/shard_map/concatenate | solution.py:375
  1.3 0.9 %copy.9 = bf16[1,128,256]{1,2,0:T(8,128)(2,1)S(1)} copy(bf16[1,128,256]{2,1,0:T(8,128)(2,1)} %param.12) | data formatting | bytes 131072 | tf_op args[5]
  2.3 0.0 copy-start.2
  2.3 0.0 copy-start.3
  2.3 5.1 %collective-permute-start.2 = (bf16[1,272,128]{2,1,0:T(8,128)(2,1)S(1)}, bf16[1,272,128]{2,1,0:T(8,128)(2,1)S(1)}, u32[]{:S(2)}, u32[]{:S(2)}) collective-permute-start(bf16[1,272,128]{2,1,0:T(8,128)(2,1)S(1)} %maximum_bitcast_fusion), channel_id=1, source_target_pairs={{0,24},{1,25},{2,26},{3,27},{4,28},{5,29},{6,30},{7,31},{8,16},{9,... | collective-permute-start | bytes 208904 | tf_op jit(solution)/shard_map/ppermute | solution.py:346
  7.5 0.0 collective-permute-start.1
  7.5 0.6 collective-permute-start
  8.1 2.6 %collective-permute-start.9 = (bf16[1,272,128]{2,1,0:T(8,128)(2,1)S(1)}, bf16[1,272,128]{2,1,0:T(8,128)(2,1)S(1)}, u32[]{:S(2)}, u32[]{:S(2)}) collective-permute-start(bf16[1,272,128]{2,1,0:T(8,128)(2,1)S(1)} %maximum_bitcast_fusion), channel_id=1, source_target_pairs={{0,6},{1,7},{2,4},{3,5},{4,2},{5,3},{6,0},{7,1},{8,14},{9,15},{10,... | collective-permute-start | bytes 208904 | tf_op jit(solution)/shard_map/ppermute | solution.py:346
  10.7 0.5 collective-permute-start.8
  11.2 0.0 collective-permute-done.2
  11.2 0.8 %collective-permute-start.3 = (bf16[1,272,128]{2,1,0:T(8,128)(2,1)S(1)}, bf16[1,272,128]{2,1,0:T(8,128)(2,1)S(1)}, u32[]{:S(2)}, u32[]{:S(2)}) collective-permute-start(bf16[1,272,128]{2,1,0:T(8,128)(2,1)S(1)} %maximum_bitcast_fusion), channel_id=1, source_target_pairs={{0,2},{1,3},{2,0},{3,1},{4,6},{5,7},{6,4},{7,5},{8,10},{9,11},{10,... | collective-permute-start | bytes 208904 | tf_op jit(solution)/shard_map/ppermute | solution.py:346
  12.0 1.4 %collective-permute-done.1 = bf16[1,272,128]{2,1,0:T(8,128)(2,1)S(1)} collective-permute-done((bf16[1,272,128]{2,1,0:T(8,128)(2,1)S(1)}, bf16[1,272,128]{2,1,0:T(8,128)(2,1)S(1)}, u32[]{:S(2)}, u32[]{:S(2)}) %collective-permute-start.1) | collective-permute-done | bytes 69664 | tf_op jit(solution)/shard_map/ppermute | solution.py:346
  13.4 0.0 collective-permute-done
  13.4 2.1 %collective-permute-done.3 = bf16[1,272,128]{2,1,0:T(8,128)(2,1)S(1)} collective-permute-done((bf16[1,272,128]{2,1,0:T(8,128)(2,1)S(1)}, bf16[1,272,128]{2,1,0:T(8,128)(2,1)S(1)}, u32[]{:S(2)}, u32[]{:S(2)}) %collective-permute-start.3) | collective-permute-done | bytes 69664 | tf_op jit(solution)/shard_map/ppermute | solution.py:346
  15.5 1.8 %collective-permute-start.7 = (bf16[3,272,128]{2,1,0:T(8,128)(2,1)S(1)}, bf16[3,272,128]{2,1,0:T(8,128)(2,1)S(1)}, u32[]{:S(2)}, u32[]{:S(2)}) collective-permute-start(bf16[3,272,128]{2,1,0:T(8,128)(2,1)S(1)} %pad_maximum_fusion.2), channel_id=1, source_target_pairs={{0,6},{1,7},{2,4},{3,5},{4,2},{5,3},{6,0},{7,1},{8,14},{9,15},{10,... | collective-permute-start | bytes 626696 | tf_op jit(solution)/shard_map/ppermute | solution.py:346
  17.3 0.5 collective-permute-start.6
  17.8 0.0 collective-permute-start.4
  17.9 0.0 copy-start
  17.9 0.0 collective-permute-done.8
  17.9 1.3 %collective-permute-start.5 = (bf16[3,272,128]{2,1,0:T(8,128)(2,1)S(1)}, bf16[3,272,128]{2,1,0:T(8,128)(2,1)S(1)}, u32[]{:S(2)}, u32[]{:S(2)}) collective-permute-start(bf16[3,272,128]{2,1,0:T(8,128)(2,1)S(1)} %pad_maximum_fusion.2), channel_id=1, source_target_pairs={{0,2},{1,3},{2,0},{3,1},{4,6},{5,7},{6,4},{7,5},{8,10},{9,11},{10,... | collective-permute-start | bytes 626696 | tf_op jit(solution)/shard_map/ppermute | solution.py:346
  19.2 0.0 collective-permute-done.9
  19.2 3.4 %collective-permute-done.7 = bf16[3,272,128]{2,1,0:T(8,128)(2,1)S(1)} collective-permute-done((bf16[3,272,128]{2,1,0:T(8,128)(2,1)S(1)}, bf16[3,272,128]{2,1,0:T(8,128)(2,1)S(1)}, u32[]{:S(2)}, u32[]{:S(2)}) %collective-permute-start.7) | collective-permute-done | bytes 208928 | tf_op jit(solution)/shard_map/ppermute | solution.py:346
  22.6 3.4 %collective-permute-done.6 = bf16[3,272,128]{2,1,0:T(8,128)(2,1)S(1)} collective-permute-done((bf16[3,272,128]{2,1,0:T(8,128)(2,1)S(1)}, bf16[3,272,128]{2,1,0:T(8,128)(2,1)S(1)}, u32[]{:S(2)}, u32[]{:S(2)}) %collective-permute-start.6) | collective-permute-done | bytes 208928 | tf_op jit(solution)/shard_map/ppermute | solution.py:346
  26.0 0.8 %collective-permute-done.5 = bf16[3,272,128]{2,1,0:T(8,128)(2,1)S(1)} collective-permute-done((bf16[3,272,128]{2,1,0:T(8,128)(2,1)S(1)}, bf16[3,272,128]{2,1,0:T(8,128)(2,1)S(1)}, u32[]{:S(2)}, u32[]{:S(2)}) %collective-permute-start.5) | collective-permute-done | bytes 208928 | tf_op jit(solution)/shard_map/ppermute | solution.py:346
  26.8 0.0 collective-permute-done.4.refs_2_
  26.9 0.1 collective-permute-start.10
  27.0 0.0 copy-done.2
  27.0 0.0 copy-done.3
  27.1 0.0 copy-done
  27.1 0.0 copy-start.1
  27.1 2.1 %order.1 = (f32[4,256]{1,0:T(4,128)S(1)}, s32[2,256]{1,0:T(2,128)S(1)}, f32[2,1280,128]{2,1,0:T(8,128)S(1)}) custom-call(f32[4,256,128]{2,1,0:T(8,128)S(1)} %pad_maximum_fusion.samples_ref, s32[4,256]{1,0:T(4,128)S(1)} %bitcast.12), custom_call_target="tpu_custom_call" | custom-call | flops 4000000000 | bytes 10000000 | tf_op jit(solution)/shard_map/order/pallas_call | solution.py:398
  29.2 0.2 collective-permute-done.10.refs_3_
  29.4 0.0 copy-done.1
  29.4 24.3 %render.1 = (f32[3,256]{1,0:T(4,128)}, f32[32,4,256]{2,1,0:T(4,128)S(1)}) custom-call(s32[2,256]{1,0:T(2,128)S(1)} %get-tuple-element.16.meta_ref, s32[1]{0:T(128)} %bitcast.8.me_ref, f32[4,256]{1,0:T(4,128)S(1)} %get-tuple-element.17.slots_ref, f32[2,1280,128]{2,1,0:T(8,128)S(1)} %get-tuple-element.18.rows_ref, f32[3,256]{1,0:T(4,128)S(1)} %copy-done.1, ...), custom_call_target="tpu_custom_call" | custom-call | flops 20000000000 | bytes 30000000 | tf_op jit(solution)/shard_map/render/pallas_call | solution.py:414
  53.7 12.8 %all_to_all.5 = f32[32,4,256]{2,1,0:T(4,128)S(1)} all-to-all(f32[32,4,256]{2,1,0:T(4,128)S(1)} %get-tuple-element.25), channel_id=1, replica_groups=mesh['region'=32] {'region'}, dimensions={0} | all-to-all | bytes 262144 | tf_op jit(solution)/shard_map/all_to_all | solution.py:437
  66.5 0.6 reduce_sum.9
  (11 shorter events, 0.2 us)
Async XLA Ops:
  2.3 24.7 %copy-start.2 = (f32[256,3,128]{2,0,1:T(8,128)S(1)}, f32[256,3,128]{2,0,1:T(8,128)}, u32[]{:S(2)}) copy-start(f32[256,3,128]{2,0,1:T(8,128)} %param.7) | copy-start | bytes 1179652
  2.3 24.7 %copy-start.3 = (f32[256,128]{1,0:T(8,128)S(1)}, f32[256,128]{1,0:T(8,128)}, u32[]{:S(2)}) copy-start(f32[256,128]{1,0:T(8,128)} %param.8) | copy-start | bytes 393220
  2.3 8.9 %collective-permute-start.2 = (bf16[1,272,128]{2,1,0:T(8,128)(2,1)S(1)}, bf16[1,272,128]{2,1,0:T(8,128)(2,1)S(1)}, u32[]{:S(2)}, u32[]{:S(2)}) collective-permute-start(bf16[1,272,128]{2,1,0:T(8,128)(2,1)S(1)} %maximum_bitcast_fusion), channel_id=1, source_target_pairs={{0,24},{1,25},{2,26},{3,27},{4,28},{5,29},{6,30},{7,31},{8,16},{9,... | collective-permute-start | bytes 208904 | tf_op jit(solution)/shard_map/ppermute | solution.py:346
  7.5 5.9 %collective-permute-start.1 = (bf16[1,272,128]{2,1,0:T(8,128)(2,1)S(1)}, bf16[1,272,128]{2,1,0:T(8,128)(2,1)S(1)}, u32[]{:S(2)}, u32[]{:S(2)}) collective-permute-start(bf16[1,272,128]{2,1,0:T(8,128)(2,1)S(1)} %maximum_bitcast_fusion), channel_id=1, source_target_pairs={{0,16},{1,17},{2,18},{3,19},{4,20},{5,21},{6,22},{7,23},{8,24},{9,... | collective-permute-start | bytes 208904 | tf_op jit(solution)/shard_map/ppermute | solution.py:346
  7.5 5.9 %collective-permute-start = (bf16[1,272,128]{2,1,0:T(8,128)(2,1)S(1)}, bf16[1,272,128]{2,1,0:T(8,128)(2,1)S(1)}, u32[]{:S(2)}, u32[]{:S(2)}) collective-permute-start(bf16[1,272,128]{2,1,0:T(8,128)(2,1)S(1)} %maximum_bitcast_fusion), channel_id=1, source_target_pairs={{0,8},{1,9},{2,10},{3,11},{4,12},{5,13},{6,14},{7,15},{8,0},{9,1},... | collective-permute-start | bytes 208904 | tf_op jit(solution)/shard_map/ppermute | solution.py:346
  8.1 11.1 %collective-permute-start.9 = (bf16[1,272,128]{2,1,0:T(8,128)(2,1)S(1)}, bf16[1,272,128]{2,1,0:T(8,128)(2,1)S(1)}, u32[]{:S(2)}, u32[]{:S(2)}) collective-permute-start(bf16[1,272,128]{2,1,0:T(8,128)(2,1)S(1)} %maximum_bitcast_fusion), channel_id=1, source_target_pairs={{0,6},{1,7},{2,4},{3,5},{4,2},{5,3},{6,0},{7,1},{8,14},{9,15},{10,... | collective-permute-start | bytes 208904 | tf_op jit(solution)/shard_map/ppermute | solution.py:346
  10.7 7.2 %collective-permute-start.8 = (bf16[1,272,128]{2,1,0:T(8,128)(2,1)S(1)}, bf16[1,272,128]{2,1,0:T(8,128)(2,1)S(1)}, u32[]{:S(2)}, u32[]{:S(2)}) collective-permute-start(bf16[1,272,128]{2,1,0:T(8,128)(2,1)S(1)} %maximum_bitcast_fusion), channel_id=1, source_target_pairs={{0,4},{1,5},{2,6},{3,7},{4,0},{5,1},{6,2},{7,3},{8,12},{9,13},{10,... | collective-permute-start | bytes 208904 | tf_op jit(solution)/shard_map/ppermute | solution.py:346
  11.2 4.3 %collective-permute-start.3 = (bf16[1,272,128]{2,1,0:T(8,128)(2,1)S(1)}, bf16[1,272,128]{2,1,0:T(8,128)(2,1)S(1)}, u32[]{:S(2)}, u32[]{:S(2)}) collective-permute-start(bf16[1,272,128]{2,1,0:T(8,128)(2,1)S(1)} %maximum_bitcast_fusion), channel_id=1, source_target_pairs={{0,2},{1,3},{2,0},{3,1},{4,6},{5,7},{6,4},{7,5},{8,10},{9,11},{10,... | collective-permute-start | bytes 208904 | tf_op jit(solution)/shard_map/ppermute | solution.py:346
  15.5 7.1 %collective-permute-start.7 = (bf16[3,272,128]{2,1,0:T(8,128)(2,1)S(1)}, bf16[3,272,128]{2,1,0:T(8,128)(2,1)S(1)}, u32[]{:S(2)}, u32[]{:S(2)}) collective-permute-start(bf16[3,272,128]{2,1,0:T(8,128)(2,1)S(1)} %pad_maximum_fusion.2), channel_id=1, source_target_pairs={{0,6},{1,7},{2,4},{3,5},{4,2},{5,3},{6,0},{7,1},{8,14},{9,15},{10,... | collective-permute-start | bytes 626696 | tf_op jit(solution)/shard_map/ppermute | solution.py:346
  17.3 8.7 %collective-permute-start.6 = (bf16[3,272,128]{2,1,0:T(8,128)(2,1)S(1)}, bf16[3,272,128]{2,1,0:T(8,128)(2,1)S(1)}, u32[]{:S(2)}, u32[]{:S(2)}) collective-permute-start(bf16[3,272,128]{2,1,0:T(8,128)(2,1)S(1)} %pad_maximum_fusion.2), channel_id=1, source_target_pairs={{0,4},{1,5},{2,6},{3,7},{4,0},{5,1},{6,2},{7,3},{8,12},{9,13},{10,... | collective-permute-start | bytes 626696 | tf_op jit(solution)/shard_map/ppermute | solution.py:346
  17.8 9.0 %collective-permute-start.4 = (bf16[4,272,128]{2,1,0:T(8,128)(2,1)S(1)}, bf16[4,272,128]{2,1,0:T(8,128)(2,1)S(1)}, u32[]{:S(2)}, u32[]{:S(2)}) collective-permute-start(bf16[4,272,128]{2,1,0:T(8,128)(2,1)S(1)} %pad_maximum_fusion.1.refs_0_), channel_id=1, source_target_pairs={{0,1},{1,0},{2,3},{3,2},{4,5},{5,4},{6,7},{7,6},{8,9},{9,8},{10,11... | collective-permute-start | bytes 835592 | tf_op jit(solution)/shard_map/ppermute | solution.py:346
  17.9 9.2 %copy-start = (s32[256,4]{0,1:T(4,128)S(1)}, s32[256,4]{0,1:T(4,128)}, u32[]{:S(2)}) copy-start(s32[256,4]{0,1:T(4,128)} %param.9) | copy-start | bytes 12292
  17.9 9.0 %collective-permute-start.5 = (bf16[3,272,128]{2,1,0:T(8,128)(2,1)S(1)}, bf16[3,272,128]{2,1,0:T(8,128)(2,1)S(1)}, u32[]{:S(2)}, u32[]{:S(2)}) collective-permute-start(bf16[3,272,128]{2,1,0:T(8,128)(2,1)S(1)} %pad_maximum_fusion.2), channel_id=1, source_target_pairs={{0,2},{1,3},{2,0},{3,1},{4,6},{5,7},{6,4},{7,5},{8,10},{9,11},{10,... | collective-permute-start | bytes 626696 | tf_op jit(solution)/shard_map/ppermute | solution.py:346
  26.9 2.4 %collective-permute-start.10 = (bf16[12,272,128]{2,1,0:T(8,128)(2,1)S(1)}, bf16[12,272,128]{2,1,0:T(8,128)(2,1)S(1)}, u32[]{:S(2)}, u32[]{:S(2)}) collective-permute-start(bf16[12,272,128]{2,1,0:T(8,128)(2,1)S(1)} %constant_dynamic-update-slice_fusion.refs_1_), channel_id=1, source_target_pairs={{0,1},{1,0},{2,3},{3,2},{4,5},{5,4},{6,7},{7,6},{8,9},{9,8},{10,11... | collective-permute-start | bytes 2506760 | tf_op jit(solution)/shard_map/ppermute | solution.py:346
  27.1 2.3 %copy-start.1 = (f32[3,256]{1,0:T(4,128)S(1)}, f32[3,256]{1,0:T(4,128)}, u32[]{:S(2)}) copy-start(f32[3,256]{1,0:T(4,128)} %colour_grad_ref.1) | copy-start | bytes 9220
